TPU v7x, 32 devices: a whole 2x2x4 slice. The times are simulated.
32 devices in a mesh: groups: 2 (over y), feat: 4 (over z), head: 4 (over x, core).
Axes of the slice: x: 2, y: 2, z: 4, core: 2. Of those that a mesh axis runs over, the one named last changes fastest.
Arguments:
- token_ids: int32 [32], P('groups'), parts along dimension 0, may hold values from 0 to 75967
- embedding: bfloat16 [75968, 5120], P('head', 'feat'), may hold values from -16 to 16
- retained: bfloat16 [2, 32, 8, 8256, 128], P(None, 'groups', 'head', 'feat'), parts along dimension 1, may hold values from -0.29882812 to 0.29882812
- query_weight: bfloat16 [2, 5120, 5120], P(None, 'feat', 'head'), may hold values from -0.078125 to 0.078125
- key_weight: bfloat16 [2, 5120, 1024], P(None, 'feat', 'head'), may hold values from -0.078125 to 0.078125
- value_weight: bfloat16 [2, 5120, 1024], P(None, 'feat', 'head'), may hold values from -0.078125 to 0.078125
- gate_weight: bfloat16 [2, 5120, 8], P(None, 'feat', 'head'), may hold values from -0.078125 to 0.078125
- gate_bias: float32 [2, 8], P(None, 'head'), may hold values from -4 to 3
- norm_gain: float32 [2, 5120], P(None, 'feat'), may hold values from 0.1 to 1.9
- read_gain: float32 [2, 128], replicated, may hold values from 0.1 to 1.9
- out_weight: bfloat16 [2, 5120, 5120], P(None, 'head', 'feat'), may hold values from -0.078125 to 0.078125
Outputs:
- hidden_out: bfloat16 [32, 5120], P('groups', 'feat'), parts along dimension 0
There are 2 independent parts, one for each index of `groups`. A program takes and returns all parts, laid end to end along the dimension named above; an argument that names none is the same for every part. Nothing has to cross between parts.
All inputs are finite; a program needn't handle non-finite values.
Results may differ from a plain program's by a relative error of at most 0.01345.
The roundings to bfloat16 on the way count: a program that leaves them out, or rounds other values in their place, can miss the bound.
Values may be sent and summed in bfloat16 or wider, within the bound.
No kernel may reach another device: no remote copies, remote signals or barrier semaphores. Data moves between devices by JAX's collectives and lax.ppermute only.
A program may use at most 192 MiB of HBM per device.

v0:
```python
import math

import jax
import jax.numpy as jnp
import numpy as np
from jax import lax
from jax.sharding import PartitionSpec as P

D = 5120


def body(
    token_ids,
    embedding,
    retained,
    query_weight,
    key_weight,
    value_weight,
    gate_weight,
    gate_bias,
    norm_gain,
    read_gain,
    out_weight,
):
    layer_count, requests, local_heads, block_feat, head_size = retained.shape
    group_size = query_weight.shape[2] // (local_heads * head_size)
    table_rows = embedding.shape[0]
    row_start = lax.axis_index("head") * table_rows
    local_ids = token_ids - row_start
    inside = (local_ids >= 0) & (local_ids < table_rows)
    picked = jnp.take(embedding, jnp.clip(local_ids, 0, table_rows - 1), axis=0)
    picked = jnp.where(inside[:, None], picked.astype(jnp.float32), 0.0)
    stream = lax.psum(picked.astype(jnp.bfloat16), "head")
    pair_left, pair_right = np.triu_indices(head_size)
    feat_start = lax.axis_index("feat") * block_feat
    block_left = lax.dynamic_slice_in_dim(
        jnp.asarray(pair_left.astype(np.int32)), feat_start, block_feat
    )
    block_right = lax.dynamic_slice_in_dim(
        jnp.asarray(pair_right.astype(np.int32)), feat_start, block_feat
    )
    positions = jnp.arange(head_size, dtype=jnp.int32)[:, None]
    select_left = (positions == block_left[None, :]).astype(jnp.bfloat16)
    select_right = (positions == block_right[None, :]).astype(jnp.bfloat16)
    pair_scale = jnp.where(block_left == block_right, 1.0, math.sqrt(2.0)).astype(jnp.float32)

    def expand(vectors):
        flat = vectors.reshape(-1, head_size)
        left_part = jnp.dot(flat, select_left, preferred_element_type=jnp.float32)
        right_part = jnp.dot(flat, select_right, preferred_element_type=jnp.float32)
        return left_part * right_part * pair_scale

    for layer_index in range(layer_count):
        stream_wide = stream.astype(jnp.float32)
        sum_sq = lax.psum(jnp.sum(stream_wide * stream_wide, axis=1), "feat")
        normed = (
            stream_wide * lax.rsqrt(sum_sq[:, None] / D + 1e-06) * norm_gain[layer_index]
        ).astype(jnp.bfloat16)
        part_query = jnp.dot(normed, query_weight[layer_index], preferred_element_type=jnp.float32)
        part_key = jnp.dot(normed, key_weight[layer_index], preferred_element_type=jnp.float32)
        part_value = jnp.dot(normed, value_weight[layer_index], preferred_element_type=jnp.float32)
        part_gate = jnp.dot(normed, gate_weight[layer_index], preferred_element_type=jnp.float32)
        sum_query, sum_key, sum_value, gate_total = lax.psum(
            (part_query, part_key, part_value, part_gate), "feat"
        )
        query = sum_query.astype(jnp.bfloat16)
        key_rows = sum_key.astype(jnp.bfloat16)
        value_rows = sum_value.astype(jnp.bfloat16)
        decay_rate = jnp.exp(-jax.nn.softplus(gate_total + gate_bias[layer_index]))
        phi_query = (
            expand(query)
            .astype(jnp.bfloat16)
            .reshape(requests, local_heads, group_size, block_feat)
        )
        phi_key = (
            (expand(key_rows) / head_size)
            .astype(jnp.bfloat16)
            .reshape(requests, local_heads, block_feat)
        )
        history = jnp.einsum(
            "rhgf,rhfe->rhge", phi_query, retained[layer_index], preferred_element_type=jnp.float32
        )
        cross_term = jnp.einsum(
            "rhgf,rhf->rhg", phi_query, phi_key, preferred_element_type=jnp.float32
        )
        value_wide = value_rows.astype(jnp.float32).reshape(requests, local_heads, 1, head_size)
        partial_value = decay_rate[:, :, None, None] * history + cross_term[..., None] * value_wide
        readout = lax.psum(partial_value, "feat")
        scaled = (
            readout
            * lax.rsqrt(jnp.mean(readout * readout, axis=-1, keepdims=True) + 1e-06)
            * read_gain[layer_index]
        )
        mixed = scaled.astype(jnp.bfloat16).reshape(requests, local_heads * group_size * head_size)
        branch = jnp.dot(mixed, out_weight[layer_index], preferred_element_type=jnp.float32)
        summed = lax.psum(branch, "head")
        stream = (stream_wide + summed).astype(jnp.bfloat16)
    return stream


def solution(mesh):
    return jax.shard_map(
        body,
        mesh=mesh,
        in_specs=(
            P("groups"),
            P("head", "feat"),
            P(None, "groups", "head", "feat", None),
            P(None, "feat", "head"),
            P(None, "feat", "head"),
            P(None, "feat", "head"),
            P(None, "feat", "head"),
            P(None, "head"),
            P(None, "feat"),
            P(),
            P(None, "head", "feat"),
        ),
        out_specs=P("groups", "feat"),
        check_vma=False,
    )
```

profile of v0, /device:TPU:0, one launch (start us, length us, event | category | flops | bytes accessed | tf_op | source)
XLA Modules:
  0.0 259.7 jit_solution(4829169520611257211)
XLA Ops:
  6.5 0.8 dynamic_slice.6
  7.3 0.8 compare_select_fusion
  8.1 0.8 dynamic_slice.7
  8.9 0.7 compare_and_fusion
  9.6 1.7 gather_fusion
  11.4 12.9 %psum.105 = bf16[16,1280]{1,0:T(8,128)(2,1)S(1)} all-reduce(bf16[16,1280]{1,0:T(8,128)(2,1)S(1)} %select_convert_fusion), channel_id=1, replica_groups=mesh['groups'=2,'feat'=4,'head'=4] {'head'}, use_global_device_ids=true, to_apply=%region_0.1 | all-reduce | flops 20480 | bytes 81920 | tf_op jit(solution)/shard_map/psum | solution.py:33
  24.3 0.8 slice_reduce_fusion
  25.2 0.1 fusion.64
  25.3 11.9 %psum.106 = f32[16]{0:T(128)S(1)} all-reduce(f32[16]{0:T(128)S(1)} %fusion.64), channel_id=1, replica_groups=mesh['groups'=2,'feat'=4,'head'=4] {'feat'}, use_global_device_ids=true, to_apply=%region_2.3 | all-reduce | flops 16 | bytes 128 | tf_op jit(solution)/shard_map/psum | solution.py:55
  37.2 2.7 %fusion.22 = f32[16,1280]{1,0:T(8,128)S(1)} fusion(bf16[2,1280,1280]{2,1,0:T(8,128)(2,1)} %param.16, bf16[16,1280]{1,0:T(8,128)(2,1)S(1)} %psum.105, f32[1280]{0:T(1024)S(1)} %get-tuple-element.6, f32[16]{0:T(128)S(1)} %add_rsqrt_fusion.3), kind=kOutput, calls=%fused_computation.27 | convolution fusion | flops 52510720 | bytes 3404864 | tf_op jit(solution)/shard_map/dot_general | solution.py:59
  39.9 0.2 fusion.48
  40.1 0.3 fusion.50
  40.4 0.2 copy-done.5
  40.6 0.2 fusion.74
  40.8 17.5 %all-reduce.1 = (bf16[16,1280]{1,0:T(8,128)(2,1)S(1)}, bf16[16,256]{1,0:T(8,128)(2,1)S(1)}, bf16[16,256]{1,0:T(8,128)(2,1)S(1)}, f32[16,2]{0,1:T(2,128)S(1)}) all-reduce(f32[16,1280]{1,0:T(8,128)S(1)} %fusion.22, f32[16,256]{1,0:T(8,128)S(1)} %fusion.48, ...), channel_id=1, replica_groups=mesh['groups'=2,'feat'=4,'head'=4] {'feat'}, use_global_device_ids=true, to_apply=%region_4.5 | all-reduce | flops 28704 | bytes 172288 | tf_op jit(solution)/shard_map/psum | solution.py:63
  58.4 0.4 fusion.43
  58.8 0.4 fusion.8
  59.2 0.3 reshape.74
  59.5 0.3 fusion.42
  59.8 0.3 fusion.14
  60.3 0.1 copy.16
  60.4 0.7 fusion.91
  61.1 8.0 %fusion.31 = f32[16,2,5,128]{3,2,1,0:T(8,128)} fusion(bf16[16,2,5,2064]{3,2,1,0:T(8,128)(2,1)S(1)} %reshape.74, bf16[2,16,2,2064,128]{4,3,2,1,0:T(8,128)(2,1)} %param.15, f32[16,2,128]{2,1,0:T(2,128)S(1)} %reshape.83, f32[16,2,5]{2,1,0:T(2,128)S(1)} %bitcast.72, f32[16,2]{1,0:T(8,128)S(1)} %copy.16), kind=kOutput, calls=%fused_computation.34 | convolution fusion | flops 84602880 | bytes 17667840 | tf_op jit(solution)/shard_map/rhgf,rhfe->rhge/dot_general | solution.py:80
  69.2 33.6 %all-reduce.7.cloned.1.call-done = f32[16,2,5,128]{3,2,1,0:T(8,128)} async-done(((f32[16,2,5,128]{3,2,1,0:T(8,128)}), f32[16,2,5,128]{3,2,1,0:T(8,128)}) %all-reduce.7.cloned.1.call-update) | async-done | bytes 81936 | tf_op jit(solution)/shard_map/psum | solution.py:88
  102.8 1.0 multiply_reduce_fusion.1
  103.9 1.0 multiply_convert_fusion.1
  105.0 3.1 %fusion.20 = f32[16,1280]{1,0:T(8,128)} fusion(bf16[16,1280]{1,0:T(8,128)(2,1)S(1)} %reshape.77, bf16[2,1280,1280]{2,1,0:T(8,128)(2,1)} %param.23), kind=kOutput, calls=%fused_computation.25 | convolution fusion | flops 52428800 | bytes 3399680 | tf_op jit(solution)/shard_map/dot_general | solution.py:95
  108.1 29.5 %all-reduce.9.cloned.1.call-done = f32[16,1280]{1,0:T(8,128)} async-done(((f32[16,1280]{1,0:T(8,128)}), f32[16,1280]{1,0:T(8,128)}) %all-reduce.9.cloned.1.call-update) | async-done | bytes 81936 | tf_op jit(solution)/shard_map/psum | solution.py:96
  137.6 1.0 fusion.68
  138.6 11.7 %psum.113 = f32[16]{0:T(128)S(1)} all-reduce(f32[16]{0:T(128)S(1)} %get-tuple-element.15), channel_id=1, replica_groups=mesh['groups'=2,'feat'=4,'head'=4] {'feat'}, use_global_device_ids=true, to_apply=%region_11.12 | all-reduce | flops 16 | bytes 128 | tf_op jit(solution)/shard_map/psum | solution.py:55
  150.3 2.6 %fusion.18 = f32[16,1280]{1,0:T(8,128)S(1)} fusion(bf16[2,1280,1280]{2,1,0:T(8,128)(2,1)} %param.16, bf16[16,1280]{1,0:T(8,128)(2,1)S(1)} %get-tuple-element.16, f32[1280]{0:T(1024)S(1)} %get-tuple-element.5, f32[16]{0:T(128)S(1)} %add_rsqrt_fusion.2), kind=kOutput, calls=%fused_computation.23 | convolution fusion | flops 52510720 | bytes 3404864 | tf_op jit(solution)/shard_map/dot_general | solution.py:59
  153.0 0.2 fusion.44
  153.2 0.3 fusion.46
  153.4 0.2 fusion.72
  153.7 17.7 %all-reduce = (bf16[16,1280]{1,0:T(8,128)(2,1)S(1)}, bf16[16,256]{1,0:T(8,128)(2,1)S(1)}, bf16[16,256]{1,0:T(8,128)(2,1)S(1)}, f32[16,2]{0,1:T(2,128)S(1)}) all-reduce(f32[16,1280]{1,0:T(8,128)S(1)} %fusion.18, f32[16,256]{1,0:T(8,128)S(1)} %fusion.44, ...), channel_id=1, replica_groups=mesh['groups'=2,'feat'=4,'head'=4] {'feat'}, use_global_device_ids=true, to_apply=%region_13.14 | all-reduce | flops 28704 | bytes 172288 | tf_op jit(solution)/shard_map/psum | solution.py:63
  171.5 0.4 fusion.41
  171.8 0.4 fusion.9
  172.2 0.3 reshape.79
  172.6 0.3 fusion.40
  172.9 0.3 fusion.15
  173.4 0.7 fusion.92
  174.1 8.0 %fusion.37 = f32[16,2,5,128]{3,2,1,0:T(8,128)} fusion(bf16[16,2,5,2064]{3,2,1,0:T(8,128)(2,1)S(1)} %reshape.79, bf16[2,16,2,2064,128]{4,3,2,1,0:T(8,128)(2,1)} %param.15, f32[16,2,128]{2,1,0:T(2,128)S(1)} %reshape.84, f32[16,2,5]{2,1,0:T(2,128)S(1)} %bitcast.73, f32[16,2]{1,0:T(8,128)S(1)} %copy.17), kind=kOutput, calls=%fused_computation.36 | convolution fusion | flops 84602880 | bytes 17667840 | tf_op jit(solution)/shard_map/rhgf,rhfe->rhge/dot_general | solution.py:80
  182.2 34.7 %all-reduce.11.cloned.1.call-done = f32[16,2,5,128]{3,2,1,0:T(8,128)} async-done(((f32[16,2,5,128]{3,2,1,0:T(8,128)}), f32[16,2,5,128]{3,2,1,0:T(8,128)}) %all-reduce.11.cloned.1.call-update) | async-done | bytes 81936 | tf_op jit(solution)/shard_map/psum | solution.py:88
  216.9 1.0 multiply_reduce_fusion
  218.0 1.0 multiply_convert_fusion
  219.0 3.1 %fusion.16 = f32[16,1280]{1,0:T(8,128)} fusion(bf16[16,1280]{1,0:T(8,128)(2,1)S(1)} %reshape.82, bf16[2,1280,1280]{2,1,0:T(8,128)(2,1)} %param.23), kind=kOutput, calls=%fused_computation.21 | convolution fusion | flops 52428800 | bytes 3399680 | tf_op jit(solution)/shard_map/dot_general | solution.py:95
  222.2 29.5 %all-reduce.13.cloned.1.call-done = f32[16,1280]{1,0:T(8,128)} async-done(((f32[16,1280]{1,0:T(8,128)}), f32[16,1280]{1,0:T(8,128)}) %all-reduce.13.cloned.1.call-update) | async-done | bytes 81936 | tf_op jit(solution)/shard_map/psum | solution.py:96
  251.7 1.5 fusion.71
  (40 shorter events, 1.1 us)
Async XLA Ops:
  6.5 96.3 %all-reduce.7.cloned.1.call-start = ((), (), s32[]{:S(2)}) async-start(), calls=%async_computation | async-start | bytes 262144 | tf_op jit(solution)/shard_map/psum | solution.py:88
  37.2 2.7 %copy-start.2 = (bf16[2,1280,256]{2,1,0:T(8,128)(2,1)S(1)}, bf16[2,1280,256]{2,1,0:T(8,128)(2,1)}, u32[]{:S(2)}) copy-start(bf16[2,1280,256]{2,1,0:T(8,128)(2,1)} %param.18) | copy-start | bytes 3932164
  37.2 2.9 %copy-start.3 = (bf16[2,1280,256]{2,1,0:T(8,128)(2,1)S(1)}, bf16[2,1280,256]{2,1,0:T(8,128)(2,1)}, u32[]{:S(2)}) copy-start(bf16[2,1280,256]{2,1,0:T(8,128)(2,1)} %param.17) | copy-start | bytes 3932164
  39.9 0.7 copy-start.5
  59.2 1.0 copy-start
  61.1 8.1 %copy-start.1 = (f32[2,128]{1,0:T(2,128)S(1)}, f32[2,128]{1,0:T(2,128)}, u32[]{:S(2)}) copy-start(f32[2,128]{1,0:T(2,128)} %param.22) | copy-start | bytes 3076
  69.2 68.4 %all-reduce.9.cloned.1.call-start = ((), (), s32[]{:S(2)}) async-start(), calls=%async_computation.1 | async-start | bytes 163840 | tf_op jit(solution)/shard_map/psum | solution.py:96
  108.1 108.8 %all-reduce.11.cloned.1.call-start = ((), (), s32[]{:S(2)}) async-start(), calls=%async_computation.2 | async-start | bytes 262144 | tf_op jit(solution)/shard_map/psum | solution.py:88
  150.3 2.8 %copy-start.4 = (bf16[2,1280,256]{2,1,0:T(8,128)(2,1)S(1)}, bf16[2,1280,256]{2,1,0:T(8,128)(2,1)}, u32[]{:S(2)}) copy-start(bf16[2,1280,256]{2,1,0:T(8,128)(2,1)} %param.17) | copy-start | bytes 3932164
  182.2 69.5 %all-reduce.13.cloned.1.call-start = ((), (), s32[]{:S(2)}) async-start(), calls=%async_computation.3 | async-start | bytes 163840 | tf_op jit(solution)/shard_map/psum | solution.py:96
Sparse Core Ops, SparseCore 0:
  69.3 33.5 all-reduce.6
  108.2 29.3 all-reduce.8
  182.3 34.5 all-reduce.10
  222.3 29.3 all-reduce.12
where the time goes:
time: 261 us; the launch traced here: 260 us
  waiting for transfers between devices  127 us (49%)
  blocking collectives  71.8 us (28%)
  matrix products  33 us (13%)
  between operations  13.4 us (5%)
  other arithmetic  8.47 us (3%)
  local copies, waits for them, and re-layouts  5.56 us (2%)
    psum x2, waiting for transfers between devices, body(): readout = lax.psum(partial_value, 'feat')  68.3 us
    psum x2, waiting for transfers between devices, body(): summed = lax.psum(branch, 'head')  59 us
    psum x2, blocking collectives, body(): lax.psum((part_query, part_key, part_value, part_gate), 'feat')  35.2 us
    psum x2, blocking collectives, body(): sum_sq = lax.psum(jnp.sum(stream_wide * stream_wide, axis=1), 'feat')  23.6 us
    dot_general x2, matrix products, body(): jnp.einsum('rhgf,rhfe->rhge', phi_query, retained[layer_index], preferred...  16 us
    psum x1, blocking collectives, body(): stream = lax.psum(picked.astype(jnp.bfloat16), 'head')  12.9 us
    dot_general x2, matrix products, body(): jnp.dot(mixed, out_weight[layer_index], preferred_element_type=jnp.float32)  6.21 us
    dot_general x2, matrix products, body(): jnp.dot(normed, query_weight[layer_index], preferred_element_type=jnp.flo...  5.28 us
  transfers between devices with their start and end apart: 4, of which 4 were waited for; matrix products, arithmetic and copies ran while one was open for 0% of the time, Pallas kernels for 0%

commit v1 on v0

v1 whole, which is shorter than its diff:
```python
import functools
import math

import jax
import jax.numpy as jnp
import numpy as np
from jax import lax
from jax.experimental import pallas as pl
from jax.experimental.pallas import tpu as pltpu
from jax.sharding import PartitionSpec as P

D = 5120
EPS = 1e-6
LANES = 128
SLOTS = 8
ROWS = 16
MIB = 2**20
F32 = jnp.float32
BF16 = jnp.bfloat16

VMEM_SPEC = pl.BlockSpec(memory_space=pltpu.VMEM)
HBM_SPEC = pl.BlockSpec(memory_space=pltpu.HBM)
SMEM_SPEC = pl.BlockSpec(memory_space=pltpu.SMEM)


def params(mib):
    return pltpu.CompilerParams(vmem_limit_bytes=mib * MIB)


def resident(array):
    return pltpu.with_memory_space_constraint(array, pltpu.VMEM)


def off_chip(array):
    return pltpu.with_memory_space_constraint(array, pltpu.HBM)


def exchange(own, wire, axis, size):
    if size > 4:
        return [lax.psum(own.astype(F32), axis)]
    others = [
        lax.ppermute(wire, axis, [(rank, rank ^ step) for rank in range(size)])
        for step in range(1, size)
    ]
    return [own] + others


def split(wide):
    high = wide.astype(BF16)
    return high, (wide - high.astype(F32)).astype(BF16)


def split_dot(wide, weight):
    rows = wide.shape[0]
    out = jnp.dot(jnp.concatenate(split(wide), axis=0), weight, preferred_element_type=F32)
    return out[:rows] + out[rows:]


def add_terms(refs):
    terms = [ref[...].astype(F32) for ref in refs]
    while len(terms) > 1:
        terms = [sum(terms[at : at + 2]) for at in range(0, len(terms), 2)]
    return terms[0]


def pick_kernel(ids_ref, table_ref, out_ref, groups_ref, sems):
    requests = out_ref.shape[0]
    table_rows = table_ref.shape[0]
    row_start = lax.axis_index("head") * table_rows
    row_at = lax.broadcasted_iota(jnp.int32, (requests, requests * ROWS), 0)
    column_at = lax.broadcasted_iota(jnp.int32, (requests, requests * ROWS), 1)
    chosen = jnp.zeros((requests, requests * ROWS), F32)
    copies = []
    for request in range(requests):
        local_id = ids_ref[request] - row_start
        inside = (local_id >= 0) & (local_id < table_rows)
        row = jnp.clip(local_id, 0, table_rows - 1)
        first = pl.multiple_of((row // ROWS) * ROWS, ROWS)
        copy = pltpu.make_async_copy(
            table_ref.at[pl.ds(first, ROWS), :],
            groups_ref.at[pl.ds(request * ROWS, ROWS), :],
            sems.at[request],
        )
        copy.start()
        copies.append(copy)
        place = jnp.where(inside, request * ROWS + row - first, -1)
        chosen = jnp.where((row_at == request) & (column_at == place), 1.0, chosen)
    for copy in copies:
        copy.wait()
    out_ref[...] = jnp.dot(
        chosen.astype(BF16), groups_ref[...], preferred_element_type=F32
    ).astype(BF16)


def pick_rows(token_ids, embedding):
    table_rows, width = embedding.shape
    requests = token_ids.shape[0]
    if table_rows % ROWS:
        local_ids = token_ids - lax.axis_index("head") * table_rows
        inside = (local_ids >= 0) & (local_ids < table_rows)
        picked = jnp.take(embedding, jnp.clip(local_ids, 0, table_rows - 1), axis=0)
        return jnp.where(inside[:, None], picked, jnp.zeros_like(picked))
    return pl.pallas_call(
        pick_kernel,
        out_shape=jax.ShapeDtypeStruct((requests, width), BF16),
        in_specs=[SMEM_SPEC, HBM_SPEC],
        out_specs=VMEM_SPEC,
        scratch_shapes=[
            pltpu.VMEM((requests * ROWS, width), BF16),
            pltpu.SemaphoreType.DMA((requests,)),
        ],
        compiler_params=params(8),
        name="pick_rows",
    )(off_chip(token_ids), off_chip(embedding))


def fetch_kernel(plan, count, *refs):
    sources, outs, sems = refs[:count], refs[count:-1], refs[-1]
    copies = []
    for at, (source, index) in enumerate(plan):
        copy = pltpu.make_async_copy(sources[source].at[index], outs[at], sems.at[at])
        copy.start()
        copies.append(copy)
    for copy in copies:
        copy.wait()


def fetch(sources, plan):
    shapes = []
    for source, index in plan:
        array = sources[source]
        index = index if isinstance(index, tuple) else (index,)
        shape = []
        for at, extent in enumerate(array.shape):
            if at >= len(index):
                shape.append(extent)
            elif isinstance(index[at], slice):
                shape.append(index[at].stop - index[at].start)
        shapes.append(pltpu.VMEM(tuple(shape), array.dtype))
    return pl.pallas_call(
        functools.partial(fetch_kernel, plan, len(sources)),
        out_shape=shapes,
        in_specs=[HBM_SPEC] * len(sources),
        out_specs=[VMEM_SPEC] * len(plan),
        scratch_shapes=[pltpu.SemaphoreType.DMA((len(plan),))],
        compiler_params=params(2),
        name="fetch",
    )(*[off_chip(source) for source in sources])


def select_kernel(pairs_ref, left_ref, right_ref, scale_ref):
    mine = lax.axis_index("feat")
    left = pairs_ref[mine, 0:1, :]
    right = pairs_ref[mine, 1:2, :]
    at = lax.broadcasted_iota(jnp.int32, left_ref.shape, 0)
    at = jnp.where(at >= left_ref.shape[0] // 2, at - left_ref.shape[0] // 2, at)
    left_ref[...] = jnp.where(at == left, 1.0, 0.0).astype(BF16)
    right_ref[...] = jnp.where(at == right, 1.0, 0.0).astype(BF16)
    scale_ref[...] = jnp.where(left == right, 1.0, math.sqrt(2.0)).astype(F32)


def selectors(head_size, block_feat, feat_size):
    pairs = np.stack(np.triu_indices(head_size)).astype(np.int32)
    pairs = pairs.reshape(2, feat_size, block_feat).transpose(1, 0, 2)
    return pl.pallas_call(
        select_kernel,
        out_shape=[
            pltpu.VMEM((2 * head_size, block_feat), BF16),
            pltpu.VMEM((2 * head_size, block_feat), BF16),
            pltpu.VMEM((1, block_feat), F32),
        ],
        in_specs=[VMEM_SPEC],
        out_specs=[VMEM_SPEC] * 3,
        compiler_params=params(8),
        name="selectors",
    )(jnp.asarray(pairs))


def project_kernel(layer, count, carried, *refs):
    terms = refs[carried:count]
    gain_ref, query_ref, key_ref, value_ref, gate_ref = refs[count : count + 5]
    stream_ref, own_ref, wire_ref = refs[count + 5 :]
    stream = add_terms(terms)
    if carried:
        stream = refs[0][...].astype(F32) + stream
    stream = stream.astype(BF16)
    stream_ref[...] = stream
    wide = stream.astype(F32)
    sum_sq = jnp.sum(wide * wide, axis=1, keepdims=True)
    scaled = wide * gain_ref[layer : layer + 1, :]
    start = 0
    for weight_ref in (query_ref, key_ref, value_ref):
        width = weight_ref.shape[2]
        part = split_dot(scaled, weight_ref[layer])
        own_ref[:, start : start + width] = part
        wire_ref[:, start : start + width] = part.astype(BF16)
        start += width
    lane = lax.broadcasted_iota(jnp.int32, (stream.shape[0], LANES), 1)
    half = LANES // 2
    place = jnp.where(lane >= half, lane - half, lane)
    extra = jnp.where(place == 0, sum_sq, 0.0)
    for head in range(gate_ref.shape[1]):
        column = gate_ref[layer, head : head + 1, :].astype(F32)
        gate = jnp.sum(scaled * column, axis=1, keepdims=True)
        extra = jnp.where(place == head + 1, gate, extra)
    own_ref[:, start:] = jnp.where(lane < half, extra, 0.0)
    rounded = extra.astype(BF16).astype(F32)
    wire_ref[:, start:] = jnp.where(lane < half, rounded, extra - rounded).astype(BF16)


def project(layer, carried, terms, norm_gain, weights, gate_weight):
    terms = carried + terms
    requests, width = terms[0].shape
    total = sum(weight.shape[2] for weight in weights) + LANES
    return pl.pallas_call(
        functools.partial(project_kernel, layer, len(terms), len(carried)),
        out_shape=[
            jax.ShapeDtypeStruct((requests, width), BF16),
            jax.ShapeDtypeStruct((requests, total), F32),
            jax.ShapeDtypeStruct((requests, total), BF16),
        ],
        in_specs=[VMEM_SPEC] * (len(terms) + 5),
        out_specs=[VMEM_SPEC] * 3,
        compiler_params=params(8),
        name="project",
    )(*terms, norm_gain, *[resident(weight) for weight in weights], gate_weight)


def read_kernel(layer, sizes, count, held, *refs):
    local_heads, group_size, head_size = sizes
    terms = refs[:count]
    bias_ref, left_ref, right_ref, scale_ref = refs[count : count + 4]
    held_refs = refs[count + 4 : count + 4 + len(held)]
    rest = refs[count + 4 + len(held) :]
    state_ref, own_ref, wire_ref, rows_ref, phi_ref, cross_ref, history_ref, late_ref, sems = rest
    requests = own_ref.shape[0]
    block_feat = phi_ref.shape[2]
    early = sum(held)
    copies = []
    for at in range(requests - early):
        copy = pltpu.make_async_copy(state_ref.at[layer, early + at], late_ref.at[at], sems.at[at])
        copy.start()
        copies.append(copy)

    total = add_terms(terms)
    query_width = local_heads * group_size * head_size
    kv_width = local_heads * head_size
    extra = total[:, query_width + 2 * kv_width :]
    half = LANES // 2
    extra = extra[:, :half] + extra[:, half:]
    inverse = lax.rsqrt(extra[:, 0:1] / D + EPS)
    normed = total[:, : query_width + 2 * kv_width] * inverse

    span = local_heads * SLOTS
    key_slot = group_size
    for head in range(local_heads):
        for slot in range(SLOTS):
            if slot < group_size:
                start = (head * group_size + slot) * head_size
                part = normed[:, start : start + head_size]
            elif slot == key_slot:
                start = query_width + head * head_size
                part = normed[:, start : start + head_size]
            else:
                part = jnp.zeros((requests, head_size), F32)
            rows_ref[pl.ds(head * SLOTS + slot, requests, stride=span), :] = part
    vectors = jnp.concatenate(split(rows_ref[...]), axis=1)

    step = 2 * LANES
    for start in range(0, block_feat, step):
        stop = min(start + step, block_feat)
        left = jnp.dot(vectors, left_ref[:, start:stop], preferred_element_type=F32)
        right = jnp.dot(vectors, right_ref[:, start:stop], preferred_element_type=F32)
        phi = left * right * scale_ref[:, start:stop]
        for part, values in enumerate(split(phi)):
            phi_ref[part, :, start:stop] = values
        wide = phi.reshape(requests * local_heads, SLOTS, stop - start)
        cross = (wide * wide[:, key_slot : key_slot + 1, :]).reshape(-1, stop - start)
        for at in range(0, stop - start, LANES):
            lanes = min(LANES, stop - start - at)
            piece = cross[:, at : at + lanes]
            if start + at == 0:
                cross_ref[:, :lanes] = piece
            else:
                cross_ref[:, :lanes] += piece

    def one_request(request, states):
        mine = slice(request * span, (request + 1) * span)
        rows = jnp.concatenate([phi_ref[0, mine, :], phi_ref[1, mine, :]], axis=0)
        state = jnp.concatenate(states, axis=1) if local_heads > 1 else states[0]
        out = jnp.dot(rows, state, preferred_element_type=F32)
        out = out[:span] + out[span:]
        for head in range(local_heads):
            at = head * SLOTS
            history_ref[request * span + at : request * span + at + SLOTS, :] = out[
                at : at + SLOTS, head * head_size : (head + 1) * head_size
            ]

    request = 0
    for held_ref, many in zip(held_refs, held):
        for at in range(many):
            one_request(request, [held_ref[at, head] for head in range(local_heads)])
            request += 1
    for at, copy in enumerate(copies):
        copy.wait()
        one_request(request, [late_ref[at, head] for head in range(local_heads)])
        request += 1

    for head in range(local_heads):
        logit = extra[:, head + 1 : head + 2] * inverse
        logit = logit + bias_ref[layer : layer + 1, head : head + 1]
        softplus = jnp.maximum(logit, 0.0) + jnp.log(1.0 + jnp.exp(-jnp.abs(logit)))
        decay = jnp.exp(-softplus)
        start = query_width + kv_width + head * head_size
        value = normed[:, start : start + head_size]
        for slot in range(group_size):
            picked = pl.ds(head * SLOTS + slot, requests, stride=span)
            cross = jnp.sum(cross_ref[picked, :], axis=1, keepdims=True) / head_size
            part = decay * history_ref[picked, :] + cross * value
            start = (head * group_size + slot) * head_size
            own_ref[:, start : start + head_size] = part
            wire_ref[:, start : start + head_size] = part.astype(BF16)


def read(layer, sizes, terms, gate_bias, picks, held, retained):
    local_heads, group_size, head_size = sizes
    requests = terms[0].shape[0]
    block_feat = retained.shape[3]
    width = local_heads * group_size * head_size
    counts = tuple(array.shape[0] for array in held)
    late = requests - sum(counts)
    rows = requests * local_heads * SLOTS
    return pl.pallas_call(
        functools.partial(read_kernel, layer, sizes, len(terms), counts),
        out_shape=[
            jax.ShapeDtypeStruct((requests, width), F32),
            jax.ShapeDtypeStruct((requests, width), BF16),
        ],
        in_specs=[VMEM_SPEC] * (len(terms) + 4 + len(held)) + [HBM_SPEC],
        out_specs=[VMEM_SPEC] * 2,
        scratch_shapes=[
            pltpu.VMEM((rows, head_size), F32),
            pltpu.VMEM((2, rows, block_feat), BF16),
            pltpu.VMEM((rows, LANES), F32),
            pltpu.VMEM((rows, head_size), F32),
            pltpu.VMEM((max(late, 1),) + retained.shape[2:], BF16),
            pltpu.SemaphoreType.DMA((max(late, 1),)),
        ],
        compiler_params=params(12),
        name="read",
    )(*terms, gate_bias, *[resident(pick) for pick in picks], *[resident(part) for part in held], off_chip(retained))


def mix_kernel(layer, count, *refs):
    terms = refs[:count]
    gain_ref, weight_ref, wire_ref, mixed_ref = refs[count:]
    head_size = gain_ref.shape[1]
    readout = add_terms(terms)
    gain = gain_ref[layer : layer + 1, :]
    for start in range(0, readout.shape[1], head_size):
        part = readout[:, start : start + head_size]
        mean = jnp.mean(part * part, axis=1, keepdims=True)
        mixed_ref[:, start : start + head_size] = part * lax.rsqrt(mean + EPS) * gain
    wire_ref[...] = split_dot(mixed_ref[...], weight_ref[layer]).astype(wire_ref.dtype)


def mix(layer, terms, read_gain, weight, wire_type):
    requests, rows = terms[0].shape
    return pl.pallas_call(
        functools.partial(mix_kernel, layer, len(terms)),
        out_shape=jax.ShapeDtypeStruct((requests, weight.shape[2]), wire_type),
        in_specs=[VMEM_SPEC] * (len(terms) + 2),
        out_specs=VMEM_SPEC,
        scratch_shapes=[pltpu.VMEM((requests, rows), F32)],
        compiler_params=params(8),
        name="mix",
    )(*terms, read_gain, resident(weight))


def finish_kernel(count, *refs):
    stream = refs[0][...].astype(F32) + add_terms(refs[1:count])
    refs[count][...] = stream.astype(BF16)


def finish(terms):
    return pl.pallas_call(
        functools.partial(finish_kernel, len(terms)),
        out_shape=jax.ShapeDtypeStruct(terms[0].shape, BF16),
        in_specs=[VMEM_SPEC] * len(terms),
        out_specs=VMEM_SPEC,
        compiler_params=params(2),
        name="finish",
    )(*terms)


def body(
    feat_size,
    head_ranks,
    token_ids,
    embedding,
    retained,
    query_weight,
    key_weight,
    value_weight,
    gate_weight,
    gate_bias,
    norm_gain,
    read_gain,
    out_weight,
):
    layer_count, requests, local_heads, block_feat, head_size = retained.shape
    group_size = query_weight.shape[2] // (local_heads * head_size)
    sizes = (local_heads, group_size, head_size)
    weights = (query_weight, key_weight, value_weight)
    gate_rows = gate_weight.transpose(0, 2, 1)
    picks = selectors(head_size, block_feat, feat_size)

    picked = pick_rows(token_ids, embedding)
    stream_terms = exchange(picked, picked, "head", head_ranks)
    stream = None
    for layer in range(layer_count):
        carried = [] if stream is None else [stream]
        stream, own, wire = project(layer, carried, stream_terms, norm_gain, weights, gate_rows)
        terms = exchange(own, wire, "feat", feat_size)
        early = requests * 10 // 16
        held = fetch([retained], ((0, (layer, slice(0, early))),))
        own, wire = read(layer, sizes, terms, gate_bias, picks, held, retained)
        terms = exchange(own, wire, "feat", feat_size)
        wire_type = F32 if head_ranks > 4 else BF16
        wire = mix(layer, terms, read_gain, out_weight, wire_type)
        stream_terms = exchange(wire, wire, "head", head_ranks)
    return finish([stream] + stream_terms)


def solution(mesh):
    return jax.shard_map(
        functools.partial(body, mesh.shape["feat"], mesh.shape["head"]),
        mesh=mesh,
        in_specs=(
            P("groups"),
            P("head", "feat"),
            P(None, "groups", "head", "feat", None),
            P(None, "feat", "head"),
            P(None, "feat", "head"),
            P(None, "feat", "head"),
            P(None, "feat", "head"),
            P(None, "head"),
            P(None, "feat"),
            P(),
            P(None, "head", "feat"),
        ),
        out_specs=P("groups", "feat"),
        check_vma=False,
    )
```

time: 261 us -> 66 us (0.25)
  waiting for transfers between devices: 127 us -> 15.5 us
  blocking collectives: 71.8 us -> 0 us
  matrix products: 33 us -> 0 us
  Pallas kernels: 0 us -> 25.4 us
  starting transfers between devices: 0.13 us -> 24.8 us
  between operations: 13.4 us -> 0.18 us
  other arithmetic: 8.47 us -> 0.01 us
  local copies, waits for them, and re-layouts: 5.56 us -> 0.05 us
    psum x4 -> x0, waiting for transfers between devices: 127 us -> none  [the longest x2 68.3 us: body(): readout = lax.psum(partial_value, 'feat')]
    psum x5 -> x0, blocking collectives: 71.8 us -> none  [the longest x2 35.2 us: body(): lax.psum((part_query, part_key, part_value, part_gate), 'feat')]
    dot_general x22 -> x0, matrix products: 33 us -> none  [the longest x2 16 us: body(): jnp.einsum('rhgf,rhfe->rhge', phi_query, retained[layer_index], preferred...]
    pallas_call x0 -> x11, Pallas kernels: none -> 25.4 us  [the longest x2 10.5 us: read(): pl.pallas_call(functools.partial(read_kernel, layer, sizes, len(terms), c...]
    ppermute x0 -> x21, starting transfers between devices: none -> 24.8 us  [exchange(): lax.ppermute(wire, axis, [(rank, rank ^ step) for rank in range(size)])]
    ppermute x0 -> x21, waiting for transfers between devices: none -> 15.5 us  [exchange(): lax.ppermute(wire, axis, [(rank, rank ^ step) for rank in range(size)])]
    convert_element_type x4 -> x0, other arithmetic: 3.6 us -> none  [the longest x2 2 us: body(): scaled.astype(jnp.bfloat16)]
    reduce_sum x4 -> x0, other arithmetic: 3.17 us -> none  [the longest x2 2.04 us: body(): jnp.mean(readout * readout, axis=-1, keepdims=True) + 1e-06]
  transfers between devices with their start and end apart: 4 -> 21, of which waited for: 4 -> 10; matrix products, arithmetic and copies ran while one was open for 0% -> 0% of each run, Pallas kernels for 0% -> 13%
where the time goes in v1:
time: 66 us; the launch traced here: 65.9 us
  Pallas kernels  25.4 us (38%)
  starting transfers between devices  24.8 us (38%)
  waiting for transfers between devices  15.5 us (23%)
    ppermute x21, starting transfers between devices, exchange(): lax.ppermute(wire, axis, [(rank, rank ^ step) for rank in range(size)])  24.8 us
    ppermute x21, waiting for transfers between devices, exchange(): lax.ppermute(wire, axis, [(rank, rank ^ step) for rank in range(size)])  15.5 us
    pallas_call x2, Pallas kernels, read(): pl.pallas_call(functools.partial(read_kernel, layer, sizes, len(terms), c...  10.5 us
    pallas_call x2, Pallas kernels, fetch(): pl.pallas_call(functools.partial(fetch_kernel, plan, len(sources)), out_s...  8.17 us
    pallas_call x1, Pallas kernels, pick_rows(): pl.pallas_call(pick_kernel, out_shape=jax.ShapeDtypeStruct((requests, wid...  2.62 us
    pallas_call x2, Pallas kernels, project(): pl.pallas_call(functools.partial(project_kernel, layer, len(terms), len(c...  1.68 us
    pallas_call x2, Pallas kernels, mix(): pl.pallas_call(functools.partial(mix_kernel, layer, len(terms)), out_shap...  1.44 us
  transfers between devices with their start and end apart: 21, of which 10 were waited for; matrix products, arithmetic and copies ran while one was open for 0% of the time, Pallas kernels for 13%

profile of v1, /device:TPU:0, one launch (start us, length us, event | category | flops | bytes accessed | tf_op | source)
XLA Modules:
  0.0 65.9 jit_solution(14902484720768353697)
XLA Ops:
  0.0 2.6 %pick_rows.1.refs_0_ = bf16[16,1280]{1,0:T(8,128)(2,1)S(1)} custom-call(s32[16]{0:T(128)} %ids_ref.1, bf16[18992,1280]{1,0:T(8,128)(2,1)} %table_ref.1), custom_call_target="tpu_custom_call" | custom-call | tf_op jit(solution)/shard_map/pick_rows/pallas_call | solution.py:103
  2.6 0.0 copy-start.3
  2.7 2.6 %collective-permute-start.2 = (bf16[16,1280]{1,0:T(8,128)(2,1)S(1)}, bf16[16,1280]{1,0:T(8,128)(2,1)S(1)}, u32[]{:S(2)}, u32[]{:S(2)}) collective-permute-start(bf16[16,1280]{1,0:T(8,128)(2,1)S(1)} %pick_rows.1.refs_0_), channel_id=1, source_target_pairs={{0,3},{1,2},{2,1},{3,0},{4,7},{5,6},{6,5},{7,4},{8,11},{9,10},{10,... | collective-permute-start | bytes 122888 | tf_op jit(solution)/shard_map/ppermute | solution.py:42
  5.2 0.7 %collective-permute-start.1 = (bf16[16,1280]{1,0:T(8,128)(2,1)S(1)}, bf16[16,1280]{1,0:T(8,128)(2,1)S(1)}, u32[]{:S(2)}, u32[]{:S(2)}) collective-permute-start(bf16[16,1280]{1,0:T(8,128)(2,1)S(1)} %pick_rows.1.refs_0_), channel_id=1, source_target_pairs={{0,2},{1,3},{2,0},{3,1},{4,6},{5,7},{6,4},{7,5},{8,10},{9,11},{10,... | collective-permute-start | bytes 122888 | tf_op jit(solution)/shard_map/ppermute | solution.py:42
  5.9 0.0 collective-permute-start
  6.0 1.2 %collective-permute-done.2.refs_3_ = bf16[16,1280]{1,0:T(8,128)(2,1)S(1)} collective-permute-done((bf16[16,1280]{1,0:T(8,128)(2,1)S(1)}, bf16[16,1280]{1,0:T(8,128)(2,1)S(1)}, u32[]{:S(2)}, u32[]{:S(2)}) %collective-permute-start.2) | collective-permute-done | bytes 40992 | tf_op jit(solution)/shard_map/ppermute | solution.py:42
  7.1 2.3 %collective-permute-done.1.refs_2_ = bf16[16,1280]{1,0:T(8,128)(2,1)S(1)} collective-permute-done((bf16[16,1280]{1,0:T(8,128)(2,1)S(1)}, bf16[16,1280]{1,0:T(8,128)(2,1)S(1)}, u32[]{:S(2)}, u32[]{:S(2)}) %collective-permute-start.1) | collective-permute-done | bytes 40992 | tf_op jit(solution)/shard_map/ppermute | solution.py:42
  9.5 0.8 %project.2 = (bf16[16,1280]{1,0:T(8,128)(2,1)S(1)}, f32[16,1920]{1,0:T(8,128)S(1)}, bf16[16,1920]{1,0:T(8,128)(2,1)S(1)}) custom-call(bf16[16,1280]{1,0:T(8,128)(2,1)S(1)} %pick_rows.1.refs_0_, bf16[16,1280]{1,0:T(8,128)(2,1)S(1)} %collective-permute-done.refs_1_, bf16[16,1280]{1,0:T(8,128)(2,1)S(1)} %collective-permute-done.1.refs_2_, ...), custom_call_target="tpu_custom_call" | custom-call | tf_op jit(solution)/shard_map/project/pallas_call | solution.py:215
  10.3 3.6 %collective-permute-start.5 = (bf16[16,1920]{1,0:T(8,128)(2,1)S(1)}, bf16[16,1920]{1,0:T(8,128)(2,1)S(1)}, u32[]{:S(2)}, u32[]{:S(2)}) collective-permute-start(bf16[16,1920]{1,0:T(8,128)(2,1)S(1)} %get-tuple-element.20), channel_id=1, source_target_pairs={{0,12},{4,8},{8,4},{12,0},{1,13},{5,9},{9,5},{13,1},{2,14},{6,10},... | collective-permute-start | bytes 184328 | tf_op jit(solution)/shard_map/ppermute | solution.py:42
  13.9 0.0 collective-permute-start.4
  13.9 0.8 %collective-permute-start.3 = (bf16[16,1920]{1,0:T(8,128)(2,1)S(1)}, bf16[16,1920]{1,0:T(8,128)(2,1)S(1)}, u32[]{:S(2)}, u32[]{:S(2)}) collective-permute-start(bf16[16,1920]{1,0:T(8,128)(2,1)S(1)} %get-tuple-element.20), channel_id=1, source_target_pairs={{0,4},{4,0},{8,12},{12,8},{1,5},{5,1},{9,13},{13,9},{2,6},{6,2},{1... | collective-permute-start | bytes 184328 | tf_op jit(solution)/shard_map/ppermute | solution.py:42
  14.7 0.4 selectors.1
  15.1 0.0 copy-start.6
  15.1 0.0 slice-start
  15.1 4.2 %fetch.2.refs_8_ = bf16[10,2,2064,128]{3,2,1,0:T(8,128)(2,1)S(1)} custom-call(bf16[2,16,2,2064,128]{4,3,2,1,0:T(8,128)(2,1)} %refs_9_.3), custom_call_target="tpu_custom_call" | custom-call | tf_op jit(solution)/shard_map/fetch/pallas_call | solution.py:140
  19.3 0.0 collective-permute-done.5.refs_3_
  19.3 0.0 collective-permute-done.4.refs_2_
  19.4 0.0 copy-start.7
  19.4 5.2 %read.2 = (f32[16,1280]{1,0:T(8,128)S(1)}, bf16[16,1280]{1,0:T(8,128)(2,1)S(1)}) custom-call(f32[16,1920]{1,0:T(8,128)S(1)} %get-tuple-element.19.refs_0_, bf16[16,1920]{1,0:T(8,128)(2,1)S(1)} %collective-permute-done.3.refs_1_, bf16[16,1920]{1,0:T(8,128)(2,1)S(1)} %collective-permute-done.4.refs_2_, bf16[16,1920]{1,0:T(8,128)(2,1)S(1)} %collective-permute-done.5.refs_3_, ...), custom_call_target="tpu_custom_call" | custom-call | tf_op jit(solution)/shard_map/read/pallas_call | solution.py:333
  24.6 3.7 %collective-permute-start.8 = (bf16[16,1280]{1,0:T(8,128)(2,1)S(1)}, bf16[16,1280]{1,0:T(8,128)(2,1)S(1)}, u32[]{:S(2)}, u32[]{:S(2)}) collective-permute-start(bf16[16,1280]{1,0:T(8,128)(2,1)S(1)} %get-tuple-element.25), channel_id=1, source_target_pairs={{0,12},{4,8},{8,4},{12,0},{1,13},{5,9},{9,5},{13,1},{2,14},{6,10},... | collective-permute-start | bytes 122888 | tf_op jit(solution)/shard_map/ppermute | solution.py:42
  28.3 0.0 collective-permute-start.7
  28.3 0.8 %collective-permute-start.6 = (bf16[16,1280]{1,0:T(8,128)(2,1)S(1)}, bf16[16,1280]{1,0:T(8,128)(2,1)S(1)}, u32[]{:S(2)}, u32[]{:S(2)}) collective-permute-start(bf16[16,1280]{1,0:T(8,128)(2,1)S(1)} %get-tuple-element.25), channel_id=1, source_target_pairs={{0,4},{4,0},{8,12},{12,8},{1,5},{5,1},{9,13},{13,9},{2,6},{6,2},{1... | collective-permute-start | bytes 122888 | tf_op jit(solution)/shard_map/ppermute | solution.py:42
  29.1 1.4 %collective-permute-done.8.refs_3_ = bf16[16,1280]{1,0:T(8,128)(2,1)S(1)} collective-permute-done((bf16[16,1280]{1,0:T(8,128)(2,1)S(1)}, bf16[16,1280]{1,0:T(8,128)(2,1)S(1)}, u32[]{:S(2)}, u32[]{:S(2)}) %collective-permute-start.8) | collective-permute-done | bytes 40992 | tf_op jit(solution)/shard_map/ppermute | solution.py:42
  30.5 2.7 %collective-permute-done.7.refs_2_ = bf16[16,1280]{1,0:T(8,128)(2,1)S(1)} collective-permute-done((bf16[16,1280]{1,0:T(8,128)(2,1)S(1)}, bf16[16,1280]{1,0:T(8,128)(2,1)S(1)}, u32[]{:S(2)}, u32[]{:S(2)}) %collective-permute-start.7) | collective-permute-done | bytes 40992 | tf_op jit(solution)/shard_map/ppermute | solution.py:42
  33.2 0.7 %mix.2.refs_1_ = bf16[16,1280]{1,0:T(8,128)(2,1)S(1)} custom-call(f32[16,1280]{1,0:T(8,128)S(1)} %get-tuple-element.24.refs_0_, bf16[16,1280]{1,0:T(8,128)(2,1)S(1)} %collective-permute-done.6.refs_1_, bf16[16,1280]{1,0:T(8,128)(2,1)S(1)} %collective-permute-done.7.refs_2_, bf16[16,1280]{1,0:T(8,128)(2,1)S(1)} %collective-permute-done.8.refs_3_, ...), custom_call_target="tpu_custom_call" | custom-call | tf_op jit(solution)/shard_map/mix/pallas_call | solution.py:369
  33.9 0.0 collective-permute-start.11
  34.0 1.1 %collective-permute-start.10 = (bf16[16,1280]{1,0:T(8,128)(2,1)S(1)}, bf16[16,1280]{1,0:T(8,128)(2,1)S(1)}, u32[]{:S(2)}, u32[]{:S(2)}) collective-permute-start(bf16[16,1280]{1,0:T(8,128)(2,1)S(1)} %mix.2.refs_1_), channel_id=1, source_target_pairs={{0,2},{1,3},{2,0},{3,1},{4,6},{5,7},{6,4},{7,5},{8,10},{9,11},{10,... | collective-permute-start | bytes 122888 | tf_op jit(solution)/shard_map/ppermute | solution.py:42
  35.1 0.7 %collective-permute-start.9 = (bf16[16,1280]{1,0:T(8,128)(2,1)S(1)}, bf16[16,1280]{1,0:T(8,128)(2,1)S(1)}, u32[]{:S(2)}, u32[]{:S(2)}) collective-permute-start(bf16[16,1280]{1,0:T(8,128)(2,1)S(1)} %mix.2.refs_1_), channel_id=1, source_target_pairs={{0,1},{1,0},{2,3},{3,2},{4,5},{5,4},{6,7},{7,6},{8,9},{9,8},{10,11... | collective-permute-start | bytes 122888 | tf_op jit(solution)/shard_map/ppermute | solution.py:42
  35.8 1.6 %collective-permute-done.11.refs_4_ = bf16[16,1280]{1,0:T(8,128)(2,1)S(1)} collective-permute-done((bf16[16,1280]{1,0:T(8,128)(2,1)S(1)}, bf16[16,1280]{1,0:T(8,128)(2,1)S(1)}, u32[]{:S(2)}, u32[]{:S(2)}) %collective-permute-start.11) | collective-permute-done | bytes 40992 | tf_op jit(solution)/shard_map/ppermute | solution.py:42
  37.5 0.9 %collective-permute-done.10.refs_3_ = bf16[16,1280]{1,0:T(8,128)(2,1)S(1)} collective-permute-done((bf16[16,1280]{1,0:T(8,128)(2,1)S(1)}, bf16[16,1280]{1,0:T(8,128)(2,1)S(1)}, u32[]{:S(2)}, u32[]{:S(2)}) %collective-permute-start.10) | collective-permute-done | bytes 40992 | tf_op jit(solution)/shard_map/ppermute | solution.py:42
  38.3 0.8 %project.3 = (bf16[16,1280]{1,0:T(8,128)(2,1)S(1)}, f32[16,1920]{1,0:T(8,128)S(1)}, bf16[16,1920]{1,0:T(8,128)(2,1)S(1)}) custom-call(bf16[16,1280]{1,0:T(8,128)(2,1)S(1)} %get-tuple-element.18.refs_0_, bf16[16,1280]{1,0:T(8,128)(2,1)S(1)} %mix.2.refs_1_, bf16[16,1280]{1,0:T(8,128)(2,1)S(1)} %collective-permute-done.9.refs_2_, ...), custom_call_target="tpu_custom_call" | custom-call | tf_op jit(solution)/shard_map/project/pallas_call | solution.py:215
  39.1 1.5 %collective-permute-start.14 = (bf16[16,1920]{1,0:T(8,128)(2,1)S(1)}, bf16[16,1920]{1,0:T(8,128)(2,1)S(1)}, u32[]{:S(2)}, u32[]{:S(2)}) collective-permute-start(bf16[16,1920]{1,0:T(8,128)(2,1)S(1)} %get-tuple-element.28), channel_id=1, source_target_pairs={{0,12},{4,8},{8,4},{12,0},{1,13},{5,9},{9,5},{13,1},{2,14},{6,10},... | collective-permute-start | bytes 184328 | tf_op jit(solution)/shard_map/ppermute | solution.py:42
  40.6 0.6 collective-permute-start.13
  41.3 2.3 %collective-permute-start.12 = (bf16[16,1920]{1,0:T(8,128)(2,1)S(1)}, bf16[16,1920]{1,0:T(8,128)(2,1)S(1)}, u32[]{:S(2)}, u32[]{:S(2)}) collective-permute-start(bf16[16,1920]{1,0:T(8,128)(2,1)S(1)} %get-tuple-element.28), channel_id=1, source_target_pairs={{0,4},{4,0},{8,12},{12,8},{1,5},{5,1},{9,13},{13,9},{2,6},{6,2},{1... | collective-permute-start | bytes 184328 | tf_op jit(solution)/shard_map/ppermute | solution.py:42
  43.6 4.0 %fetch.3.refs_8_ = bf16[10,2,2064,128]{3,2,1,0:T(8,128)(2,1)S(1)} custom-call(bf16[2,16,2,2064,128]{4,3,2,1,0:T(8,128)(2,1)} %refs_9_.3), custom_call_target="tpu_custom_call" | custom-call | tf_op jit(solution)/shard_map/fetch/pallas_call | solution.py:140
  47.6 0.0 collective-permute-done.13.refs_2_
  47.6 5.3 %read.3 = (f32[16,1280]{1,0:T(8,128)S(1)}, bf16[16,1280]{1,0:T(8,128)(2,1)S(1)}) custom-call(f32[16,1920]{1,0:T(8,128)S(1)} %get-tuple-element.27.refs_0_, bf16[16,1920]{1,0:T(8,128)(2,1)S(1)} %collective-permute-done.12.refs_1_, bf16[16,1920]{1,0:T(8,128)(2,1)S(1)} %collective-permute-done.13.refs_2_, bf16[16,1920]{1,0:T(8,128)(2,1)S(1)} %collective-permute-done.14.refs_3_, ...), custom_call_target="tpu_custom_call" | custom-call | tf_op jit(solution)/shard_map/read/pallas_call | solution.py:333
  52.9 2.5 %collective-permute-start.17 = (bf16[16,1280]{1,0:T(8,128)(2,1)S(1)}, bf16[16,1280]{1,0:T(8,128)(2,1)S(1)}, u32[]{:S(2)}, u32[]{:S(2)}) collective-permute-start(bf16[16,1280]{1,0:T(8,128)(2,1)S(1)} %get-tuple-element.30), channel_id=1, source_target_pairs={{0,12},{4,8},{8,4},{12,0},{1,13},{5,9},{9,5},{13,1},{2,14},{6,10},... | collective-permute-start | bytes 122888 | tf_op jit(solution)/shard_map/ppermute | solution.py:42
  55.4 2.0 %collective-permute-start.15 = (bf16[16,1280]{1,0:T(8,128)(2,1)S(1)}, bf16[16,1280]{1,0:T(8,128)(2,1)S(1)}, u32[]{:S(2)}, u32[]{:S(2)}) collective-permute-start(bf16[16,1280]{1,0:T(8,128)(2,1)S(1)} %get-tuple-element.30), channel_id=1, source_target_pairs={{0,4},{4,0},{8,12},{12,8},{1,5},{5,1},{9,13},{13,9},{2,6},{6,2},{1... | collective-permute-start | bytes 122888 | tf_op jit(solution)/shard_map/ppermute | solution.py:42
  57.4 1.5 %collective-permute-done.17.refs_3_ = bf16[16,1280]{1,0:T(8,128)(2,1)S(1)} collective-permute-done((bf16[16,1280]{1,0:T(8,128)(2,1)S(1)}, bf16[16,1280]{1,0:T(8,128)(2,1)S(1)}, u32[]{:S(2)}, u32[]{:S(2)}) %collective-permute-start.17) | collective-permute-done | bytes 40992 | tf_op jit(solution)/shard_map/ppermute | solution.py:42
  58.9 1.4 %collective-permute-done.16.refs_2_ = bf16[16,1280]{1,0:T(8,128)(2,1)S(1)} collective-permute-done((bf16[16,1280]{1,0:T(8,128)(2,1)S(1)}, bf16[16,1280]{1,0:T(8,128)(2,1)S(1)}, u32[]{:S(2)}, u32[]{:S(2)}) %collective-permute-start.16) | collective-permute-done | bytes 40992 | tf_op jit(solution)/shard_map/ppermute | solution.py:42
  60.3 0.7 %mix.3.refs_1_ = bf16[16,1280]{1,0:T(8,128)(2,1)S(1)} custom-call(f32[16,1280]{1,0:T(8,128)S(1)} %get-tuple-element.29.refs_0_, bf16[16,1280]{1,0:T(8,128)(2,1)S(1)} %collective-permute-done.15.refs_1_, bf16[16,1280]{1,0:T(8,128)(2,1)S(1)} %collective-permute-done.16.refs_2_, bf16[16,1280]{1,0:T(8,128)(2,1)S(1)} %collective-permute-done.17.refs_3_, ...), custom_call_target="tpu_custom_call" | custom-call | tf_op jit(solution)/shard_map/mix/pallas_call | solution.py:369
  61.0 0.1 collective-permute-start.20
  61.1 1.2 %collective-permute-start.19 = (bf16[16,1280]{1,0:T(8,128)(2,1)S(1)}, bf16[16,1280]{1,0:T(8,128)(2,1)S(1)}, u32[]{:S(2)}, u32[]{:S(2)}) collective-permute-start(bf16[16,1280]{1,0:T(8,128)(2,1)S(1)} %mix.3.refs_1_), channel_id=1, source_target_pairs={{0,2},{1,3},{2,0},{3,1},{4,6},{5,7},{6,4},{7,5},{8,10},{9,11},{10,... | collective-permute-start | bytes 122888 | tf_op jit(solution)/shard_map/ppermute | solution.py:42
  62.4 0.6 collective-permute-start.18
  62.9 1.8 %collective-permute-done.20.refs_4_ = bf16[16,1280]{1,0:T(8,128)(2,1)S(1)} collective-permute-done((bf16[16,1280]{1,0:T(8,128)(2,1)S(1)}, bf16[16,1280]{1,0:T(8,128)(2,1)S(1)}, u32[]{:S(2)}, u32[]{:S(2)}) %collective-permute-start.20) | collective-permute-done | bytes 40992 | tf_op jit(solution)/shard_map/ppermute | solution.py:42
  64.8 0.5 collective-permute-done.19.refs_3_
  65.3 0.7 finish.1
  (26 shorter events, 0.1 us)
Async XLA Ops:
  0.0 9.4 %copy-start.4 = (f32[2,1280]{1,0:T(2,128)S(1)}, f32[2,1280]{1,0:T(2,128)}, u32[]{:S(2)}) copy-start(f32[2,1280]{1,0:T(2,128)} %refs_5_.6) | copy-start | bytes 30724
  0.0 9.4 %copy-start.2 = (bf16[2,1280,256]{2,1,0:T(8,128)(2,1)S(1)}, bf16[2,1280,256]{2,1,0:T(8,128)(2,1)}, u32[]{:S(2)}) copy-start(bf16[2,1280,256]{2,1,0:T(8,128)(2,1)} %refs_8_.1) | copy-start | bytes 3932164
  0.0 9.4 %copy-start.1 = (bf16[2,1280,256]{2,1,0:T(8,128)(2,1)S(1)}, bf16[2,1280,256]{2,1,0:T(8,128)(2,1)}, u32[]{:S(2)}) copy-start(bf16[2,1280,256]{2,1,0:T(8,128)(2,1)} %refs_7_.3) | copy-start | bytes 3932164
  0.0 9.4 %copy-start = (bf16[2,1280,1280]{2,1,0:T(8,128)(2,1)S(1)}, bf16[2,1280,1280]{2,1,0:T(8,128)(2,1)}, u32[]{:S(2)}) copy-start(bf16[2,1280,1280]{2,1,0:T(8,128)(2,1)} %refs_6_.3) | copy-start | bytes 19660804
  0.0 9.4 %copy-start.5 = (bf16[2,1280,2]{1,2,0:T(2,128)(2,1)S(1)}, bf16[2,1280,2]{1,2,0:T(2,128)(2,1)}, u32[]{:S(2)}) copy-start(bf16[2,1280,2]{1,2,0:T(2,128)(2,1)} %param.18) | copy-start | bytes 30724
  2.6 12.1 %copy-start.3 = (s32[4,2,2064]{2,1,0:T(2,128)S(1)}, s32[4,2,2064]{2,1,0:T(2,128)}, u32[]{:S(2)}) copy-start(s32[4,2,2064]{2,1,0:T(2,128)} %constant.2.clone.pairs_ref) | copy-start | bytes 198148
  2.7 4.5 %collective-permute-start.2 = (bf16[16,1280]{1,0:T(8,128)(2,1)S(1)}, bf16[16,1280]{1,0:T(8,128)(2,1)S(1)}, u32[]{:S(2)}, u32[]{:S(2)}) collective-permute-start(bf16[16,1280]{1,0:T(8,128)(2,1)S(1)} %pick_rows.1.refs_0_), channel_id=1, source_target_pairs={{0,3},{1,2},{2,1},{3,0},{4,7},{5,6},{6,5},{7,4},{8,11},{9,10},{10,... | collective-permute-start | bytes 122888 | tf_op jit(solution)/shard_map/ppermute | solution.py:42
  5.2 4.2 %collective-permute-start.1 = (bf16[16,1280]{1,0:T(8,128)(2,1)S(1)}, bf16[16,1280]{1,0:T(8,128)(2,1)S(1)}, u32[]{:S(2)}, u32[]{:S(2)}) collective-permute-start(bf16[16,1280]{1,0:T(8,128)(2,1)S(1)} %pick_rows.1.refs_0_), channel_id=1, source_target_pairs={{0,2},{1,3},{2,0},{3,1},{4,6},{5,7},{6,4},{7,5},{8,10},{9,11},{10,... | collective-permute-start | bytes 122888 | tf_op jit(solution)/shard_map/ppermute | solution.py:42
  5.9 3.5 %collective-permute-start = (bf16[16,1280]{1,0:T(8,128)(2,1)S(1)}, bf16[16,1280]{1,0:T(8,128)(2,1)S(1)}, u32[]{:S(2)}, u32[]{:S(2)}) collective-permute-start(bf16[16,1280]{1,0:T(8,128)(2,1)S(1)} %pick_rows.1.refs_0_), channel_id=1, source_target_pairs={{0,1},{1,0},{2,3},{3,2},{4,5},{5,4},{6,7},{7,6},{8,9},{9,8},{10,11... | collective-permute-start | bytes 122888 | tf_op jit(solution)/shard_map/ppermute | solution.py:42
  10.3 9.0 %collective-permute-start.5 = (bf16[16,1920]{1,0:T(8,128)(2,1)S(1)}, bf16[16,1920]{1,0:T(8,128)(2,1)S(1)}, u32[]{:S(2)}, u32[]{:S(2)}) collective-permute-start(bf16[16,1920]{1,0:T(8,128)(2,1)S(1)} %get-tuple-element.20), channel_id=1, source_target_pairs={{0,12},{4,8},{8,4},{12,0},{1,13},{5,9},{9,5},{13,1},{2,14},{6,10},... | collective-permute-start | bytes 184328 | tf_op jit(solution)/shard_map/ppermute | solution.py:42
  13.9 5.4 %collective-permute-start.4 = (bf16[16,1920]{1,0:T(8,128)(2,1)S(1)}, bf16[16,1920]{1,0:T(8,128)(2,1)S(1)}, u32[]{:S(2)}, u32[]{:S(2)}) collective-permute-start(bf16[16,1920]{1,0:T(8,128)(2,1)S(1)} %get-tuple-element.20), channel_id=1, source_target_pairs={{0,8},{4,12},{8,0},{12,4},{1,9},{5,13},{9,1},{13,5},{2,10},{6,14},... | collective-permute-start | bytes 184328 | tf_op jit(solution)/shard_map/ppermute | solution.py:42
  13.9 5.4 %collective-permute-start.3 = (bf16[16,1920]{1,0:T(8,128)(2,1)S(1)}, bf16[16,1920]{1,0:T(8,128)(2,1)S(1)}, u32[]{:S(2)}, u32[]{:S(2)}) collective-permute-start(bf16[16,1920]{1,0:T(8,128)(2,1)S(1)} %get-tuple-element.20), channel_id=1, source_target_pairs={{0,4},{4,0},{8,12},{12,8},{1,5},{5,1},{9,13},{13,9},{2,6},{6,2},{1... | collective-permute-start | bytes 184328 | tf_op jit(solution)/shard_map/ppermute | solution.py:42
  15.1 4.3 %copy-start.6 = (f32[2,2]{1,0:T(2,128)S(1)}, f32[2,2]{1,0:T(2,128)}, u32[]{:S(2)}) copy-start(f32[2,2]{1,0:T(2,128)} %refs_4_.8) | copy-start | bytes 52
  15.1 18.1 %slice-start = ((s8[6553600]{0:T(1024)(128)(4,1)}), s8[4194304]{0:T(1024)(128)(4,1)S(1)}, s32[]{:S(2)}) async-start(s8[6553600]{0:T(1024)(128)(4,1)} %bitcast.1), calls=%async_computation | async-start | bytes 8388608
  19.3 13.8 %slice-start.1 = ((s8[6553600]{0:T(1024)(128)(4,1)}), s8[2359296]{0:T(1024)(128)(4,1)S(1)}, s32[]{:S(2)}) async-start(s8[6553600]{0:T(1024)(128)(4,1)} %bitcast.1), calls=%async_computation.1 | async-start | bytes 4718592
  19.4 13.8 %copy-start.7 = (f32[2,128]{1,0:T(2,128)S(1)}, f32[2,128]{1,0:T(2,128)}, u32[]{:S(2)}) copy-start(f32[2,128]{1,0:T(2,128)} %refs_4_.9) | copy-start | bytes 3076
  24.6 5.9 %collective-permute-start.8 = (bf16[16,1280]{1,0:T(8,128)(2,1)S(1)}, bf16[16,1280]{1,0:T(8,128)(2,1)S(1)}, u32[]{:S(2)}, u32[]{:S(2)}) collective-permute-start(bf16[16,1280]{1,0:T(8,128)(2,1)S(1)} %get-tuple-element.25), channel_id=1, source_target_pairs={{0,12},{4,8},{8,4},{12,0},{1,13},{5,9},{9,5},{13,1},{2,14},{6,10},... | collective-permute-start | bytes 122888 | tf_op jit(solution)/shard_map/ppermute | solution.py:42
  28.3 4.9 %collective-permute-start.7 = (bf16[16,1280]{1,0:T(8,128)(2,1)S(1)}, bf16[16,1280]{1,0:T(8,128)(2,1)S(1)}, u32[]{:S(2)}, u32[]{:S(2)}) collective-permute-start(bf16[16,1280]{1,0:T(8,128)(2,1)S(1)} %get-tuple-element.25), channel_id=1, source_target_pairs={{0,8},{4,12},{8,0},{12,4},{1,9},{5,13},{9,1},{13,5},{2,10},{6,14},... | collective-permute-start | bytes 122888 | tf_op jit(solution)/shard_map/ppermute | solution.py:42
  28.3 4.9 %collective-permute-start.6 = (bf16[16,1280]{1,0:T(8,128)(2,1)S(1)}, bf16[16,1280]{1,0:T(8,128)(2,1)S(1)}, u32[]{:S(2)}, u32[]{:S(2)}) collective-permute-start(bf16[16,1280]{1,0:T(8,128)(2,1)S(1)} %get-tuple-element.25), channel_id=1, source_target_pairs={{0,4},{4,0},{8,12},{12,8},{1,5},{5,1},{9,13},{13,9},{2,6},{6,2},{1... | collective-permute-start | bytes 122888 | tf_op jit(solution)/shard_map/ppermute | solution.py:42
  33.9 3.5 %collective-permute-start.11 = (bf16[16,1280]{1,0:T(8,128)(2,1)S(1)}, bf16[16,1280]{1,0:T(8,128)(2,1)S(1)}, u32[]{:S(2)}, u32[]{:S(2)}) collective-permute-start(bf16[16,1280]{1,0:T(8,128)(2,1)S(1)} %mix.2.refs_1_), channel_id=1, source_target_pairs={{0,3},{1,2},{2,1},{3,0},{4,7},{5,6},{6,5},{7,4},{8,11},{9,10},{10,... | collective-permute-start | bytes 122888 | tf_op jit(solution)/shard_map/ppermute | solution.py:42
  34.0 4.4 %collective-permute-start.10 = (bf16[16,1280]{1,0:T(8,128)(2,1)S(1)}, bf16[16,1280]{1,0:T(8,128)(2,1)S(1)}, u32[]{:S(2)}, u32[]{:S(2)}) collective-permute-start(bf16[16,1280]{1,0:T(8,128)(2,1)S(1)} %mix.2.refs_1_), channel_id=1, source_target_pairs={{0,2},{1,3},{2,0},{3,1},{4,6},{5,7},{6,4},{7,5},{8,10},{9,11},{10,... | collective-permute-start | bytes 122888 | tf_op jit(solution)/shard_map/ppermute | solution.py:42
  35.1 3.2 %collective-permute-start.9 = (bf16[16,1280]{1,0:T(8,128)(2,1)S(1)}, bf16[16,1280]{1,0:T(8,128)(2,1)S(1)}, u32[]{:S(2)}, u32[]{:S(2)}) collective-permute-start(bf16[16,1280]{1,0:T(8,128)(2,1)S(1)} %mix.2.refs_1_), channel_id=1, source_target_pairs={{0,1},{1,0},{2,3},{3,2},{4,5},{5,4},{6,7},{7,6},{8,9},{9,8},{10,11... | collective-permute-start | bytes 122888 | tf_op jit(solution)/shard_map/ppermute | solution.py:42
  39.1 8.4 %collective-permute-start.14 = (bf16[16,1920]{1,0:T(8,128)(2,1)S(1)}, bf16[16,1920]{1,0:T(8,128)(2,1)S(1)}, u32[]{:S(2)}, u32[]{:S(2)}) collective-permute-start(bf16[16,1920]{1,0:T(8,128)(2,1)S(1)} %get-tuple-element.28), channel_id=1, source_target_pairs={{0,12},{4,8},{8,4},{12,0},{1,13},{5,9},{9,5},{13,1},{2,14},{6,10},... | collective-permute-start | bytes 184328 | tf_op jit(solution)/shard_map/ppermute | solution.py:42
  40.6 7.0 %collective-permute-start.13 = (bf16[16,1920]{1,0:T(8,128)(2,1)S(1)}, bf16[16,1920]{1,0:T(8,128)(2,1)S(1)}, u32[]{:S(2)}, u32[]{:S(2)}) collective-permute-start(bf16[16,1920]{1,0:T(8,128)(2,1)S(1)} %get-tuple-element.28), channel_id=1, source_target_pairs={{0,8},{4,12},{8,0},{12,4},{1,9},{5,13},{9,1},{13,5},{2,10},{6,14},... | collective-permute-start | bytes 184328 | tf_op jit(solution)/shard_map/ppermute | solution.py:42
  41.3 6.4 %collective-permute-start.12 = (bf16[16,1920]{1,0:T(8,128)(2,1)S(1)}, bf16[16,1920]{1,0:T(8,128)(2,1)S(1)}, u32[]{:S(2)}, u32[]{:S(2)}) collective-permute-start(bf16[16,1920]{1,0:T(8,128)(2,1)S(1)} %get-tuple-element.28), channel_id=1, source_target_pairs={{0,4},{4,0},{8,12},{12,8},{1,5},{5,1},{9,13},{13,9},{2,6},{6,2},{1... | collective-permute-start | bytes 184328 | tf_op jit(solution)/shard_map/ppermute | solution.py:42
  52.9 6.0 %collective-permute-start.17 = (bf16[16,1280]{1,0:T(8,128)(2,1)S(1)}, bf16[16,1280]{1,0:T(8,128)(2,1)S(1)}, u32[]{:S(2)}, u32[]{:S(2)}) collective-permute-start(bf16[16,1280]{1,0:T(8,128)(2,1)S(1)} %get-tuple-element.30), channel_id=1, source_target_pairs={{0,12},{4,8},{8,4},{12,0},{1,13},{5,9},{9,5},{13,1},{2,14},{6,10},... | collective-permute-start | bytes 122888 | tf_op jit(solution)/shard_map/ppermute | solution.py:42
  55.4 4.9 %collective-permute-start.16 = (bf16[16,1280]{1,0:T(8,128)(2,1)S(1)}, bf16[16,1280]{1,0:T(8,128)(2,1)S(1)}, u32[]{:S(2)}, u32[]{:S(2)}) collective-permute-start(bf16[16,1280]{1,0:T(8,128)(2,1)S(1)} %get-tuple-element.30), channel_id=1, source_target_pairs={{0,8},{4,12},{8,0},{12,4},{1,9},{5,13},{9,1},{13,5},{2,10},{6,14},... | collective-permute-start | bytes 122888 | tf_op jit(solution)/shard_map/ppermute | solution.py:42
  55.4 4.9 %collective-permute-start.15 = (bf16[16,1280]{1,0:T(8,128)(2,1)S(1)}, bf16[16,1280]{1,0:T(8,128)(2,1)S(1)}, u32[]{:S(2)}, u32[]{:S(2)}) collective-permute-start(bf16[16,1280]{1,0:T(8,128)(2,1)S(1)} %get-tuple-element.30), channel_id=1, source_target_pairs={{0,4},{4,0},{8,12},{12,8},{1,5},{5,1},{9,13},{13,9},{2,6},{6,2},{1... | collective-permute-start | bytes 122888 | tf_op jit(solution)/shard_map/ppermute | solution.py:42
  61.0 3.7 %collective-permute-start.20 = (bf16[16,1280]{1,0:T(8,128)(2,1)S(1)}, bf16[16,1280]{1,0:T(8,128)(2,1)S(1)}, u32[]{:S(2)}, u32[]{:S(2)}) collective-permute-start(bf16[16,1280]{1,0:T(8,128)(2,1)S(1)} %mix.3.refs_1_), channel_id=1, source_target_pairs={{0,3},{1,2},{2,1},{3,0},{4,7},{5,6},{6,5},{7,4},{8,11},{9,10},{10,... | collective-permute-start | bytes 122888 | tf_op jit(solution)/shard_map/ppermute | solution.py:42
  61.1 4.2 %collective-permute-start.19 = (bf16[16,1280]{1,0:T(8,128)(2,1)S(1)}, bf16[16,1280]{1,0:T(8,128)(2,1)S(1)}, u32[]{:S(2)}, u32[]{:S(2)}) collective-permute-start(bf16[16,1280]{1,0:T(8,128)(2,1)S(1)} %mix.3.refs_1_), channel_id=1, source_target_pairs={{0,2},{1,3},{2,0},{3,1},{4,6},{5,7},{6,4},{7,5},{8,10},{9,11},{10,... | collective-permute-start | bytes 122888 | tf_op jit(solution)/shard_map/ppermute | solution.py:42
  62.4 2.9 %collective-permute-start.18 = (bf16[16,1280]{1,0:T(8,128)(2,1)S(1)}, bf16[16,1280]{1,0:T(8,128)(2,1)S(1)}, u32[]{:S(2)}, u32[]{:S(2)}) collective-permute-start(bf16[16,1280]{1,0:T(8,128)(2,1)S(1)} %mix.3.refs_1_), channel_id=1, source_target_pairs={{0,1},{1,0},{2,3},{3,2},{4,5},{5,4},{6,7},{7,6},{8,9},{9,8},{10,11... | collective-permute-start | bytes 122888 | tf_op jit(solution)/shard_map/ppermute | solution.py:42

commit v2 on v1

--- a/solution.py
+++ b/solution.py
@@ -9,16 +9,18 @@
 from jax.experimental.pallas import tpu as pltpu
 from jax.sharding import PartitionSpec as P
 
-D = 5120
 EPS = 1e-6
 LANES = 128
-SLOTS = 8
+SUBLANES = 8
 ROWS = 16
+FIRST_LAYER = (0, 7, 9)
+LATER_LAYER = (5, 4, 7)
 MIB = 2**20
 F32 = jnp.float32
 BF16 = jnp.bfloat16
 
 VMEM_SPEC = pl.BlockSpec(memory_space=pltpu.VMEM)
+ANY_SPEC = pl.BlockSpec(memory_space=pl.ANY)
 HBM_SPEC = pl.BlockSpec(memory_space=pltpu.HBM)
 SMEM_SPEC = pl.BlockSpec(memory_space=pltpu.SMEM)
 
@@ -35,12 +37,16 @@
     return pltpu.with_memory_space_constraint(array, pltpu.HBM)
 
 
+def wire_type(size):
+    return BF16 if size <= 4 else F32
+
+
 def exchange(own, wire, axis, size):
-    if size > 4:
-        return [lax.psum(own.astype(F32), axis)]
+    if wire_type(size) == F32:
+        return [own.astype(F32) - wire.astype(F32), lax.psum(wire.astype(F32), axis)]
     others = [
         lax.ppermute(wire, axis, [(rank, rank ^ step) for rank in range(size)])
-        for step in range(1, size)
+        for step in reversed(range(1, size))
     ]
     return [own] + others
 
@@ -70,6 +76,7 @@
     row_at = lax.broadcasted_iota(jnp.int32, (requests, requests * ROWS), 0)
     column_at = lax.broadcasted_iota(jnp.int32, (requests, requests * ROWS), 1)
     chosen = jnp.zeros((requests, requests * ROWS), F32)
+    groups_ref[...] = jnp.zeros_like(groups_ref)
     copies = []
     for request in range(requests):
         local_id = ids_ref[request] - row_start
@@ -81,12 +88,12 @@
             groups_ref.at[pl.ds(request * ROWS, ROWS), :],
             sems.at[request],
         )
-        copy.start()
-        copies.append(copy)
+        pl.when(inside)(copy.start)
+        copies.append((inside, copy))
         place = jnp.where(inside, request * ROWS + row - first, -1)
         chosen = jnp.where((row_at == request) & (column_at == place), 1.0, chosen)
-    for copy in copies:
-        copy.wait()
+    for inside, copy in copies:
+        pl.when(inside)(copy.wait)
     out_ref[...] = jnp.dot(
         chosen.astype(BF16), groups_ref[...], preferred_element_type=F32
     ).astype(BF16)
@@ -176,10 +183,10 @@
     )(jnp.asarray(pairs))
 
 
-def project_kernel(layer, count, carried, *refs):
+def project_kernel(layer, count, carried, held, *refs):
     terms = refs[carried:count]
     gain_ref, query_ref, key_ref, value_ref, gate_ref = refs[count : count + 5]
-    stream_ref, own_ref, wire_ref = refs[count + 5 :]
+    stream_ref, own_ref, wire_ref = refs[count + 5 + held :]
     stream = add_terms(terms)
     if carried:
         stream = refs[0][...].astype(F32) + stream
@@ -193,7 +200,7 @@
         width = weight_ref.shape[2]
         part = split_dot(scaled, weight_ref[layer])
         own_ref[:, start : start + width] = part
-        wire_ref[:, start : start + width] = part.astype(BF16)
+        wire_ref[:, start : start + width] = part.astype(wire_ref.dtype)
         start += width
     lane = lax.broadcasted_iota(jnp.int32, (stream.shape[0], LANES), 1)
     half = LANES // 2
@@ -205,65 +212,60 @@
         extra = jnp.where(place == head + 1, gate, extra)
     own_ref[:, start:] = jnp.where(lane < half, extra, 0.0)
     rounded = extra.astype(BF16).astype(F32)
-    wire_ref[:, start:] = jnp.where(lane < half, rounded, extra - rounded).astype(BF16)
-
-
-def project(layer, carried, terms, norm_gain, weights, gate_weight):
+    wire_ref[:, start:] = jnp.where(lane < half, rounded, extra - rounded).astype(wire_ref.dtype)
+
+
+def project(layer, carried, wire, terms, norm_gain, weights, gate_weight, held):
     terms = carried + terms
     requests, width = terms[0].shape
     total = sum(weight.shape[2] for weight in weights) + LANES
     return pl.pallas_call(
-        functools.partial(project_kernel, layer, len(terms), len(carried)),
+        functools.partial(project_kernel, layer, len(terms), len(carried), len(held)),
         out_shape=[
             jax.ShapeDtypeStruct((requests, width), BF16),
             jax.ShapeDtypeStruct((requests, total), F32),
-            jax.ShapeDtypeStruct((requests, total), BF16),
+            jax.ShapeDtypeStruct((requests, total), wire),
         ],
-        in_specs=[VMEM_SPEC] * (len(terms) + 5),
+        in_specs=[VMEM_SPEC] * (len(terms) + 5) + [ANY_SPEC] * len(held),
         out_specs=[VMEM_SPEC] * 3,
         compiler_params=params(8),
         name="project",
-    )(*terms, norm_gain, *[resident(weight) for weight in weights], gate_weight)
+    )(
+        *terms,
+        norm_gain,
+        *[resident(weight) for weight in weights],
+        gate_weight,
+        *[resident(part) for part in held],
+    )
 
 
 def read_kernel(layer, sizes, count, held, *refs):
-    local_heads, group_size, head_size = sizes
+    local_heads, group_size, slots, head_size, model_width = sizes
     terms = refs[:count]
     bias_ref, left_ref, right_ref, scale_ref = refs[count : count + 4]
     held_refs = refs[count + 4 : count + 4 + len(held)]
     rest = refs[count + 4 + len(held) :]
-    state_ref, own_ref, wire_ref, rows_ref, phi_ref, cross_ref, history_ref, late_ref, sems = rest
+    own_ref, wire_ref, rows_ref, phi_ref, history_ref = rest
     requests = own_ref.shape[0]
-    block_feat = phi_ref.shape[2]
-    early = sum(held)
-    copies = []
-    for at in range(requests - early):
-        copy = pltpu.make_async_copy(state_ref.at[layer, early + at], late_ref.at[at], sems.at[at])
-        copy.start()
-        copies.append(copy)
-
+    block_feat = phi_ref.shape[1]
     total = add_terms(terms)
     query_width = local_heads * group_size * head_size
     kv_width = local_heads * head_size
     extra = total[:, query_width + 2 * kv_width :]
     half = LANES // 2
     extra = extra[:, :half] + extra[:, half:]
-    inverse = lax.rsqrt(extra[:, 0:1] / D + EPS)
+    inverse = lax.rsqrt(extra[:, 0:1] / model_width + EPS)
     normed = total[:, : query_width + 2 * kv_width] * inverse
 
-    span = local_heads * SLOTS
-    key_slot = group_size
+    span = local_heads * slots
     for head in range(local_heads):
-        for slot in range(SLOTS):
+        for slot in range(slots):
             if slot < group_size:
                 start = (head * group_size + slot) * head_size
                 part = normed[:, start : start + head_size]
-            elif slot == key_slot:
-                start = query_width + head * head_size
-                part = normed[:, start : start + head_size]
             else:
                 part = jnp.zeros((requests, head_size), F32)
-            rows_ref[pl.ds(head * SLOTS + slot, requests, stride=span), :] = part
+            rows_ref[pl.ds(head * slots + slot, requests, stride=span), :] = part
     vectors = jnp.concatenate(split(rows_ref[...]), axis=1)
 
     step = 2 * LANES
@@ -271,29 +273,16 @@
         stop = min(start + step, block_feat)
         left = jnp.dot(vectors, left_ref[:, start:stop], preferred_element_type=F32)
         right = jnp.dot(vectors, right_ref[:, start:stop], preferred_element_type=F32)
-        phi = left * right * scale_ref[:, start:stop]
-        for part, values in enumerate(split(phi)):
-            phi_ref[part, :, start:stop] = values
-        wide = phi.reshape(requests * local_heads, SLOTS, stop - start)
-        cross = (wide * wide[:, key_slot : key_slot + 1, :]).reshape(-1, stop - start)
-        for at in range(0, stop - start, LANES):
-            lanes = min(LANES, stop - start - at)
-            piece = cross[:, at : at + lanes]
-            if start + at == 0:
-                cross_ref[:, :lanes] = piece
-            else:
-                cross_ref[:, :lanes] += piece
+        phi_ref[:, start:stop] = (left * right * scale_ref[:, start:stop]).astype(BF16)
 
     def one_request(request, states):
-        mine = slice(request * span, (request + 1) * span)
-        rows = jnp.concatenate([phi_ref[0, mine, :], phi_ref[1, mine, :]], axis=0)
+        rows = phi_ref[request * span : (request + 1) * span, :]
         state = jnp.concatenate(states, axis=1) if local_heads > 1 else states[0]
         out = jnp.dot(rows, state, preferred_element_type=F32)
-        out = out[:span] + out[span:]
         for head in range(local_heads):
-            at = head * SLOTS
-            history_ref[request * span + at : request * span + at + SLOTS, :] = out[
-                at : at + SLOTS, head * head_size : (head + 1) * head_size
+            at = head * slots
+            history_ref[request * span + at : request * span + at + slots, :] = out[
+                at : at + slots, head * head_size : (head + 1) * head_size
             ]
 
     request = 0
@@ -301,59 +290,54 @@
         for at in range(many):
             one_request(request, [held_ref[at, head] for head in range(local_heads)])
             request += 1
-    for at, copy in enumerate(copies):
-        copy.wait()
-        one_request(request, [late_ref[at, head] for head in range(local_heads)])
-        request += 1
 
     for head in range(local_heads):
         logit = extra[:, head + 1 : head + 2] * inverse
         logit = logit + bias_ref[layer : layer + 1, head : head + 1]
         softplus = jnp.maximum(logit, 0.0) + jnp.log(1.0 + jnp.exp(-jnp.abs(logit)))
         decay = jnp.exp(-softplus)
-        start = query_width + kv_width + head * head_size
-        value = normed[:, start : start + head_size]
+        start = query_width + head * head_size
+        key = normed[:, start : start + head_size]
+        value = normed[:, start + kv_width : start + kv_width + head_size]
         for slot in range(group_size):
-            picked = pl.ds(head * SLOTS + slot, requests, stride=span)
-            cross = jnp.sum(cross_ref[picked, :], axis=1, keepdims=True) / head_size
-            part = decay * history_ref[picked, :] + cross * value
             start = (head * group_size + slot) * head_size
-            own_ref[:, start : start + head_size] = part
-            wire_ref[:, start : start + head_size] = part.astype(BF16)
-
-
-def read(layer, sizes, terms, gate_bias, picks, held, retained):
-    local_heads, group_size, head_size = sizes
+            query = normed[:, start : start + head_size]
+            product = jnp.sum(query * key, axis=1, keepdims=True)
+            cross = product * product / head_size
+            part = decay * history_ref[pl.ds(head * slots + slot, requests, stride=span), :]
+            own_ref[:, start : start + head_size] = part + cross * value
+            wire_ref[:, start : start + head_size] = part.astype(wire_ref.dtype)
+
+
+def read(layer, sizes, wire, terms, gate_bias, picks, held):
+    local_heads, group_size, slots, head_size, _ = sizes
     requests = terms[0].shape[0]
-    block_feat = retained.shape[3]
+    block_feat = picks[0].shape[1]
     width = local_heads * group_size * head_size
     counts = tuple(array.shape[0] for array in held)
-    late = requests - sum(counts)
-    rows = requests * local_heads * SLOTS
+    rows = requests * local_heads * slots
     return pl.pallas_call(
         functools.partial(read_kernel, layer, sizes, len(terms), counts),
         out_shape=[
             jax.ShapeDtypeStruct((requests, width), F32),
-            jax.ShapeDtypeStruct((requests, width), BF16),
+            jax.ShapeDtypeStruct((requests, width), wire),
         ],
-        in_specs=[VMEM_SPEC] * (len(terms) + 4 + len(held)) + [HBM_SPEC],
+        in_specs=[VMEM_SPEC] * (len(terms) + 4 + len(held)),
         out_specs=[VMEM_SPEC] * 2,
         scratch_shapes=[
             pltpu.VMEM((rows, head_size), F32),
-            pltpu.VMEM((2, rows, block_feat), BF16),
-            pltpu.VMEM((rows, LANES), F32),
+            pltpu.VMEM((rows, block_feat), BF16),
             pltpu.VMEM((rows, head_size), F32),
-            pltpu.VMEM((max(late, 1),) + retained.shape[2:], BF16),
-            pltpu.SemaphoreType.DMA((max(late, 1),)),
         ],
-        compiler_params=params(12),
+        compiler_params=params(6),
         name="read",
-    )(*terms, gate_bias, *[resident(pick) for pick in picks], *[resident(part) for part in held], off_chip(retained))
-
-
-def mix_kernel(layer, count, *refs):
+    )(*terms, gate_bias, *[resident(array) for array in (*picks, *held)])
+
+
+def mix_kernel(layer, count, held, *refs):
     terms = refs[:count]
-    gain_ref, weight_ref, wire_ref, mixed_ref = refs[count:]
+    gain_ref, weight_ref = refs[count : count + 2]
+    wire_ref, mixed_ref = refs[count + 2 + held :]
     head_size = gain_ref.shape[1]
     readout = add_terms(terms)
     gain = gain_ref[layer : layer + 1, :]
@@ -364,17 +348,17 @@
     wire_ref[...] = split_dot(mixed_ref[...], weight_ref[layer]).astype(wire_ref.dtype)
 
 
-def mix(layer, terms, read_gain, weight, wire_type):
+def mix(layer, wire, terms, read_gain, weight, held):
     requests, rows = terms[0].shape
     return pl.pallas_call(
-        functools.partial(mix_kernel, layer, len(terms)),
-        out_shape=jax.ShapeDtypeStruct((requests, weight.shape[2]), wire_type),
-        in_specs=[VMEM_SPEC] * (len(terms) + 2),
+        functools.partial(mix_kernel, layer, len(terms), len(held)),
+        out_shape=jax.ShapeDtypeStruct((requests, weight.shape[2]), wire),
+        in_specs=[VMEM_SPEC] * (len(terms) + 2) + [ANY_SPEC] * len(held),
         out_specs=VMEM_SPEC,
         scratch_shapes=[pltpu.VMEM((requests, rows), F32)],
         compiler_params=params(8),
         name="mix",
-    )(*terms, read_gain, resident(weight))
+    )(*terms, read_gain, resident(weight), *[resident(part) for part in held])
 
 
 def finish_kernel(count, *refs):
@@ -410,26 +394,40 @@
 ):
     layer_count, requests, local_heads, block_feat, head_size = retained.shape
     group_size = query_weight.shape[2] // (local_heads * head_size)
-    sizes = (local_heads, group_size, head_size)
+    slots = -(-group_size // SUBLANES) * SUBLANES
+    model_width = norm_gain.shape[1] * feat_size
+    sizes = (local_heads, group_size, slots, head_size, model_width)
+    feat_wire = wire_type(feat_size)
+    head_wire = wire_type(head_ranks)
     weights = (query_weight, key_weight, value_weight)
     gate_rows = gate_weight.transpose(0, 2, 1)
     picks = selectors(head_size, block_feat, feat_size)
 
+    def fetch_state(layer, stage):
+        shares = LATER_LAYER if layer else FIRST_LAYER
+        start = requests * sum(shares[:stage]) // sum(shares)
+        stop = requests * sum(shares[: stage + 1]) // sum(shares)
+        if layer >= layer_count or start == stop:
+            return []
+        return list(fetch([retained], ((0, (layer, slice(start, stop))),)))
+
     picked = pick_rows(token_ids, embedding)
     stream_terms = exchange(picked, picked, "head", head_ranks)
-    stream = None
+    carried, held = [], []
     for layer in range(layer_count):
-        carried = [] if stream is None else [stream]
-        stream, own, wire = project(layer, carried, stream_terms, norm_gain, weights, gate_rows)
+        held = held + fetch_state(layer, 1)
+        stream, own, wire = project(
+            layer, carried, feat_wire, stream_terms, norm_gain, weights, gate_rows, held
+        )
         terms = exchange(own, wire, "feat", feat_size)
-        early = requests * 10 // 16
-        held = fetch([retained], ((0, (layer, slice(0, early))),))
-        own, wire = read(layer, sizes, terms, gate_bias, picks, held, retained)
+        held = held + fetch_state(layer, 2)
+        own, wire = read(layer, sizes, feat_wire, terms, gate_bias, picks, held)
         terms = exchange(own, wire, "feat", feat_size)
-        wire_type = F32 if head_ranks > 4 else BF16
-        wire = mix(layer, terms, read_gain, out_weight, wire_type)
+        held = fetch_state(layer + 1, 0)
+        wire = mix(layer, head_wire, terms, read_gain, out_weight, held)
         stream_terms = exchange(wire, wire, "head", head_ranks)
-    return finish([stream] + stream_terms)
+        carried = [stream]
+    return finish(carried + stream_terms)
 
 
 def solution(mesh):

time: 66 us -> 62 us (0.939)
  waiting for transfers between devices: 15.5 us -> 8.99 us
  Pallas kernels: 25.4 us -> 27.2 us
    ppermute x21, waiting for transfers between devices: 15.5 us -> 8.99 us  [exchange(): lax.ppermute(wire, axis, [(rank, rank ^ step) for rank in range(size)])]
    pallas_call x2 -> x5, Pallas kernels: 8.17 us -> 14.6 us  [fetch(): pl.pallas_call(functools.partial(fetch_kernel, plan, len(sources)), out_s...]
    pallas_call x2, Pallas kernels: 10.5 us -> 6.51 us  [read(): pl.pallas_call(functools.partial(read_kernel, layer, sizes, len(terms), c...]
    pallas_call x1, Pallas kernels: 2.62 us -> 1.93 us  [pick_rows(): pl.pallas_call(pick_kernel, out_shape=jax.ShapeDtypeStruct((requests, wid...]
  transfers between devices with their start and end apart: 21 -> 21, of which waited for: 10 -> 9; matrix products, arithmetic and copies ran while one was open for 0% -> 0% of each run, Pallas kernels for 13% -> 24%
where the time goes in v2:
time: 62 us; the launch traced here: 61.6 us
  Pallas kernels  27.2 us (44%)
  starting transfers between devices  25.1 us (40%)
  waiting for transfers between devices  8.99 us (14%)
    ppermute x21, starting transfers between devices, exchange(): lax.ppermute(wire, axis, [(rank, rank ^ step) for rank in range(size)])  25.1 us
    pallas_call x5, Pallas kernels, fetch(): pl.pallas_call(functools.partial(fetch_kernel, plan, len(sources)), out_s...  14.6 us
    ppermute x21, waiting for transfers between devices, exchange(): lax.ppermute(wire, axis, [(rank, rank ^ step) for rank in range(size)])  8.99 us
    pallas_call x2, Pallas kernels, read(): pl.pallas_call(functools.partial(read_kernel, layer, sizes, len(terms), c...  6.51 us
    pallas_call x1, Pallas kernels, pick_rows(): pl.pallas_call(pick_kernel, out_shape=jax.ShapeDtypeStruct((requests, wid...  1.93 us
    pallas_call x2, Pallas kernels, project(): pl.pallas_call(functools.partial(project_kernel, layer, len(terms), len(c...  1.67 us
    pallas_call x2, Pallas kernels, mix(): pl.pallas_call(functools.partial(mix_kernel, layer, len(terms), len(held)...  1.43 us
  transfers between devices with their start and end apart: 21, of which 9 were waited for; matrix products, arithmetic and copies ran while one was open for 0% of the time, Pallas kernels for 24%

profile of v2, /device:TPU:0, one launch (start us, length us, event | category | flops | bytes accessed | tf_op | source)
XLA Modules:
  0.0 61.6 jit_solution(12466209747840430842)
XLA Ops:
  0.0 1.9 %pick_rows.1.refs_0_ = bf16[16,1280]{1,0:T(8,128)(2,1)S(1)} custom-call(s32[16]{0:T(128)} %ids_ref.1, bf16[18992,1280]{1,0:T(8,128)(2,1)} %table_ref.1), custom_call_target="tpu_custom_call" | custom-call | tf_op jit(solution)/shard_map/pick_rows/pallas_call | solution.py:110
  1.9 0.0 copy-start
  2.0 0.0 copy-start.1
  2.0 0.0 copy-start.2
  2.0 0.0 copy-start.4
  2.0 0.0 copy-start.5
  2.0 2.5 %collective-permute-start = (bf16[16,1280]{1,0:T(8,128)(2,1)S(1)}, bf16[16,1280]{1,0:T(8,128)(2,1)S(1)}, u32[]{:S(2)}, u32[]{:S(2)}) collective-permute-start(bf16[16,1280]{1,0:T(8,128)(2,1)S(1)} %pick_rows.1.refs_0_), channel_id=1, source_target_pairs={{0,3},{1,2},{2,1},{3,0},{4,7},{5,6},{6,5},{7,4},{8,11},{9,10},{10,... | collective-permute-start | bytes 122888 | tf_op jit(solution)/shard_map/ppermute | solution.py:48
  4.5 0.6 %collective-permute-start.1 = (bf16[16,1280]{1,0:T(8,128)(2,1)S(1)}, bf16[16,1280]{1,0:T(8,128)(2,1)S(1)}, u32[]{:S(2)}, u32[]{:S(2)}) collective-permute-start(bf16[16,1280]{1,0:T(8,128)(2,1)S(1)} %pick_rows.1.refs_0_), channel_id=1, source_target_pairs={{0,2},{1,3},{2,0},{3,1},{4,6},{5,7},{6,4},{7,5},{8,10},{9,11},{10,... | collective-permute-start | bytes 122888 | tf_op jit(solution)/shard_map/ppermute | solution.py:48
  5.1 0.0 collective-permute-start.2
  5.2 3.1 %fetch.5.refs_9_.refs_8_ = bf16[7,2,2064,128]{3,2,1,0:T(8,128)(2,1)S(1)} custom-call(bf16[2,16,2,2064,128]{4,3,2,1,0:T(8,128)(2,1)} %refs_0_.9), custom_call_target="tpu_custom_call" | custom-call | tf_op jit(solution)/shard_map/fetch/pallas_call | solution.py:147
  8.3 0.3 collective-permute-done.1.refs_2_
  8.7 0.8 %project.2 = (bf16[16,1280]{1,0:T(8,128)(2,1)S(1)}, f32[16,1920]{1,0:T(8,128)S(1)}, bf16[16,1920]{1,0:T(8,128)(2,1)S(1)}) custom-call(bf16[16,1280]{1,0:T(8,128)(2,1)S(1)} %pick_rows.1.refs_0_, bf16[16,1280]{1,0:T(8,128)(2,1)S(1)} %collective-permute-done.refs_1_, bf16[16,1280]{1,0:T(8,128)(2,1)S(1)} %collective-permute-done.1.refs_2_, ...), custom_call_target="tpu_custom_call" | custom-call | tf_op jit(solution)/shard_map/project/pallas_call | solution.py:222
  9.5 4.2 %collective-permute-start.3 = (bf16[16,1920]{1,0:T(8,128)(2,1)S(1)}, bf16[16,1920]{1,0:T(8,128)(2,1)S(1)}, u32[]{:S(2)}, u32[]{:S(2)}) collective-permute-start(bf16[16,1920]{1,0:T(8,128)(2,1)S(1)} %get-tuple-element.20), channel_id=1, source_target_pairs={{0,12},{4,8},{8,4},{12,0},{1,13},{5,9},{9,5},{13,1},{2,14},{6,10},... | collective-permute-start | bytes 184328 | tf_op jit(solution)/shard_map/ppermute | solution.py:48
  13.8 0.6 %collective-permute-start.5 = (bf16[16,1920]{1,0:T(8,128)(2,1)S(1)}, bf16[16,1920]{1,0:T(8,128)(2,1)S(1)}, u32[]{:S(2)}, u32[]{:S(2)}) collective-permute-start(bf16[16,1920]{1,0:T(8,128)(2,1)S(1)} %get-tuple-element.20), channel_id=1, source_target_pairs={{0,4},{4,0},{8,12},{12,8},{1,5},{5,1},{9,13},{13,9},{2,6},{6,2},{1... | collective-permute-start | bytes 184328 | tf_op jit(solution)/shard_map/ppermute | solution.py:48
  14.4 3.7 %fetch.6.refs_9_ = bf16[9,2,2064,128]{3,2,1,0:T(8,128)(2,1)S(1)} custom-call(bf16[2,16,2,2064,128]{4,3,2,1,0:T(8,128)(2,1)} %refs_0_.9), custom_call_target="tpu_custom_call" | custom-call | tf_op jit(solution)/shard_map/fetch/pallas_call | solution.py:147
  18.1 0.4 selectors.1
  18.5 0.6 collective-permute-done.4.refs_2_
  19.1 3.3 %read.2 = (f32[16,1280]{1,0:T(8,128)S(1)}, bf16[16,1280]{1,0:T(8,128)(2,1)S(1)}) custom-call(f32[16,1920]{1,0:T(8,128)S(1)} %get-tuple-element.19.refs_0_, bf16[16,1920]{1,0:T(8,128)(2,1)S(1)} %collective-permute-done.3.refs_1_, bf16[16,1920]{1,0:T(8,128)(2,1)S(1)} %collective-permute-done.4.refs_2_, bf16[16,1920]{1,0:T(8,128)(2,1)S(1)} %collective-permute-done.5.refs_3_, ...), custom_call_target="tpu_custom_call" | custom-call | tf_op jit(solution)/shard_map/read/pallas_call | solution.py:319
  22.4 0.0 slice-start
  22.4 0.0 copy-start.7
  22.4 3.3 %collective-permute-start.6 = (bf16[16,1280]{1,0:T(8,128)(2,1)S(1)}, bf16[16,1280]{1,0:T(8,128)(2,1)S(1)}, u32[]{:S(2)}, u32[]{:S(2)}) collective-permute-start(bf16[16,1280]{1,0:T(8,128)(2,1)S(1)} %get-tuple-element.25), channel_id=1, source_target_pairs={{0,12},{4,8},{8,4},{12,0},{1,13},{5,9},{9,5},{13,1},{2,14},{6,10},... | collective-permute-start | bytes 122888 | tf_op jit(solution)/shard_map/ppermute | solution.py:48
  25.7 1.2 %collective-permute-start.8 = (bf16[16,1280]{1,0:T(8,128)(2,1)S(1)}, bf16[16,1280]{1,0:T(8,128)(2,1)S(1)}, u32[]{:S(2)}, u32[]{:S(2)}) collective-permute-start(bf16[16,1280]{1,0:T(8,128)(2,1)S(1)} %get-tuple-element.25), channel_id=1, source_target_pairs={{0,4},{4,0},{8,12},{12,8},{1,5},{5,1},{9,13},{13,9},{2,6},{6,2},{1... | collective-permute-start | bytes 122888 | tf_op jit(solution)/shard_map/ppermute | solution.py:48
  26.9 2.5 %fetch.7.refs_6_.refs_10_.refs_8_ = bf16[5,2,2064,128]{3,2,1,0:T(8,128)(2,1)S(1)} custom-call(bf16[2,16,2,2064,128]{4,3,2,1,0:T(8,128)(2,1)} %refs_0_.9), custom_call_target="tpu_custom_call" | custom-call | tf_op jit(solution)/shard_map/fetch/pallas_call | solution.py:147
  29.4 1.2 %collective-permute-done.7.refs_2_ = bf16[16,1280]{1,0:T(8,128)(2,1)S(1)} collective-permute-done((bf16[16,1280]{1,0:T(8,128)(2,1)S(1)}, bf16[16,1280]{1,0:T(8,128)(2,1)S(1)}, u32[]{:S(2)}, u32[]{:S(2)}) %collective-permute-start.7) | collective-permute-done | bytes 40992 | tf_op jit(solution)/shard_map/ppermute | solution.py:48
  30.6 0.7 %mix.2.refs_1_ = bf16[16,1280]{1,0:T(8,128)(2,1)S(1)} custom-call(f32[16,1280]{1,0:T(8,128)S(1)} %get-tuple-element.24.refs_0_, bf16[16,1280]{1,0:T(8,128)(2,1)S(1)} %collective-permute-done.6.refs_1_, bf16[16,1280]{1,0:T(8,128)(2,1)S(1)} %collective-permute-done.7.refs_2_, bf16[16,1280]{1,0:T(8,128)(2,1)S(1)} %collective-permute-done.8.refs_3_, ...), custom_call_target="tpu_custom_call" | custom-call | tf_op jit(solution)/shard_map/mix/pallas_call | solution.py:353
  31.3 0.0 collective-permute-start.9
  31.3 1.6 %collective-permute-start.10 = (bf16[16,1280]{1,0:T(8,128)(2,1)S(1)}, bf16[16,1280]{1,0:T(8,128)(2,1)S(1)}, u32[]{:S(2)}, u32[]{:S(2)}) collective-permute-start(bf16[16,1280]{1,0:T(8,128)(2,1)S(1)} %mix.2.refs_1_), channel_id=1, source_target_pairs={{0,2},{1,3},{2,0},{3,1},{4,6},{5,7},{6,4},{7,5},{8,10},{9,11},{10,... | collective-permute-start | bytes 122888 | tf_op jit(solution)/shard_map/ppermute | solution.py:48
  32.9 0.2 collective-permute-start.11
  33.2 2.2 %fetch.8.refs_11_.refs_9_ = bf16[4,2,2064,128]{3,2,1,0:T(8,128)(2,1)S(1)} custom-call(bf16[2,16,2,2064,128]{4,3,2,1,0:T(8,128)(2,1)} %refs_0_.9), custom_call_target="tpu_custom_call" | custom-call | tf_op jit(solution)/shard_map/fetch/pallas_call | solution.py:147
  35.4 0.3 collective-permute-done.10.refs_3_
  35.7 0.8 %project.3 = (bf16[16,1280]{1,0:T(8,128)(2,1)S(1)}, f32[16,1920]{1,0:T(8,128)S(1)}, bf16[16,1920]{1,0:T(8,128)(2,1)S(1)}) custom-call(bf16[16,1280]{1,0:T(8,128)(2,1)S(1)} %get-tuple-element.18.refs_0_, bf16[16,1280]{1,0:T(8,128)(2,1)S(1)} %mix.2.refs_1_, bf16[16,1280]{1,0:T(8,128)(2,1)S(1)} %collective-permute-done.9.refs_2_, ...), custom_call_target="tpu_custom_call" | custom-call | tf_op jit(solution)/shard_map/project/pallas_call | solution.py:222
  36.5 2.1 %collective-permute-start.12 = (bf16[16,1920]{1,0:T(8,128)(2,1)S(1)}, bf16[16,1920]{1,0:T(8,128)(2,1)S(1)}, u32[]{:S(2)}, u32[]{:S(2)}) collective-permute-start(bf16[16,1920]{1,0:T(8,128)(2,1)S(1)} %get-tuple-element.28), channel_id=1, source_target_pairs={{0,12},{4,8},{8,4},{12,0},{1,13},{5,9},{9,5},{13,1},{2,14},{6,10},... | collective-permute-start | bytes 184328 | tf_op jit(solution)/shard_map/ppermute | solution.py:48
  38.6 0.1 collective-permute-start.13
  38.6 2.3 %collective-permute-start.14 = (bf16[16,1920]{1,0:T(8,128)(2,1)S(1)}, bf16[16,1920]{1,0:T(8,128)(2,1)S(1)}, u32[]{:S(2)}, u32[]{:S(2)}) collective-permute-start(bf16[16,1920]{1,0:T(8,128)(2,1)S(1)} %get-tuple-element.28), channel_id=1, source_target_pairs={{0,4},{4,0},{8,12},{12,8},{1,5},{5,1},{9,13},{13,9},{2,6},{6,2},{1... | collective-permute-start | bytes 184328 | tf_op jit(solution)/shard_map/ppermute | solution.py:48
  40.9 3.1 %fetch.9.refs_10_ = bf16[7,2,2064,128]{3,2,1,0:T(8,128)(2,1)S(1)} custom-call(bf16[2,16,2,2064,128]{4,3,2,1,0:T(8,128)(2,1)} %refs_0_.9), custom_call_target="tpu_custom_call" | custom-call | tf_op jit(solution)/shard_map/fetch/pallas_call | solution.py:147
  44.0 1.1 %collective-permute-done.13.refs_2_ = bf16[16,1920]{1,0:T(8,128)(2,1)S(1)} collective-permute-done((bf16[16,1920]{1,0:T(8,128)(2,1)S(1)}, bf16[16,1920]{1,0:T(8,128)(2,1)S(1)}, u32[]{:S(2)}, u32[]{:S(2)}) %collective-permute-start.13) | collective-permute-done | bytes 61472 | tf_op jit(solution)/shard_map/ppermute | solution.py:48
  45.2 3.3 %read.3 = (f32[16,1280]{1,0:T(8,128)S(1)}, bf16[16,1280]{1,0:T(8,128)(2,1)S(1)}) custom-call(f32[16,1920]{1,0:T(8,128)S(1)} %get-tuple-element.27.refs_0_, bf16[16,1920]{1,0:T(8,128)(2,1)S(1)} %collective-permute-done.12.refs_1_, bf16[16,1920]{1,0:T(8,128)(2,1)S(1)} %collective-permute-done.13.refs_2_, bf16[16,1920]{1,0:T(8,128)(2,1)S(1)} %collective-permute-done.14.refs_3_, ...), custom_call_target="tpu_custom_call" | custom-call | tf_op jit(solution)/shard_map/read/pallas_call | solution.py:319
  48.5 2.5 %collective-permute-start.15 = (bf16[16,1280]{1,0:T(8,128)(2,1)S(1)}, bf16[16,1280]{1,0:T(8,128)(2,1)S(1)}, u32[]{:S(2)}, u32[]{:S(2)}) collective-permute-start(bf16[16,1280]{1,0:T(8,128)(2,1)S(1)} %get-tuple-element.30), channel_id=1, source_target_pairs={{0,12},{4,8},{8,4},{12,0},{1,13},{5,9},{9,5},{13,1},{2,14},{6,10},... | collective-permute-start | bytes 122888 | tf_op jit(solution)/shard_map/ppermute | solution.py:48
  51.0 2.0 %collective-permute-start.17 = (bf16[16,1280]{1,0:T(8,128)(2,1)S(1)}, bf16[16,1280]{1,0:T(8,128)(2,1)S(1)}, u32[]{:S(2)}, u32[]{:S(2)}) collective-permute-start(bf16[16,1280]{1,0:T(8,128)(2,1)S(1)} %get-tuple-element.30), channel_id=1, source_target_pairs={{0,4},{4,0},{8,12},{12,8},{1,5},{5,1},{9,13},{13,9},{2,6},{6,2},{1... | collective-permute-start | bytes 122888 | tf_op jit(solution)/shard_map/ppermute | solution.py:48
  52.9 1.5 %collective-permute-done.15.refs_1_ = bf16[16,1280]{1,0:T(8,128)(2,1)S(1)} collective-permute-done((bf16[16,1280]{1,0:T(8,128)(2,1)S(1)}, bf16[16,1280]{1,0:T(8,128)(2,1)S(1)}, u32[]{:S(2)}, u32[]{:S(2)}) %collective-permute-start.15) | collective-permute-done | bytes 40992 | tf_op jit(solution)/shard_map/ppermute | solution.py:48
  54.4 1.5 %collective-permute-done.16.refs_2_ = bf16[16,1280]{1,0:T(8,128)(2,1)S(1)} collective-permute-done((bf16[16,1280]{1,0:T(8,128)(2,1)S(1)}, bf16[16,1280]{1,0:T(8,128)(2,1)S(1)}, u32[]{:S(2)}, u32[]{:S(2)}) %collective-permute-start.16) | collective-permute-done | bytes 40992 | tf_op jit(solution)/shard_map/ppermute | solution.py:48
  55.9 0.7 %mix.3.refs_1_ = bf16[16,1280]{1,0:T(8,128)(2,1)S(1)} custom-call(f32[16,1280]{1,0:T(8,128)S(1)} %get-tuple-element.29.refs_0_, bf16[16,1280]{1,0:T(8,128)(2,1)S(1)} %collective-permute-done.15.refs_1_, bf16[16,1280]{1,0:T(8,128)(2,1)S(1)} %collective-permute-done.16.refs_2_, bf16[16,1280]{1,0:T(8,128)(2,1)S(1)} %collective-permute-done.17.refs_3_, ...), custom_call_target="tpu_custom_call" | custom-call | tf_op jit(solution)/shard_map/mix/pallas_call | solution.py:353
  56.6 0.1 collective-permute-start.18
  56.6 1.4 %collective-permute-start.19 = (bf16[16,1280]{1,0:T(8,128)(2,1)S(1)}, bf16[16,1280]{1,0:T(8,128)(2,1)S(1)}, u32[]{:S(2)}, u32[]{:S(2)}) collective-permute-start(bf16[16,1280]{1,0:T(8,128)(2,1)S(1)} %mix.3.refs_1_), channel_id=1, source_target_pairs={{0,2},{1,3},{2,0},{3,1},{4,6},{5,7},{6,4},{7,5},{8,10},{9,11},{10,... | collective-permute-start | bytes 122888 | tf_op jit(solution)/shard_map/ppermute | solution.py:48
  58.1 0.4 collective-permute-start.20
  58.5 2.0 %collective-permute-done.18.refs_2_ = bf16[16,1280]{1,0:T(8,128)(2,1)S(1)} collective-permute-done((bf16[16,1280]{1,0:T(8,128)(2,1)S(1)}, bf16[16,1280]{1,0:T(8,128)(2,1)S(1)}, u32[]{:S(2)}, u32[]{:S(2)}) %collective-permute-start.18) | collective-permute-done | bytes 40992 | tf_op jit(solution)/shard_map/ppermute | solution.py:48
  60.5 0.5 collective-permute-done.19.refs_3_
  61.0 0.7 %finish.1 = bf16[16,1280]{1,0:T(8,128)(2,1)} custom-call(bf16[16,1280]{1,0:T(8,128)(2,1)S(1)} %get-tuple-element.26.refs_0_, bf16[16,1280]{1,0:T(8,128)(2,1)S(1)} %mix.3.refs_1_, bf16[16,1280]{1,0:T(8,128)(2,1)S(1)} %collective-permute-done.18.refs_2_, bf16[16,1280]{1,0:T(8,128)(2,1)S(1)} %collective-permute-done.19.refs_3_, ...), custom_call_target="tpu_custom_call" | custom-call | tf_op jit(solution)/shard_map/finish/pallas_call | solution.py:370
  (29 shorter events, 0.1 us)
Async XLA Ops:
  1.9 6.7 %copy-start = (bf16[2,1280,1280]{2,1,0:T(8,128)(2,1)S(1)}, bf16[2,1280,1280]{2,1,0:T(8,128)(2,1)}, u32[]{:S(2)}) copy-start(bf16[2,1280,1280]{2,1,0:T(8,128)(2,1)} %refs_6_.3) | copy-start | bytes 19660804
  2.0 6.7 %copy-start.1 = (bf16[2,1280,256]{2,1,0:T(8,128)(2,1)S(1)}, bf16[2,1280,256]{2,1,0:T(8,128)(2,1)}, u32[]{:S(2)}) copy-start(bf16[2,1280,256]{2,1,0:T(8,128)(2,1)} %refs_7_.3) | copy-start | bytes 3932164
  2.0 6.7 %copy-start.2 = (bf16[2,1280,256]{2,1,0:T(8,128)(2,1)S(1)}, bf16[2,1280,256]{2,1,0:T(8,128)(2,1)}, u32[]{:S(2)}) copy-start(bf16[2,1280,256]{2,1,0:T(8,128)(2,1)} %refs_8_.1) | copy-start | bytes 3932164
  2.0 6.7 %copy-start.4 = (f32[2,1280]{1,0:T(2,128)S(1)}, f32[2,1280]{1,0:T(2,128)}, u32[]{:S(2)}) copy-start(f32[2,1280]{1,0:T(2,128)} %refs_5_.6) | copy-start | bytes 30724
  2.0 6.7 %copy-start.5 = (bf16[2,1280,2]{1,2,0:T(2,128)(2,1)S(1)}, bf16[2,1280,2]{1,2,0:T(2,128)(2,1)}, u32[]{:S(2)}) copy-start(bf16[2,1280,2]{1,2,0:T(2,128)(2,1)} %param.18) | copy-start | bytes 30724
  2.0 6.3 %collective-permute-start = (bf16[16,1280]{1,0:T(8,128)(2,1)S(1)}, bf16[16,1280]{1,0:T(8,128)(2,1)S(1)}, u32[]{:S(2)}, u32[]{:S(2)}) collective-permute-start(bf16[16,1280]{1,0:T(8,128)(2,1)S(1)} %pick_rows.1.refs_0_), channel_id=1, source_target_pairs={{0,3},{1,2},{2,1},{3,0},{4,7},{5,6},{6,5},{7,4},{8,11},{9,10},{10,... | collective-permute-start | bytes 122888 | tf_op jit(solution)/shard_map/ppermute | solution.py:48
  4.5 4.1 %collective-permute-start.1 = (bf16[16,1280]{1,0:T(8,128)(2,1)S(1)}, bf16[16,1280]{1,0:T(8,128)(2,1)S(1)}, u32[]{:S(2)}, u32[]{:S(2)}) collective-permute-start(bf16[16,1280]{1,0:T(8,128)(2,1)S(1)} %pick_rows.1.refs_0_), channel_id=1, source_target_pairs={{0,2},{1,3},{2,0},{3,1},{4,6},{5,7},{6,4},{7,5},{8,10},{9,11},{10,... | collective-permute-start | bytes 122888 | tf_op jit(solution)/shard_map/ppermute | solution.py:48
  5.1 3.5 %collective-permute-start.2 = (bf16[16,1280]{1,0:T(8,128)(2,1)S(1)}, bf16[16,1280]{1,0:T(8,128)(2,1)S(1)}, u32[]{:S(2)}, u32[]{:S(2)}) collective-permute-start(bf16[16,1280]{1,0:T(8,128)(2,1)S(1)} %pick_rows.1.refs_0_), channel_id=1, source_target_pairs={{0,1},{1,0},{2,3},{3,2},{4,5},{5,4},{6,7},{7,6},{8,9},{9,8},{10,11... | collective-permute-start | bytes 122888 | tf_op jit(solution)/shard_map/ppermute | solution.py:48
  9.5 8.6 %copy-start.3 = (s32[4,2,2064]{2,1,0:T(2,128)S(1)}, s32[4,2,2064]{2,1,0:T(2,128)}, u32[]{:S(2)}) copy-start(s32[4,2,2064]{2,1,0:T(2,128)} %constant.2.clone.pairs_ref) | copy-start | bytes 198148
  9.5 9.6 %copy-start.6 = (f32[2,2]{1,0:T(2,128)S(1)}, f32[2,2]{1,0:T(2,128)}, u32[]{:S(2)}) copy-start(f32[2,2]{1,0:T(2,128)} %refs_4_.8) | copy-start | bytes 52
  9.5 9.0 %collective-permute-start.3 = (bf16[16,1920]{1,0:T(8,128)(2,1)S(1)}, bf16[16,1920]{1,0:T(8,128)(2,1)S(1)}, u32[]{:S(2)}, u32[]{:S(2)}) collective-permute-start(bf16[16,1920]{1,0:T(8,128)(2,1)S(1)} %get-tuple-element.20), channel_id=1, source_target_pairs={{0,12},{4,8},{8,4},{12,0},{1,13},{5,9},{9,5},{13,1},{2,14},{6,10},... | collective-permute-start | bytes 184328 | tf_op jit(solution)/shard_map/ppermute | solution.py:48
  13.8 5.3 %collective-permute-start.4 = (bf16[16,1920]{1,0:T(8,128)(2,1)S(1)}, bf16[16,1920]{1,0:T(8,128)(2,1)S(1)}, u32[]{:S(2)}, u32[]{:S(2)}) collective-permute-start(bf16[16,1920]{1,0:T(8,128)(2,1)S(1)} %get-tuple-element.20), channel_id=1, source_target_pairs={{0,8},{4,12},{8,0},{12,4},{1,9},{5,13},{9,1},{13,5},{2,10},{6,14},... | collective-permute-start | bytes 184328 | tf_op jit(solution)/shard_map/ppermute | solution.py:48
  13.8 5.3 %collective-permute-start.5 = (bf16[16,1920]{1,0:T(8,128)(2,1)S(1)}, bf16[16,1920]{1,0:T(8,128)(2,1)S(1)}, u32[]{:S(2)}, u32[]{:S(2)}) collective-permute-start(bf16[16,1920]{1,0:T(8,128)(2,1)S(1)} %get-tuple-element.20), channel_id=1, source_target_pairs={{0,4},{4,0},{8,12},{12,8},{1,5},{5,1},{9,13},{13,9},{2,6},{6,2},{1... | collective-permute-start | bytes 184328 | tf_op jit(solution)/shard_map/ppermute | solution.py:48
  22.4 8.2 %slice-start = ((s8[6553600]{0:T(1024)(128)(4,1)}), s8[4194304]{0:T(1024)(128)(4,1)S(1)}, s32[]{:S(2)}) async-start(s8[6553600]{0:T(1024)(128)(4,1)} %bitcast.1), calls=%async_computation | async-start | bytes 8388608
  22.4 8.2 %slice-start.1 = ((s8[6553600]{0:T(1024)(128)(4,1)}), s8[2359296]{0:T(1024)(128)(4,1)S(1)}, s32[]{:S(2)}) async-start(s8[6553600]{0:T(1024)(128)(4,1)} %bitcast.1), calls=%async_computation.1 | async-start | bytes 4718592
  22.4 8.2 %copy-start.7 = (f32[2,128]{1,0:T(2,128)S(1)}, f32[2,128]{1,0:T(2,128)}, u32[]{:S(2)}) copy-start(f32[2,128]{1,0:T(2,128)} %refs_4_.9) | copy-start | bytes 3076
  22.4 7.0 %collective-permute-start.6 = (bf16[16,1280]{1,0:T(8,128)(2,1)S(1)}, bf16[16,1280]{1,0:T(8,128)(2,1)S(1)}, u32[]{:S(2)}, u32[]{:S(2)}) collective-permute-start(bf16[16,1280]{1,0:T(8,128)(2,1)S(1)} %get-tuple-element.25), channel_id=1, source_target_pairs={{0,12},{4,8},{8,4},{12,0},{1,13},{5,9},{9,5},{13,1},{2,14},{6,10},... | collective-permute-start | bytes 122888 | tf_op jit(solution)/shard_map/ppermute | solution.py:48
  25.7 4.9 %collective-permute-start.7 = (bf16[16,1280]{1,0:T(8,128)(2,1)S(1)}, bf16[16,1280]{1,0:T(8,128)(2,1)S(1)}, u32[]{:S(2)}, u32[]{:S(2)}) collective-permute-start(bf16[16,1280]{1,0:T(8,128)(2,1)S(1)} %get-tuple-element.25), channel_id=1, source_target_pairs={{0,8},{4,12},{8,0},{12,4},{1,9},{5,13},{9,1},{13,5},{2,10},{6,14},... | collective-permute-start | bytes 122888 | tf_op jit(solution)/shard_map/ppermute | solution.py:48
  25.7 4.9 %collective-permute-start.8 = (bf16[16,1280]{1,0:T(8,128)(2,1)S(1)}, bf16[16,1280]{1,0:T(8,128)(2,1)S(1)}, u32[]{:S(2)}, u32[]{:S(2)}) collective-permute-start(bf16[16,1280]{1,0:T(8,128)(2,1)S(1)} %get-tuple-element.25), channel_id=1, source_target_pairs={{0,4},{4,0},{8,12},{12,8},{1,5},{5,1},{9,13},{13,9},{2,6},{6,2},{1... | collective-permute-start | bytes 122888 | tf_op jit(solution)/shard_map/ppermute | solution.py:48
  31.3 4.1 %collective-permute-start.9 = (bf16[16,1280]{1,0:T(8,128)(2,1)S(1)}, bf16[16,1280]{1,0:T(8,128)(2,1)S(1)}, u32[]{:S(2)}, u32[]{:S(2)}) collective-permute-start(bf16[16,1280]{1,0:T(8,128)(2,1)S(1)} %mix.2.refs_1_), channel_id=1, source_target_pairs={{0,3},{1,2},{2,1},{3,0},{4,7},{5,6},{6,5},{7,4},{8,11},{9,10},{10,... | collective-permute-start | bytes 122888 | tf_op jit(solution)/shard_map/ppermute | solution.py:48
  31.3 4.3 %collective-permute-start.10 = (bf16[16,1280]{1,0:T(8,128)(2,1)S(1)}, bf16[16,1280]{1,0:T(8,128)(2,1)S(1)}, u32[]{:S(2)}, u32[]{:S(2)}) collective-permute-start(bf16[16,1280]{1,0:T(8,128)(2,1)S(1)} %mix.2.refs_1_), channel_id=1, source_target_pairs={{0,2},{1,3},{2,0},{3,1},{4,6},{5,7},{6,4},{7,5},{8,10},{9,11},{10,... | collective-permute-start | bytes 122888 | tf_op jit(solution)/shard_map/ppermute | solution.py:48
  32.9 2.7 %collective-permute-start.11 = (bf16[16,1280]{1,0:T(8,128)(2,1)S(1)}, bf16[16,1280]{1,0:T(8,128)(2,1)S(1)}, u32[]{:S(2)}, u32[]{:S(2)}) collective-permute-start(bf16[16,1280]{1,0:T(8,128)(2,1)S(1)} %mix.2.refs_1_), channel_id=1, source_target_pairs={{0,1},{1,0},{2,3},{3,2},{4,5},{5,4},{6,7},{7,6},{8,9},{9,8},{10,11... | collective-permute-start | bytes 122888 | tf_op jit(solution)/shard_map/ppermute | solution.py:48
  36.5 7.5 %collective-permute-start.12 = (bf16[16,1920]{1,0:T(8,128)(2,1)S(1)}, bf16[16,1920]{1,0:T(8,128)(2,1)S(1)}, u32[]{:S(2)}, u32[]{:S(2)}) collective-permute-start(bf16[16,1920]{1,0:T(8,128)(2,1)S(1)} %get-tuple-element.28), channel_id=1, source_target_pairs={{0,12},{4,8},{8,4},{12,0},{1,13},{5,9},{9,5},{13,1},{2,14},{6,10},... | collective-permute-start | bytes 184328 | tf_op jit(solution)/shard_map/ppermute | solution.py:48
  38.6 6.6 %collective-permute-start.13 = (bf16[16,1920]{1,0:T(8,128)(2,1)S(1)}, bf16[16,1920]{1,0:T(8,128)(2,1)S(1)}, u32[]{:S(2)}, u32[]{:S(2)}) collective-permute-start(bf16[16,1920]{1,0:T(8,128)(2,1)S(1)} %get-tuple-element.28), channel_id=1, source_target_pairs={{0,8},{4,12},{8,0},{12,4},{1,9},{5,13},{9,1},{13,5},{2,10},{6,14},... | collective-permute-start | bytes 184328 | tf_op jit(solution)/shard_map/ppermute | solution.py:48
  38.6 6.6 %collective-permute-start.14 = (bf16[16,1920]{1,0:T(8,128)(2,1)S(1)}, bf16[16,1920]{1,0:T(8,128)(2,1)S(1)}, u32[]{:S(2)}, u32[]{:S(2)}) collective-permute-start(bf16[16,1920]{1,0:T(8,128)(2,1)S(1)} %get-tuple-element.28), channel_id=1, source_target_pairs={{0,4},{4,0},{8,12},{12,8},{1,5},{5,1},{9,13},{13,9},{2,6},{6,2},{1... | collective-permute-start | bytes 184328 | tf_op jit(solution)/shard_map/ppermute | solution.py:48
  48.5 5.9 %collective-permute-start.15 = (bf16[16,1280]{1,0:T(8,128)(2,1)S(1)}, bf16[16,1280]{1,0:T(8,128)(2,1)S(1)}, u32[]{:S(2)}, u32[]{:S(2)}) collective-permute-start(bf16[16,1280]{1,0:T(8,128)(2,1)S(1)} %get-tuple-element.30), channel_id=1, source_target_pairs={{0,12},{4,8},{8,4},{12,0},{1,13},{5,9},{9,5},{13,1},{2,14},{6,10},... | collective-permute-start | bytes 122888 | tf_op jit(solution)/shard_map/ppermute | solution.py:48
  51.0 4.9 %collective-permute-start.16 = (bf16[16,1280]{1,0:T(8,128)(2,1)S(1)}, bf16[16,1280]{1,0:T(8,128)(2,1)S(1)}, u32[]{:S(2)}, u32[]{:S(2)}) collective-permute-start(bf16[16,1280]{1,0:T(8,128)(2,1)S(1)} %get-tuple-element.30), channel_id=1, source_target_pairs={{0,8},{4,12},{8,0},{12,4},{1,9},{5,13},{9,1},{13,5},{2,10},{6,14},... | collective-permute-start | bytes 122888 | tf_op jit(solution)/shard_map/ppermute | solution.py:48
  51.0 4.9 %collective-permute-start.17 = (bf16[16,1280]{1,0:T(8,128)(2,1)S(1)}, bf16[16,1280]{1,0:T(8,128)(2,1)S(1)}, u32[]{:S(2)}, u32[]{:S(2)}) collective-permute-start(bf16[16,1280]{1,0:T(8,128)(2,1)S(1)} %get-tuple-element.30), channel_id=1, source_target_pairs={{0,4},{4,0},{8,12},{12,8},{1,5},{5,1},{9,13},{13,9},{2,6},{6,2},{1... | collective-permute-start | bytes 122888 | tf_op jit(solution)/shard_map/ppermute | solution.py:48
  56.6 3.9 %collective-permute-start.18 = (bf16[16,1280]{1,0:T(8,128)(2,1)S(1)}, bf16[16,1280]{1,0:T(8,128)(2,1)S(1)}, u32[]{:S(2)}, u32[]{:S(2)}) collective-permute-start(bf16[16,1280]{1,0:T(8,128)(2,1)S(1)} %mix.3.refs_1_), channel_id=1, source_target_pairs={{0,3},{1,2},{2,1},{3,0},{4,7},{5,6},{6,5},{7,4},{8,11},{9,10},{10,... | collective-permute-start | bytes 122888 | tf_op jit(solution)/shard_map/ppermute | solution.py:48
  56.6 4.4 %collective-permute-start.19 = (bf16[16,1280]{1,0:T(8,128)(2,1)S(1)}, bf16[16,1280]{1,0:T(8,128)(2,1)S(1)}, u32[]{:S(2)}, u32[]{:S(2)}) collective-permute-start(bf16[16,1280]{1,0:T(8,128)(2,1)S(1)} %mix.3.refs_1_), channel_id=1, source_target_pairs={{0,2},{1,3},{2,0},{3,1},{4,6},{5,7},{6,4},{7,5},{8,10},{9,11},{10,... | collective-permute-start | bytes 122888 | tf_op jit(solution)/shard_map/ppermute | solution.py:48
  58.1 2.9 %collective-permute-start.20 = (bf16[16,1280]{1,0:T(8,128)(2,1)S(1)}, bf16[16,1280]{1,0:T(8,128)(2,1)S(1)}, u32[]{:S(2)}, u32[]{:S(2)}) collective-permute-start(bf16[16,1280]{1,0:T(8,128)(2,1)S(1)} %mix.3.refs_1_), channel_id=1, source_target_pairs={{0,1},{1,0},{2,3},{3,2},{4,5},{5,4},{6,7},{7,6},{8,9},{9,8},{10,11... | collective-permute-start | bytes 122888 | tf_op jit(solution)/shard_map/ppermute | solution.py:48

commit v3 on v2

--- a/solution.py
+++ b/solution.py
@@ -3,7 +3,6 @@
 
 import jax
 import jax.numpy as jnp
-import numpy as np
 from jax import lax
 from jax.experimental import pallas as pl
 from jax.experimental.pallas import tpu as pltpu
@@ -13,7 +12,7 @@
 LANES = 128
 SUBLANES = 8
 ROWS = 16
-FIRST_LAYER = (0, 7, 9)
+FIRST_LAYER = (0, 6, 10)
 LATER_LAYER = (5, 4, 7)
 MIB = 2**20
 F32 = jnp.float32
@@ -41,14 +40,28 @@
     return BF16 if size <= 4 else F32
 
 
-def exchange(own, wire, axis, size):
-    if wire_type(size) == F32:
+def steps_of(size):
+    return tuple(reversed(range(1, size))) if size <= 4 else ()
+
+
+def exchange(own, wires, axis, size):
+    steps = steps_of(size)
+    if not steps:
+        (wire,) = wires
         return [own.astype(F32) - wire.astype(F32), lax.psum(wire.astype(F32), axis)]
-    others = [
+    if len(wires) == 1:
+        wires = wires * len(steps)
+    return [own] + [
         lax.ppermute(wire, axis, [(rank, rank ^ step) for rank in range(size)])
-        for step in reversed(range(1, size))
+        for wire, step in zip(wires, steps)
     ]
-    return [own] + others
+
+
+def own_rows(array, share, mine):
+    rows = array[:share]
+    for block in range(1, array.shape[0] // share):
+        rows = jnp.where(mine == block, array[block * share : (block + 1) * share], rows)
+    return rows
 
 
 def split(wide):
@@ -69,7 +82,29 @@
     return terms[0]
 
 
-def pick_kernel(ids_ref, table_ref, out_ref, groups_ref, sems):
+def make_selectors(left_ref, right_ref, scale_ref):
+    depth, block_feat = left_ref.shape
+    size = depth // 2
+
+    def first_of(row):
+        return row * size - row * (row - 1) // 2
+
+    column = lax.broadcasted_iota(jnp.int32, (1, block_feat), 1)
+    feature = lax.axis_index("feat") * block_feat + column
+    reach = 2 * size + 1
+    root = jnp.sqrt((reach * reach - 8 * feature).astype(F32))
+    left = ((reach - root) * 0.5).astype(jnp.int32)
+    left = jnp.where(first_of(left) > feature, left - 1, left)
+    left = jnp.where(first_of(left + 1) <= feature, left + 1, left)
+    right = feature - first_of(left) + left
+    at = lax.broadcasted_iota(jnp.int32, left_ref.shape, 0)
+    at = jnp.where(at >= size, at - size, at)
+    left_ref[...] = jnp.where(at == left, 1.0, 0.0).astype(BF16)
+    right_ref[...] = jnp.where(at == right, 1.0, 0.0).astype(BF16)
+    scale_ref[...] = jnp.where(left == right, 1.0, math.sqrt(2.0)).astype(F32)
+
+
+def pick_kernel(ids_ref, table_ref, out_ref, left_ref, right_ref, scale_ref, groups_ref, sems):
     requests = out_ref.shape[0]
     table_rows = table_ref.shape[0]
     row_start = lax.axis_index("head") * table_rows
@@ -92,6 +127,7 @@
         copies.append((inside, copy))
         place = jnp.where(inside, request * ROWS + row - first, -1)
         chosen = jnp.where((row_at == request) & (column_at == place), 1.0, chosen)
+    make_selectors(left_ref, right_ref, scale_ref)
     for inside, copy in copies:
         pl.when(inside)(copy.wait)
     out_ref[...] = jnp.dot(
@@ -99,19 +135,31 @@
     ).astype(BF16)
 
 
-def pick_rows(token_ids, embedding):
+def pick_rows(token_ids, embedding, head_size, block_feat):
     table_rows, width = embedding.shape
     requests = token_ids.shape[0]
+    picks = [
+        pltpu.VMEM((2 * head_size, block_feat), BF16),
+        pltpu.VMEM((2 * head_size, block_feat), BF16),
+        pltpu.VMEM((1, block_feat), F32),
+    ]
     if table_rows % ROWS:
+        picks = pl.pallas_call(
+            make_selectors,
+            out_shape=picks,
+            out_specs=[VMEM_SPEC] * 3,
+            compiler_params=params(8),
+            name="selectors",
+        )()
         local_ids = token_ids - lax.axis_index("head") * table_rows
         inside = (local_ids >= 0) & (local_ids < table_rows)
         picked = jnp.take(embedding, jnp.clip(local_ids, 0, table_rows - 1), axis=0)
-        return jnp.where(inside[:, None], picked, jnp.zeros_like(picked))
-    return pl.pallas_call(
+        return jnp.where(inside[:, None], picked, jnp.zeros_like(picked)), picks
+    picked, *picks = pl.pallas_call(
         pick_kernel,
-        out_shape=jax.ShapeDtypeStruct((requests, width), BF16),
+        out_shape=[jax.ShapeDtypeStruct((requests, width), BF16)] + picks,
         in_specs=[SMEM_SPEC, HBM_SPEC],
-        out_specs=VMEM_SPEC,
+        out_specs=[VMEM_SPEC] * 4,
         scratch_shapes=[
             pltpu.VMEM((requests * ROWS, width), BF16),
             pltpu.SemaphoreType.DMA((requests,)),
@@ -119,6 +167,7 @@
         compiler_params=params(8),
         name="pick_rows",
     )(off_chip(token_ids), off_chip(embedding))
+    return picked, picks
 
 
 def fetch_kernel(plan, count, *refs):
@@ -155,38 +204,10 @@
     )(*[off_chip(source) for source in sources])
 
 
-def select_kernel(pairs_ref, left_ref, right_ref, scale_ref):
-    mine = lax.axis_index("feat")
-    left = pairs_ref[mine, 0:1, :]
-    right = pairs_ref[mine, 1:2, :]
-    at = lax.broadcasted_iota(jnp.int32, left_ref.shape, 0)
-    at = jnp.where(at >= left_ref.shape[0] // 2, at - left_ref.shape[0] // 2, at)
-    left_ref[...] = jnp.where(at == left, 1.0, 0.0).astype(BF16)
-    right_ref[...] = jnp.where(at == right, 1.0, 0.0).astype(BF16)
-    scale_ref[...] = jnp.where(left == right, 1.0, math.sqrt(2.0)).astype(F32)
-
-
-def selectors(head_size, block_feat, feat_size):
-    pairs = np.stack(np.triu_indices(head_size)).astype(np.int32)
-    pairs = pairs.reshape(2, feat_size, block_feat).transpose(1, 0, 2)
-    return pl.pallas_call(
-        select_kernel,
-        out_shape=[
-            pltpu.VMEM((2 * head_size, block_feat), BF16),
-            pltpu.VMEM((2 * head_size, block_feat), BF16),
-            pltpu.VMEM((1, block_feat), F32),
-        ],
-        in_specs=[VMEM_SPEC],
-        out_specs=[VMEM_SPEC] * 3,
-        compiler_params=params(8),
-        name="selectors",
-    )(jnp.asarray(pairs))
-
-
-def project_kernel(layer, count, carried, held, *refs):
+def project_kernel(layer, count, carried, held, steps, *refs):
     terms = refs[carried:count]
     gain_ref, query_ref, key_ref, value_ref, gate_ref = refs[count : count + 5]
-    stream_ref, own_ref, wire_ref = refs[count + 5 + held :]
+    stream_ref, own_ref, *wire_refs = refs[count + 5 + held :]
     stream = add_terms(terms)
     if carried:
         stream = refs[0][...].astype(F32) + stream
@@ -195,14 +216,11 @@
     wide = stream.astype(F32)
     sum_sq = jnp.sum(wide * wide, axis=1, keepdims=True)
     scaled = wide * gain_ref[layer : layer + 1, :]
-    start = 0
-    for weight_ref in (query_ref, key_ref, value_ref):
-        width = weight_ref.shape[2]
-        part = split_dot(scaled, weight_ref[layer])
-        own_ref[:, start : start + width] = part
-        wire_ref[:, start : start + width] = part.astype(wire_ref.dtype)
-        start += width
-    lane = lax.broadcasted_iota(jnp.int32, (stream.shape[0], LANES), 1)
+    parts = [
+        split_dot(scaled, weight_ref[layer]) for weight_ref in (query_ref, key_ref, value_ref)
+    ]
+    requests = stream.shape[0]
+    lane = lax.broadcasted_iota(jnp.int32, (requests, LANES), 1)
     half = LANES // 2
     place = jnp.where(lane >= half, lane - half, lane)
     extra = jnp.where(place == 0, sum_sq, 0.0)
@@ -210,24 +228,52 @@
         column = gate_ref[layer, head : head + 1, :].astype(F32)
         gate = jnp.sum(scaled * column, axis=1, keepdims=True)
         extra = jnp.where(place == head + 1, gate, extra)
-    own_ref[:, start:] = jnp.where(lane < half, extra, 0.0)
     rounded = extra.astype(BF16).astype(F32)
-    wire_ref[:, start:] = jnp.where(lane < half, rounded, extra - rounded).astype(wire_ref.dtype)
-
-
-def project(layer, carried, wire, terms, norm_gain, weights, gate_weight, held):
+    sent = jnp.where(lane < half, rounded, extra - rounded)
+    kept = jnp.where(lane < half, extra, 0.0)
+    start = 0
+    for part, other in zip((parts[0], kept, *parts[1:]), (parts[0], sent, *parts[1:])):
+        stop = start + part.shape[1]
+        own_ref[:, start:stop] = part
+        for wire_ref in wire_refs:
+            if stop <= wire_ref.shape[1]:
+                wire_ref[:, start:stop] = other.astype(wire_ref.dtype)
+        start = stop
+    for step, wire_ref in zip(steps, wire_refs):
+        share = requests // (len(steps) + 1)
+        partner = lax.axis_index("feat") ^ step
+        packed = [
+            own_rows(part[:, at : at + LANES], share, partner)
+            for part in parts[1:]
+            for at in range(0, part.shape[1], LANES)
+        ]
+        wire_ref[:, -LANES:] = jnp.concatenate(packed, axis=0).astype(wire_ref.dtype)
+
+
+def packs(requests, weights, size):
+    blocks = sum(weight.shape[2] for weight in weights[1:]) // LANES
+    return len(steps_of(size)) > 0 and blocks == size and requests % size == 0
+
+
+def project(layer, carried, size, terms, norm_gain, weights, gate_weight, held):
     terms = carried + terms
     requests, width = terms[0].shape
+    query_width = weights[0].shape[2]
     total = sum(weight.shape[2] for weight in weights) + LANES
-    return pl.pallas_call(
-        functools.partial(project_kernel, layer, len(terms), len(carried), len(held)),
+    if packs(requests, weights, size):
+        steps, sent = steps_of(size), query_width + 2 * LANES
+    else:
+        steps, sent = (), total
+    wires = [jax.ShapeDtypeStruct((requests, sent), wire_type(size))] * max(len(steps), 1)
+    stream, own, *wires = pl.pallas_call(
+        functools.partial(project_kernel, layer, len(terms), len(carried), len(held), steps),
         out_shape=[
             jax.ShapeDtypeStruct((requests, width), BF16),
             jax.ShapeDtypeStruct((requests, total), F32),
-            jax.ShapeDtypeStruct((requests, total), wire),
-        ],
+        ]
+        + wires,
         in_specs=[VMEM_SPEC] * (len(terms) + 5) + [ANY_SPEC] * len(held),
-        out_specs=[VMEM_SPEC] * 3,
+        out_specs=[VMEM_SPEC] * (2 + len(wires)),
         compiler_params=params(8),
         name="project",
     )(
@@ -237,10 +283,11 @@
         gate_weight,
         *[resident(part) for part in held],
     )
+    return stream, own, wires
 
 
 def read_kernel(layer, sizes, count, held, *refs):
-    local_heads, group_size, slots, head_size, model_width = sizes
+    local_heads, group_size, slots, head_size, stream_width, model_width = sizes
     terms = refs[:count]
     bias_ref, left_ref, right_ref, scale_ref = refs[count : count + 4]
     held_refs = refs[count + 4 : count + 4 + len(held)]
@@ -248,21 +295,38 @@
     own_ref, wire_ref, rows_ref, phi_ref, history_ref = rest
     requests = own_ref.shape[0]
     block_feat = phi_ref.shape[1]
-    total = add_terms(terms)
     query_width = local_heads * group_size * head_size
     kv_width = local_heads * head_size
-    extra = total[:, query_width + 2 * kv_width :]
+    own, others = terms[0], terms[1:]
+    common = query_width + LANES
+    total = add_terms([ref.at[:, :common] for ref in terms])
+    extra = total[:, query_width:]
     half = LANES // 2
     extra = extra[:, :half] + extra[:, half:]
     inverse = lax.rsqrt(extra[:, 0:1] / model_width + EPS)
-    normed = total[:, : query_width + 2 * kv_width] * inverse
+    queries = total[:, :query_width] * inverse
+
+    feat_size = model_width // stream_width
+    share = requests // feat_size
+    mine = lax.axis_index("feat")
+    if others[0].shape[1] == own.shape[1]:
+        pairs = add_terms([ref.at[:, common:] for ref in terms])
+        pairs = own_rows(pairs, share, mine)
+    else:
+        packed = add_terms([ref.at[:, common:] for ref in others])
+        pairs = own_rows(own[:, common:], share, mine) + jnp.concatenate(
+            [packed[at : at + share] for at in range(0, requests, share)], axis=1
+        )
+    pairs = jnp.concatenate([pairs] * feat_size, axis=0) * inverse
+    block = lax.broadcasted_iota(jnp.int32, (requests, 1), 0) // share
+    pairs = jnp.where(block == mine, pairs, 0.0)
 
     span = local_heads * slots
     for head in range(local_heads):
         for slot in range(slots):
             if slot < group_size:
                 start = (head * group_size + slot) * head_size
-                part = normed[:, start : start + head_size]
+                part = queries[:, start : start + head_size]
             else:
                 part = jnp.zeros((requests, head_size), F32)
             rows_ref[pl.ds(head * slots + slot, requests, stride=span), :] = part
@@ -296,21 +360,22 @@
         logit = logit + bias_ref[layer : layer + 1, head : head + 1]
         softplus = jnp.maximum(logit, 0.0) + jnp.log(1.0 + jnp.exp(-jnp.abs(logit)))
         decay = jnp.exp(-softplus)
-        start = query_width + head * head_size
-        key = normed[:, start : start + head_size]
-        value = normed[:, start + kv_width : start + kv_width + head_size]
+        start = head * head_size
+        key = pairs[:, start : start + head_size]
+        value = pairs[:, start + kv_width : start + kv_width + head_size]
         for slot in range(group_size):
             start = (head * group_size + slot) * head_size
-            query = normed[:, start : start + head_size]
+            query = queries[:, start : start + head_size]
             product = jnp.sum(query * key, axis=1, keepdims=True)
             cross = product * product / head_size
             part = decay * history_ref[pl.ds(head * slots + slot, requests, stride=span), :]
-            own_ref[:, start : start + head_size] = part + cross * value
+            part = part + cross * value
+            own_ref[:, start : start + head_size] = part
             wire_ref[:, start : start + head_size] = part.astype(wire_ref.dtype)
 
 
 def read(layer, sizes, wire, terms, gate_bias, picks, held):
-    local_heads, group_size, slots, head_size, _ = sizes
+    local_heads, group_size, slots, head_size, _, _ = sizes
     requests = terms[0].shape[0]
     block_feat = picks[0].shape[1]
     width = local_heads * group_size * head_size
@@ -395,13 +460,13 @@
     layer_count, requests, local_heads, block_feat, head_size = retained.shape
     group_size = query_weight.shape[2] // (local_heads * head_size)
     slots = -(-group_size // SUBLANES) * SUBLANES
-    model_width = norm_gain.shape[1] * feat_size
-    sizes = (local_heads, group_size, slots, head_size, model_width)
+    stream_width = norm_gain.shape[1]
+    model_width = stream_width * feat_size
+    sizes = (local_heads, group_size, slots, head_size, stream_width, model_width)
     feat_wire = wire_type(feat_size)
     head_wire = wire_type(head_ranks)
     weights = (query_weight, key_weight, value_weight)
     gate_rows = gate_weight.transpose(0, 2, 1)
-    picks = selectors(head_size, block_feat, feat_size)
 
     def fetch_state(layer, stage):
         shares = LATER_LAYER if layer else FIRST_LAYER
@@ -411,21 +476,21 @@
             return []
         return list(fetch([retained], ((0, (layer, slice(start, stop))),)))
 
-    picked = pick_rows(token_ids, embedding)
-    stream_terms = exchange(picked, picked, "head", head_ranks)
+    picked, picks = pick_rows(token_ids, embedding, head_size, block_feat)
+    stream_terms = exchange(picked, [picked], "head", head_ranks)
     carried, held = [], []
     for layer in range(layer_count):
         held = held + fetch_state(layer, 1)
-        stream, own, wire = project(
-            layer, carried, feat_wire, stream_terms, norm_gain, weights, gate_rows, held
+        stream, own, wires = project(
+            layer, carried, feat_size, stream_terms, norm_gain, weights, gate_rows, held
         )
-        terms = exchange(own, wire, "feat", feat_size)
+        terms = exchange(own, wires, "feat", feat_size)
         held = held + fetch_state(layer, 2)
         own, wire = read(layer, sizes, feat_wire, terms, gate_bias, picks, held)
-        terms = exchange(own, wire, "feat", feat_size)
+        terms = exchange(own, [wire], "feat", feat_size)
         held = fetch_state(layer + 1, 0)
         wire = mix(layer, head_wire, terms, read_gain, out_weight, held)
-        stream_terms = exchange(wire, wire, "head", head_ranks)
+        stream_terms = exchange(wire, [wire], "head", head_ranks)
         carried = [stream]
     return finish(carried + stream_terms)
 

time: 62 us -> 60.8 us (0.981)
    pallas_call x2 -> x1, Pallas kernels: 2.3 us -> 1.98 us  [pick_rows(): pl.pallas_call(pick_kernel, out_shape=[jax.ShapeDtypeStruct((requests, wi...]
where the time goes in v3:
time: 60.8 us; the launch traced here: 60.4 us
  Pallas kernels  26.8 us (44%)
  starting transfers between devices  24.9 us (41%)
  waiting for transfers between devices  8.38 us (14%)
    ppermute x21, starting transfers between devices, exchange(): lax.ppermute(wire, axis, [(rank, rank ^ step) for rank in range(size)])  24.9 us
    pallas_call x5, Pallas kernels, fetch(): pl.pallas_call(functools.partial(fetch_kernel, plan, len(sources)), out_s...  14.6 us
    ppermute x21, waiting for transfers between devices, exchange(): lax.ppermute(wire, axis, [(rank, rank ^ step) for rank in range(size)])  8.38 us
    pallas_call x2, Pallas kernels, read(): pl.pallas_call(functools.partial(read_kernel, layer, sizes, len(terms), c...  6.39 us
    pallas_call x1, Pallas kernels, pick_rows(): pl.pallas_call(pick_kernel, out_shape=[jax.ShapeDtypeStruct((requests, wi...  1.98 us
    pallas_call x2, Pallas kernels, project(): pl.pallas_call(functools.partial(project_kernel, layer, len(terms), len(c...  1.7 us
    pallas_call x2, Pallas kernels, mix(): pl.pallas_call(functools.partial(mix_kernel, layer, len(terms), len(held)...  1.44 us
  transfers between devices with their start and end apart: 21, of which 9 were waited for; matrix products, arithmetic and copies ran while one was open for 0% of the time, Pallas kernels for 24%

profile of v3, /device:TPU:0, one launch (start us, length us, event | category | flops | bytes accessed | tf_op | source)
XLA Modules:
  0.0 60.4 jit_solution(412627025011934975)
XLA Ops:
  0.0 2.0 %pick_rows.1 = (bf16[16,1280]{1,0:T(8,128)(2,1)S(1)}, bf16[256,2064]{1,0:T(8,128)(2,1)S(1)}, bf16[256,2064]{1,0:T(8,128)(2,1)S(1)}, f32[1,2064]{1,0:T(1,128)S(1)}) custom-call(s32[16]{0:T(128)} %ids_ref.1, bf16[18992,1280]{1,0:T(8,128)(2,1)} %table_ref.1), custom_call_target="tpu_custom_call" | custom-call | tf_op jit(solution)/shard_map/pick_rows/pallas_call | solution.py:158
  2.0 0.0 slice-start
  2.0 0.0 copy-start
  2.0 0.0 copy-start.1
  2.0 0.0 copy-start.2
  2.0 0.0 copy-start.3
  2.1 2.4 %collective-permute-start = (bf16[16,1280]{1,0:T(8,128)(2,1)S(1)}, bf16[16,1280]{1,0:T(8,128)(2,1)S(1)}, u32[]{:S(2)}, u32[]{:S(2)}) collective-permute-start(bf16[16,1280]{1,0:T(8,128)(2,1)S(1)} %get-tuple-element.23.refs_0_), channel_id=1, source_target_pairs={{0,3},{1,2},{2,1},{3,0},{4,7},{5,6},{6,5},{7,4},{8,11},{9,10},{10,... | collective-permute-start | bytes 122888 | tf_op jit(solution)/shard_map/ppermute | solution.py:55
  4.5 0.7 %collective-permute-start.1 = (bf16[16,1280]{1,0:T(8,128)(2,1)S(1)}, bf16[16,1280]{1,0:T(8,128)(2,1)S(1)}, u32[]{:S(2)}, u32[]{:S(2)}) collective-permute-start(bf16[16,1280]{1,0:T(8,128)(2,1)S(1)} %get-tuple-element.23.refs_0_), channel_id=1, source_target_pairs={{0,2},{1,3},{2,0},{3,1},{4,6},{5,7},{6,4},{7,5},{8,10},{9,11},{10,... | collective-permute-start | bytes 122888 | tf_op jit(solution)/shard_map/ppermute | solution.py:55
  5.2 0.0 collective-permute-start.2
  5.2 2.8 %fetch.5.refs_9_.refs_8_ = bf16[6,2,2064,128]{3,2,1,0:T(8,128)(2,1)S(1)} custom-call(bf16[2,16,2,2064,128]{4,3,2,1,0:T(8,128)(2,1)} %refs_0_.9), custom_call_target="tpu_custom_call" | custom-call | tf_op jit(solution)/shard_map/fetch/pallas_call | solution.py:196
  8.0 0.6 %collective-permute-done.1.refs_2_ = bf16[16,1280]{1,0:T(8,128)(2,1)S(1)} collective-permute-done((bf16[16,1280]{1,0:T(8,128)(2,1)S(1)}, bf16[16,1280]{1,0:T(8,128)(2,1)S(1)}, u32[]{:S(2)}, u32[]{:S(2)}) %collective-permute-start.1) | collective-permute-done | bytes 40992 | tf_op jit(solution)/shard_map/ppermute | solution.py:55
  8.7 0.9 %project.2 = (bf16[16,1280]{1,0:T(8,128)(2,1)S(1)}, f32[16,1920]{1,0:T(8,128)S(1)}, bf16[16,1536]{1,0:T(8,128)(2,1)S(1)}, bf16[16,1536]{1,0:T(8,128)(2,1)S(1)}, bf16[16,1536]{1,0:T(8,128)(2,1)S(1)}) custom-call(bf16[16,1280]{1,0:T(8,128)(2,1)S(1)} %get-tuple-element.23.refs_0_, bf16[16,1280]{1,0:T(8,128)(2,1)S(1)} %collective-permute-done.refs_1_, ...), custom_call_target="tpu_custom_call" | custom-call | tf_op jit(solution)/shard_map/project/pallas_call | solution.py:268
  9.6 4.0 %collective-permute-start.3 = (bf16[16,1536]{1,0:T(8,128)(2,1)S(1)}, bf16[16,1536]{1,0:T(8,128)(2,1)S(1)}, u32[]{:S(2)}, u32[]{:S(2)}) collective-permute-start(bf16[16,1536]{1,0:T(8,128)(2,1)S(1)} %get-tuple-element.26), channel_id=1, source_target_pairs={{0,12},{4,8},{8,4},{12,0},{1,13},{5,9},{9,5},{13,1},{2,14},{6,10},... | collective-permute-start | bytes 147464 | tf_op jit(solution)/shard_map/ppermute | solution.py:55
  13.6 0.6 %collective-permute-start.5 = (bf16[16,1536]{1,0:T(8,128)(2,1)S(1)}, bf16[16,1536]{1,0:T(8,128)(2,1)S(1)}, u32[]{:S(2)}, u32[]{:S(2)}) collective-permute-start(bf16[16,1536]{1,0:T(8,128)(2,1)S(1)} %get-tuple-element.28), channel_id=1, source_target_pairs={{0,4},{4,0},{8,12},{12,8},{1,5},{5,1},{9,13},{13,9},{2,6},{6,2},{1... | collective-permute-start | bytes 147464 | tf_op jit(solution)/shard_map/ppermute | solution.py:55
  14.2 4.0 %fetch.6.refs_9_ = bf16[10,2,2064,128]{3,2,1,0:T(8,128)(2,1)S(1)} custom-call(bf16[2,16,2,2064,128]{4,3,2,1,0:T(8,128)(2,1)} %refs_0_.9), custom_call_target="tpu_custom_call" | custom-call | tf_op jit(solution)/shard_map/fetch/pallas_call | solution.py:196
  18.3 0.3 collective-permute-done.4.refs_2_
  18.6 3.2 %read.2 = (f32[16,1280]{1,0:T(8,128)S(1)}, bf16[16,1280]{1,0:T(8,128)(2,1)S(1)}) custom-call(f32[16,1920]{1,0:T(8,128)S(1)} %get-tuple-element.25.refs_0_, bf16[16,1536]{1,0:T(8,128)(2,1)S(1)} %collective-permute-done.3.refs_1_, bf16[16,1536]{1,0:T(8,128)(2,1)S(1)} %collective-permute-done.4.refs_2_, bf16[16,1536]{1,0:T(8,128)(2,1)S(1)} %collective-permute-done.5.refs_3_, ...), custom_call_target="tpu_custom_call" | custom-call | tf_op jit(solution)/shard_map/read/pallas_call | solution.py:384
  21.8 0.0 slice-start.2
  21.8 0.0 copy-start.5
  21.8 3.5 %collective-permute-start.6 = (bf16[16,1280]{1,0:T(8,128)(2,1)S(1)}, bf16[16,1280]{1,0:T(8,128)(2,1)S(1)}, u32[]{:S(2)}, u32[]{:S(2)}) collective-permute-start(bf16[16,1280]{1,0:T(8,128)(2,1)S(1)} %get-tuple-element.33), channel_id=1, source_target_pairs={{0,12},{4,8},{8,4},{12,0},{1,13},{5,9},{9,5},{13,1},{2,14},{6,10},... | collective-permute-start | bytes 122888 | tf_op jit(solution)/shard_map/ppermute | solution.py:55
  25.4 0.9 %collective-permute-start.8 = (bf16[16,1280]{1,0:T(8,128)(2,1)S(1)}, bf16[16,1280]{1,0:T(8,128)(2,1)S(1)}, u32[]{:S(2)}, u32[]{:S(2)}) collective-permute-start(bf16[16,1280]{1,0:T(8,128)(2,1)S(1)} %get-tuple-element.33), channel_id=1, source_target_pairs={{0,4},{4,0},{8,12},{12,8},{1,5},{5,1},{9,13},{13,9},{2,6},{6,2},{1... | collective-permute-start | bytes 122888 | tf_op jit(solution)/shard_map/ppermute | solution.py:55
  26.3 2.5 %fetch.7.refs_6_.refs_10_.refs_8_ = bf16[5,2,2064,128]{3,2,1,0:T(8,128)(2,1)S(1)} custom-call(bf16[2,16,2,2064,128]{4,3,2,1,0:T(8,128)(2,1)} %refs_0_.9), custom_call_target="tpu_custom_call" | custom-call | tf_op jit(solution)/shard_map/fetch/pallas_call | solution.py:196
  28.8 1.4 %collective-permute-done.7.refs_2_ = bf16[16,1280]{1,0:T(8,128)(2,1)S(1)} collective-permute-done((bf16[16,1280]{1,0:T(8,128)(2,1)S(1)}, bf16[16,1280]{1,0:T(8,128)(2,1)S(1)}, u32[]{:S(2)}, u32[]{:S(2)}) %collective-permute-start.7) | collective-permute-done | bytes 40992 | tf_op jit(solution)/shard_map/ppermute | solution.py:55
  30.3 0.7 %mix.2.refs_1_ = bf16[16,1280]{1,0:T(8,128)(2,1)S(1)} custom-call(f32[16,1280]{1,0:T(8,128)S(1)} %get-tuple-element.32.refs_0_, bf16[16,1280]{1,0:T(8,128)(2,1)S(1)} %collective-permute-done.6.refs_1_, bf16[16,1280]{1,0:T(8,128)(2,1)S(1)} %collective-permute-done.7.refs_2_, bf16[16,1280]{1,0:T(8,128)(2,1)S(1)} %collective-permute-done.8.refs_3_, ...), custom_call_target="tpu_custom_call" | custom-call | tf_op jit(solution)/shard_map/mix/pallas_call | solution.py:418
  31.0 0.0 collective-permute-start.9
  31.0 1.6 %collective-permute-start.10 = (bf16[16,1280]{1,0:T(8,128)(2,1)S(1)}, bf16[16,1280]{1,0:T(8,128)(2,1)S(1)}, u32[]{:S(2)}, u32[]{:S(2)}) collective-permute-start(bf16[16,1280]{1,0:T(8,128)(2,1)S(1)} %mix.2.refs_1_), channel_id=1, source_target_pairs={{0,2},{1,3},{2,0},{3,1},{4,6},{5,7},{6,4},{7,5},{8,10},{9,11},{10,... | collective-permute-start | bytes 122888 | tf_op jit(solution)/shard_map/ppermute | solution.py:55
  32.6 0.3 collective-permute-start.11
  32.9 2.2 %fetch.8.refs_11_.refs_9_ = bf16[4,2,2064,128]{3,2,1,0:T(8,128)(2,1)S(1)} custom-call(bf16[2,16,2,2064,128]{4,3,2,1,0:T(8,128)(2,1)} %refs_0_.9), custom_call_target="tpu_custom_call" | custom-call | tf_op jit(solution)/shard_map/fetch/pallas_call | solution.py:196
  35.1 0.3 collective-permute-done.10.refs_3_
  35.4 0.8 %project.3 = (bf16[16,1280]{1,0:T(8,128)(2,1)S(1)}, f32[16,1920]{1,0:T(8,128)S(1)}, bf16[16,1536]{1,0:T(8,128)(2,1)S(1)}, bf16[16,1536]{1,0:T(8,128)(2,1)S(1)}, bf16[16,1536]{1,0:T(8,128)(2,1)S(1)}) custom-call(bf16[16,1280]{1,0:T(8,128)(2,1)S(1)} %get-tuple-element.24.refs_0_, bf16[16,1280]{1,0:T(8,128)(2,1)S(1)} %mix.2.refs_1_, ...), custom_call_target="tpu_custom_call" | custom-call | tf_op jit(solution)/shard_map/project/pallas_call | solution.py:268
  36.2 2.1 %collective-permute-start.12 = (bf16[16,1536]{1,0:T(8,128)(2,1)S(1)}, bf16[16,1536]{1,0:T(8,128)(2,1)S(1)}, u32[]{:S(2)}, u32[]{:S(2)}) collective-permute-start(bf16[16,1536]{1,0:T(8,128)(2,1)S(1)} %get-tuple-element.36), channel_id=1, source_target_pairs={{0,12},{4,8},{8,4},{12,0},{1,13},{5,9},{9,5},{13,1},{2,14},{6,10},... | collective-permute-start | bytes 147464 | tf_op jit(solution)/shard_map/ppermute | solution.py:55
  38.4 0.1 collective-permute-start.13
  38.4 2.3 %collective-permute-start.14 = (bf16[16,1536]{1,0:T(8,128)(2,1)S(1)}, bf16[16,1536]{1,0:T(8,128)(2,1)S(1)}, u32[]{:S(2)}, u32[]{:S(2)}) collective-permute-start(bf16[16,1536]{1,0:T(8,128)(2,1)S(1)} %get-tuple-element.38), channel_id=1, source_target_pairs={{0,4},{4,0},{8,12},{12,8},{1,5},{5,1},{9,13},{13,9},{2,6},{6,2},{1... | collective-permute-start | bytes 147464 | tf_op jit(solution)/shard_map/ppermute | solution.py:55
  40.7 3.1 %fetch.9.refs_10_ = bf16[7,2,2064,128]{3,2,1,0:T(8,128)(2,1)S(1)} custom-call(bf16[2,16,2,2064,128]{4,3,2,1,0:T(8,128)(2,1)} %refs_0_.9), custom_call_target="tpu_custom_call" | custom-call | tf_op jit(solution)/shard_map/fetch/pallas_call | solution.py:196
  43.8 0.5 collective-permute-done.13.refs_2_
  44.3 3.2 %read.3 = (f32[16,1280]{1,0:T(8,128)S(1)}, bf16[16,1280]{1,0:T(8,128)(2,1)S(1)}) custom-call(f32[16,1920]{1,0:T(8,128)S(1)} %get-tuple-element.35.refs_0_, bf16[16,1536]{1,0:T(8,128)(2,1)S(1)} %collective-permute-done.12.refs_1_, bf16[16,1536]{1,0:T(8,128)(2,1)S(1)} %collective-permute-done.13.refs_2_, bf16[16,1536]{1,0:T(8,128)(2,1)S(1)} %collective-permute-done.14.refs_3_, ...), custom_call_target="tpu_custom_call" | custom-call | tf_op jit(solution)/shard_map/read/pallas_call | solution.py:384
  47.5 2.2 %collective-permute-start.15 = (bf16[16,1280]{1,0:T(8,128)(2,1)S(1)}, bf16[16,1280]{1,0:T(8,128)(2,1)S(1)}, u32[]{:S(2)}, u32[]{:S(2)}) collective-permute-start(bf16[16,1280]{1,0:T(8,128)(2,1)S(1)} %get-tuple-element.40), channel_id=1, source_target_pairs={{0,12},{4,8},{8,4},{12,0},{1,13},{5,9},{9,5},{13,1},{2,14},{6,10},... | collective-permute-start | bytes 122888 | tf_op jit(solution)/shard_map/ppermute | solution.py:55
  49.8 2.2 %collective-permute-start.17 = (bf16[16,1280]{1,0:T(8,128)(2,1)S(1)}, bf16[16,1280]{1,0:T(8,128)(2,1)S(1)}, u32[]{:S(2)}, u32[]{:S(2)}) collective-permute-start(bf16[16,1280]{1,0:T(8,128)(2,1)S(1)} %get-tuple-element.40), channel_id=1, source_target_pairs={{0,4},{4,0},{8,12},{12,8},{1,5},{5,1},{9,13},{13,9},{2,6},{6,2},{1... | collective-permute-start | bytes 122888 | tf_op jit(solution)/shard_map/ppermute | solution.py:55
  52.0 1.4 %collective-permute-done.15.refs_1_ = bf16[16,1280]{1,0:T(8,128)(2,1)S(1)} collective-permute-done((bf16[16,1280]{1,0:T(8,128)(2,1)S(1)}, bf16[16,1280]{1,0:T(8,128)(2,1)S(1)}, u32[]{:S(2)}, u32[]{:S(2)}) %collective-permute-start.15) | collective-permute-done | bytes 40992 | tf_op jit(solution)/shard_map/ppermute | solution.py:55
  53.4 1.3 %collective-permute-done.16.refs_2_ = bf16[16,1280]{1,0:T(8,128)(2,1)S(1)} collective-permute-done((bf16[16,1280]{1,0:T(8,128)(2,1)S(1)}, bf16[16,1280]{1,0:T(8,128)(2,1)S(1)}, u32[]{:S(2)}, u32[]{:S(2)}) %collective-permute-start.16) | collective-permute-done | bytes 40992 | tf_op jit(solution)/shard_map/ppermute | solution.py:55
  54.7 0.0 collective-permute-done.17.refs_3_
  54.7 0.7 %mix.3.refs_1_ = bf16[16,1280]{1,0:T(8,128)(2,1)S(1)} custom-call(f32[16,1280]{1,0:T(8,128)S(1)} %get-tuple-element.39.refs_0_, bf16[16,1280]{1,0:T(8,128)(2,1)S(1)} %collective-permute-done.15.refs_1_, bf16[16,1280]{1,0:T(8,128)(2,1)S(1)} %collective-permute-done.16.refs_2_, bf16[16,1280]{1,0:T(8,128)(2,1)S(1)} %collective-permute-done.17.refs_3_, ...), custom_call_target="tpu_custom_call" | custom-call | tf_op jit(solution)/shard_map/mix/pallas_call | solution.py:418
  55.4 0.0 collective-permute-start.18
  55.5 1.3 %collective-permute-start.19 = (bf16[16,1280]{1,0:T(8,128)(2,1)S(1)}, bf16[16,1280]{1,0:T(8,128)(2,1)S(1)}, u32[]{:S(2)}, u32[]{:S(2)}) collective-permute-start(bf16[16,1280]{1,0:T(8,128)(2,1)S(1)} %mix.3.refs_1_), channel_id=1, source_target_pairs={{0,2},{1,3},{2,0},{3,1},{4,6},{5,7},{6,4},{7,5},{8,10},{9,11},{10,... | collective-permute-start | bytes 122888 | tf_op jit(solution)/shard_map/ppermute | solution.py:55
  56.8 0.5 collective-permute-start.20
  57.3 1.9 %collective-permute-done.18.refs_2_ = bf16[16,1280]{1,0:T(8,128)(2,1)S(1)} collective-permute-done((bf16[16,1280]{1,0:T(8,128)(2,1)S(1)}, bf16[16,1280]{1,0:T(8,128)(2,1)S(1)}, u32[]{:S(2)}, u32[]{:S(2)}) %collective-permute-start.18) | collective-permute-done | bytes 40992 | tf_op jit(solution)/shard_map/ppermute | solution.py:55
  59.3 0.5 collective-permute-done.19.refs_3_
  59.8 0.7 %finish.1 = bf16[16,1280]{1,0:T(8,128)(2,1)} custom-call(bf16[16,1280]{1,0:T(8,128)(2,1)S(1)} %get-tuple-element.34.refs_0_, bf16[16,1280]{1,0:T(8,128)(2,1)S(1)} %mix.3.refs_1_, bf16[16,1280]{1,0:T(8,128)(2,1)S(1)} %collective-permute-done.18.refs_2_, bf16[16,1280]{1,0:T(8,128)(2,1)S(1)} %collective-permute-done.19.refs_3_, ...), custom_call_target="tpu_custom_call" | custom-call | tf_op jit(solution)/shard_map/finish/pallas_call | solution.py:435
  (29 shorter events, 0.1 us)
Async XLA Ops:
  2.0 6.7 %slice-start = ((s8[6553600]{0:T(1024)(128)(4,1)}), s8[4194304]{0:T(1024)(128)(4,1)S(1)}, s32[]{:S(2)}) async-start(s8[6553600]{0:T(1024)(128)(4,1)} %bitcast.1), calls=%async_computation | async-start | bytes 8388608
  2.0 6.7 %slice-start.1 = ((s8[6553600]{0:T(1024)(128)(4,1)}), s8[2359296]{0:T(1024)(128)(4,1)S(1)}, s32[]{:S(2)}) async-start(s8[6553600]{0:T(1024)(128)(4,1)} %bitcast.1), calls=%async_computation.1 | async-start | bytes 4718592
  2.0 6.7 %copy-start = (bf16[2,1280,256]{2,1,0:T(8,128)(2,1)S(1)}, bf16[2,1280,256]{2,1,0:T(8,128)(2,1)}, u32[]{:S(2)}) copy-start(bf16[2,1280,256]{2,1,0:T(8,128)(2,1)} %refs_7_.3) | copy-start | bytes 3932164
  2.0 6.7 %copy-start.1 = (bf16[2,1280,256]{2,1,0:T(8,128)(2,1)S(1)}, bf16[2,1280,256]{2,1,0:T(8,128)(2,1)}, u32[]{:S(2)}) copy-start(bf16[2,1280,256]{2,1,0:T(8,128)(2,1)} %refs_8_.1) | copy-start | bytes 3932164
  2.0 6.7 %copy-start.2 = (f32[2,1280]{1,0:T(2,128)S(1)}, f32[2,1280]{1,0:T(2,128)}, u32[]{:S(2)}) copy-start(f32[2,1280]{1,0:T(2,128)} %refs_5_.6) | copy-start | bytes 30724
  2.0 6.7 %copy-start.3 = (bf16[2,1280,2]{1,2,0:T(2,128)(2,1)S(1)}, bf16[2,1280,2]{1,2,0:T(2,128)(2,1)}, u32[]{:S(2)}) copy-start(bf16[2,1280,2]{1,2,0:T(2,128)(2,1)} %param.17) | copy-start | bytes 30724
  2.1 6.0 %collective-permute-start = (bf16[16,1280]{1,0:T(8,128)(2,1)S(1)}, bf16[16,1280]{1,0:T(8,128)(2,1)S(1)}, u32[]{:S(2)}, u32[]{:S(2)}) collective-permute-start(bf16[16,1280]{1,0:T(8,128)(2,1)S(1)} %get-tuple-element.23.refs_0_), channel_id=1, source_target_pairs={{0,3},{1,2},{2,1},{3,0},{4,7},{5,6},{6,5},{7,4},{8,11},{9,10},{10,... | collective-permute-start | bytes 122888 | tf_op jit(solution)/shard_map/ppermute | solution.py:55
  4.5 4.2 %collective-permute-start.1 = (bf16[16,1280]{1,0:T(8,128)(2,1)S(1)}, bf16[16,1280]{1,0:T(8,128)(2,1)S(1)}, u32[]{:S(2)}, u32[]{:S(2)}) collective-permute-start(bf16[16,1280]{1,0:T(8,128)(2,1)S(1)} %get-tuple-element.23.refs_0_), channel_id=1, source_target_pairs={{0,2},{1,3},{2,0},{3,1},{4,6},{5,7},{6,4},{7,5},{8,10},{9,11},{10,... | collective-permute-start | bytes 122888 | tf_op jit(solution)/shard_map/ppermute | solution.py:55
  5.2 3.5 %collective-permute-start.2 = (bf16[16,1280]{1,0:T(8,128)(2,1)S(1)}, bf16[16,1280]{1,0:T(8,128)(2,1)S(1)}, u32[]{:S(2)}, u32[]{:S(2)}) collective-permute-start(bf16[16,1280]{1,0:T(8,128)(2,1)S(1)} %get-tuple-element.23.refs_0_), channel_id=1, source_target_pairs={{0,1},{1,0},{2,3},{3,2},{4,5},{5,4},{6,7},{7,6},{8,9},{9,8},{10,11... | collective-permute-start | bytes 122888 | tf_op jit(solution)/shard_map/ppermute | solution.py:55
  9.6 8.7 %collective-permute-start.3 = (bf16[16,1536]{1,0:T(8,128)(2,1)S(1)}, bf16[16,1536]{1,0:T(8,128)(2,1)S(1)}, u32[]{:S(2)}, u32[]{:S(2)}) collective-permute-start(bf16[16,1536]{1,0:T(8,128)(2,1)S(1)} %get-tuple-element.26), channel_id=1, source_target_pairs={{0,12},{4,8},{8,4},{12,0},{1,13},{5,9},{9,5},{13,1},{2,14},{6,10},... | collective-permute-start | bytes 147464 | tf_op jit(solution)/shard_map/ppermute | solution.py:55
  13.6 5.0 %collective-permute-start.4 = (bf16[16,1536]{1,0:T(8,128)(2,1)S(1)}, bf16[16,1536]{1,0:T(8,128)(2,1)S(1)}, u32[]{:S(2)}, u32[]{:S(2)}) collective-permute-start(bf16[16,1536]{1,0:T(8,128)(2,1)S(1)} %get-tuple-element.27), channel_id=1, source_target_pairs={{0,8},{4,12},{8,0},{12,4},{1,9},{5,13},{9,1},{13,5},{2,10},{6,14},... | collective-permute-start | bytes 147464 | tf_op jit(solution)/shard_map/ppermute | solution.py:55
  13.6 5.0 %copy-start.4 = (f32[2,2]{1,0:T(2,128)S(1)}, f32[2,2]{1,0:T(2,128)}, u32[]{:S(2)}) copy-start(f32[2,2]{1,0:T(2,128)} %refs_4_.8) | copy-start | bytes 52
  13.6 5.0 %collective-permute-start.5 = (bf16[16,1536]{1,0:T(8,128)(2,1)S(1)}, bf16[16,1536]{1,0:T(8,128)(2,1)S(1)}, u32[]{:S(2)}, u32[]{:S(2)}) collective-permute-start(bf16[16,1536]{1,0:T(8,128)(2,1)S(1)} %get-tuple-element.28), channel_id=1, source_target_pairs={{0,4},{4,0},{8,12},{12,8},{1,5},{5,1},{9,13},{13,9},{2,6},{6,2},{1... | collective-permute-start | bytes 147464 | tf_op jit(solution)/shard_map/ppermute | solution.py:55
  21.8 8.5 %slice-start.2 = ((s8[6553600]{0:T(1024)(128)(4,1)}), s8[4194304]{0:T(1024)(128)(4,1)S(1)}, s32[]{:S(2)}) async-start(s8[6553600]{0:T(1024)(128)(4,1)} %bitcast.3), calls=%async_computation.2 | async-start | bytes 8388608
  21.8 8.5 %slice-start.3 = ((s8[6553600]{0:T(1024)(128)(4,1)}), s8[2359296]{0:T(1024)(128)(4,1)S(1)}, s32[]{:S(2)}) async-start(s8[6553600]{0:T(1024)(128)(4,1)} %bitcast.3), calls=%async_computation.3 | async-start | bytes 4718592
  21.8 8.5 %copy-start.5 = (f32[2,128]{1,0:T(2,128)S(1)}, f32[2,128]{1,0:T(2,128)}, u32[]{:S(2)}) copy-start(f32[2,128]{1,0:T(2,128)} %refs_4_.9) | copy-start | bytes 3076
  21.8 7.0 %collective-permute-start.6 = (bf16[16,1280]{1,0:T(8,128)(2,1)S(1)}, bf16[16,1280]{1,0:T(8,128)(2,1)S(1)}, u32[]{:S(2)}, u32[]{:S(2)}) collective-permute-start(bf16[16,1280]{1,0:T(8,128)(2,1)S(1)} %get-tuple-element.33), channel_id=1, source_target_pairs={{0,12},{4,8},{8,4},{12,0},{1,13},{5,9},{9,5},{13,1},{2,14},{6,10},... | collective-permute-start | bytes 122888 | tf_op jit(solution)/shard_map/ppermute | solution.py:55
  25.4 4.9 %collective-permute-start.7 = (bf16[16,1280]{1,0:T(8,128)(2,1)S(1)}, bf16[16,1280]{1,0:T(8,128)(2,1)S(1)}, u32[]{:S(2)}, u32[]{:S(2)}) collective-permute-start(bf16[16,1280]{1,0:T(8,128)(2,1)S(1)} %get-tuple-element.33), channel_id=1, source_target_pairs={{0,8},{4,12},{8,0},{12,4},{1,9},{5,13},{9,1},{13,5},{2,10},{6,14},... | collective-permute-start | bytes 122888 | tf_op jit(solution)/shard_map/ppermute | solution.py:55
  25.4 4.9 %collective-permute-start.8 = (bf16[16,1280]{1,0:T(8,128)(2,1)S(1)}, bf16[16,1280]{1,0:T(8,128)(2,1)S(1)}, u32[]{:S(2)}, u32[]{:S(2)}) collective-permute-start(bf16[16,1280]{1,0:T(8,128)(2,1)S(1)} %get-tuple-element.33), channel_id=1, source_target_pairs={{0,4},{4,0},{8,12},{12,8},{1,5},{5,1},{9,13},{13,9},{2,6},{6,2},{1... | collective-permute-start | bytes 122888 | tf_op jit(solution)/shard_map/ppermute | solution.py:55
  31.0 4.1 %collective-permute-start.9 = (bf16[16,1280]{1,0:T(8,128)(2,1)S(1)}, bf16[16,1280]{1,0:T(8,128)(2,1)S(1)}, u32[]{:S(2)}, u32[]{:S(2)}) collective-permute-start(bf16[16,1280]{1,0:T(8,128)(2,1)S(1)} %mix.2.refs_1_), channel_id=1, source_target_pairs={{0,3},{1,2},{2,1},{3,0},{4,7},{5,6},{6,5},{7,4},{8,11},{9,10},{10,... | collective-permute-start | bytes 122888 | tf_op jit(solution)/shard_map/ppermute | solution.py:55
  31.0 4.4 %collective-permute-start.10 = (bf16[16,1280]{1,0:T(8,128)(2,1)S(1)}, bf16[16,1280]{1,0:T(8,128)(2,1)S(1)}, u32[]{:S(2)}, u32[]{:S(2)}) collective-permute-start(bf16[16,1280]{1,0:T(8,128)(2,1)S(1)} %mix.2.refs_1_), channel_id=1, source_target_pairs={{0,2},{1,3},{2,0},{3,1},{4,6},{5,7},{6,4},{7,5},{8,10},{9,11},{10,... | collective-permute-start | bytes 122888 | tf_op jit(solution)/shard_map/ppermute | solution.py:55
  32.6 2.8 %collective-permute-start.11 = (bf16[16,1280]{1,0:T(8,128)(2,1)S(1)}, bf16[16,1280]{1,0:T(8,128)(2,1)S(1)}, u32[]{:S(2)}, u32[]{:S(2)}) collective-permute-start(bf16[16,1280]{1,0:T(8,128)(2,1)S(1)} %mix.2.refs_1_), channel_id=1, source_target_pairs={{0,1},{1,0},{2,3},{3,2},{4,5},{5,4},{6,7},{7,6},{8,9},{9,8},{10,11... | collective-permute-start | bytes 122888 | tf_op jit(solution)/shard_map/ppermute | solution.py:55
  36.2 7.6 %collective-permute-start.12 = (bf16[16,1536]{1,0:T(8,128)(2,1)S(1)}, bf16[16,1536]{1,0:T(8,128)(2,1)S(1)}, u32[]{:S(2)}, u32[]{:S(2)}) collective-permute-start(bf16[16,1536]{1,0:T(8,128)(2,1)S(1)} %get-tuple-element.36), channel_id=1, source_target_pairs={{0,12},{4,8},{8,4},{12,0},{1,13},{5,9},{9,5},{13,1},{2,14},{6,10},... | collective-permute-start | bytes 147464 | tf_op jit(solution)/shard_map/ppermute | solution.py:55
  38.4 6.0 %collective-permute-start.13 = (bf16[16,1536]{1,0:T(8,128)(2,1)S(1)}, bf16[16,1536]{1,0:T(8,128)(2,1)S(1)}, u32[]{:S(2)}, u32[]{:S(2)}) collective-permute-start(bf16[16,1536]{1,0:T(8,128)(2,1)S(1)} %get-tuple-element.37), channel_id=1, source_target_pairs={{0,8},{4,12},{8,0},{12,4},{1,9},{5,13},{9,1},{13,5},{2,10},{6,14},... | collective-permute-start | bytes 147464 | tf_op jit(solution)/shard_map/ppermute | solution.py:55
  38.4 5.9 %collective-permute-start.14 = (bf16[16,1536]{1,0:T(8,128)(2,1)S(1)}, bf16[16,1536]{1,0:T(8,128)(2,1)S(1)}, u32[]{:S(2)}, u32[]{:S(2)}) collective-permute-start(bf16[16,1536]{1,0:T(8,128)(2,1)S(1)} %get-tuple-element.38), channel_id=1, source_target_pairs={{0,4},{4,0},{8,12},{12,8},{1,5},{5,1},{9,13},{13,9},{2,6},{6,2},{1... | collective-permute-start | bytes 147464 | tf_op jit(solution)/shard_map/ppermute | solution.py:55
  47.5 5.9 %collective-permute-start.15 = (bf16[16,1280]{1,0:T(8,128)(2,1)S(1)}, bf16[16,1280]{1,0:T(8,128)(2,1)S(1)}, u32[]{:S(2)}, u32[]{:S(2)}) collective-permute-start(bf16[16,1280]{1,0:T(8,128)(2,1)S(1)} %get-tuple-element.40), channel_id=1, source_target_pairs={{0,12},{4,8},{8,4},{12,0},{1,13},{5,9},{9,5},{13,1},{2,14},{6,10},... | collective-permute-start | bytes 122888 | tf_op jit(solution)/shard_map/ppermute | solution.py:55
  49.7 5.0 %collective-permute-start.16 = (bf16[16,1280]{1,0:T(8,128)(2,1)S(1)}, bf16[16,1280]{1,0:T(8,128)(2,1)S(1)}, u32[]{:S(2)}, u32[]{:S(2)}) collective-permute-start(bf16[16,1280]{1,0:T(8,128)(2,1)S(1)} %get-tuple-element.40), channel_id=1, source_target_pairs={{0,8},{4,12},{8,0},{12,4},{1,9},{5,13},{9,1},{13,5},{2,10},{6,14},... | collective-permute-start | bytes 122888 | tf_op jit(solution)/shard_map/ppermute | solution.py:55
  49.8 5.0 %collective-permute-start.17 = (bf16[16,1280]{1,0:T(8,128)(2,1)S(1)}, bf16[16,1280]{1,0:T(8,128)(2,1)S(1)}, u32[]{:S(2)}, u32[]{:S(2)}) collective-permute-start(bf16[16,1280]{1,0:T(8,128)(2,1)S(1)} %get-tuple-element.40), channel_id=1, source_target_pairs={{0,4},{4,0},{8,12},{12,8},{1,5},{5,1},{9,13},{13,9},{2,6},{6,2},{1... | collective-permute-start | bytes 122888 | tf_op jit(solution)/shard_map/ppermute | solution.py:55
  55.4 3.8 %collective-permute-start.18 = (bf16[16,1280]{1,0:T(8,128)(2,1)S(1)}, bf16[16,1280]{1,0:T(8,128)(2,1)S(1)}, u32[]{:S(2)}, u32[]{:S(2)}) collective-permute-start(bf16[16,1280]{1,0:T(8,128)(2,1)S(1)} %mix.3.refs_1_), channel_id=1, source_target_pairs={{0,3},{1,2},{2,1},{3,0},{4,7},{5,6},{6,5},{7,4},{8,11},{9,10},{10,... | collective-permute-start | bytes 122888 | tf_op jit(solution)/shard_map/ppermute | solution.py:55
  55.5 4.3 %collective-permute-start.19 = (bf16[16,1280]{1,0:T(8,128)(2,1)S(1)}, bf16[16,1280]{1,0:T(8,128)(2,1)S(1)}, u32[]{:S(2)}, u32[]{:S(2)}) collective-permute-start(bf16[16,1280]{1,0:T(8,128)(2,1)S(1)} %mix.3.refs_1_), channel_id=1, source_target_pairs={{0,2},{1,3},{2,0},{3,1},{4,6},{5,7},{6,4},{7,5},{8,10},{9,11},{10,... | collective-permute-start | bytes 122888 | tf_op jit(solution)/shard_map/ppermute | solution.py:55
  56.8 2.9 %collective-permute-start.20 = (bf16[16,1280]{1,0:T(8,128)(2,1)S(1)}, bf16[16,1280]{1,0:T(8,128)(2,1)S(1)}, u32[]{:S(2)}, u32[]{:S(2)}) collective-permute-start(bf16[16,1280]{1,0:T(8,128)(2,1)S(1)} %mix.3.refs_1_), channel_id=1, source_target_pairs={{0,1},{1,0},{2,3},{3,2},{4,5},{5,4},{6,7},{7,6},{8,9},{9,8},{10,11... | collective-permute-start | bytes 122888 | tf_op jit(solution)/shard_map/ppermute | solution.py:55

commit v4 on v3

--- a/solution.py
+++ b/solution.py
@@ -12,8 +12,8 @@
 LANES = 128
 SUBLANES = 8
 ROWS = 16
-FIRST_LAYER = (0, 6, 10)
-LATER_LAYER = (5, 4, 7)
+FIRST_LAYER = (0, 4, 8, 4)
+LATER_LAYER = (5, 4, 7, 0)
 MIB = 2**20
 F32 = jnp.float32
 BF16 = jnp.bfloat16
@@ -40,12 +40,15 @@
     return BF16 if size <= 4 else F32
 
 
-def steps_of(size):
-    return tuple(reversed(range(1, size))) if size <= 4 else ()
+def steps_of(size, axis):
+    if size > 4:
+        return ()
+    order = (2, 3, 1) if axis == "feat" else (3, 2, 1)
+    return tuple(step for step in order if step < size)
 
 
 def exchange(own, wires, axis, size):
-    steps = steps_of(size)
+    steps = steps_of(size, axis)
     if not steps:
         (wire,) = wires
         return [own.astype(F32) - wire.astype(F32), lax.psum(wire.astype(F32), axis)]
@@ -252,7 +255,7 @@
 
 def packs(requests, weights, size):
     blocks = sum(weight.shape[2] for weight in weights[1:]) // LANES
-    return len(steps_of(size)) > 0 and blocks == size and requests % size == 0
+    return len(steps_of(size, "feat")) > 0 and blocks == size and requests % size == 0
 
 
 def project(layer, carried, size, terms, norm_gain, weights, gate_weight, held):
@@ -261,7 +264,7 @@
     query_width = weights[0].shape[2]
     total = sum(weight.shape[2] for weight in weights) + LANES
     if packs(requests, weights, size):
-        steps, sent = steps_of(size), query_width + 2 * LANES
+        steps, sent = steps_of(size, "feat"), query_width + 2 * LANES
     else:
         steps, sent = (), total
     wires = [jax.ShapeDtypeStruct((requests, sent), wire_type(size))] * max(len(steps), 1)
@@ -286,15 +289,22 @@
     return stream, own, wires
 
 
-def read_kernel(layer, sizes, count, held, *refs):
+def read_kernel(layer, sizes, count, held, late, *refs):
     local_heads, group_size, slots, head_size, stream_width, model_width = sizes
     terms = refs[:count]
     bias_ref, left_ref, right_ref, scale_ref = refs[count : count + 4]
     held_refs = refs[count + 4 : count + 4 + len(held)]
     rest = refs[count + 4 + len(held) :]
-    own_ref, wire_ref, rows_ref, phi_ref, history_ref = rest
+    own_ref, wire_ref, rows_ref, phi_ref, history_ref = rest[late:][:5]
     requests = own_ref.shape[0]
     block_feat = phi_ref.shape[1]
+    if late:
+        state_ref, late_ref, sem = rest[0], *rest[-2:]
+        early = sum(held)
+        copy = pltpu.make_async_copy(
+            state_ref.at[layer, early:requests], late_ref.at[: requests - early], sem
+        )
+        copy.start()
     query_width = local_heads * group_size * head_size
     kv_width = local_heads * head_size
     own, others = terms[0], terms[1:]
@@ -354,6 +364,10 @@
         for at in range(many):
             one_request(request, [held_ref[at, head] for head in range(local_heads)])
             request += 1
+    if late:
+        copy.wait()
+        for at in range(requests - early):
+            one_request(early + at, [late_ref[at, head] for head in range(local_heads)])
 
     for head in range(local_heads):
         logit = extra[:, head + 1 : head + 2] * inverse
@@ -374,29 +388,37 @@
             wire_ref[:, start : start + head_size] = part.astype(wire_ref.dtype)
 
 
-def read(layer, sizes, wire, terms, gate_bias, picks, held):
+def read(layer, sizes, wire, terms, gate_bias, picks, held, retained):
     local_heads, group_size, slots, head_size, _, _ = sizes
     requests = terms[0].shape[0]
     block_feat = picks[0].shape[1]
     width = local_heads * group_size * head_size
     counts = tuple(array.shape[0] for array in held)
+    missing = requests - sum(counts)
+    late = int(missing > 0)
     rows = requests * local_heads * slots
     return pl.pallas_call(
-        functools.partial(read_kernel, layer, sizes, len(terms), counts),
+        functools.partial(read_kernel, layer, sizes, len(terms), counts, late),
         out_shape=[
             jax.ShapeDtypeStruct((requests, width), F32),
             jax.ShapeDtypeStruct((requests, width), wire),
         ],
-        in_specs=[VMEM_SPEC] * (len(terms) + 4 + len(held)),
+        in_specs=[VMEM_SPEC] * (len(terms) + 4 + len(held)) + [HBM_SPEC] * late,
         out_specs=[VMEM_SPEC] * 2,
         scratch_shapes=[
             pltpu.VMEM((rows, head_size), F32),
             pltpu.VMEM((rows, block_feat), BF16),
             pltpu.VMEM((rows, head_size), F32),
-        ],
-        compiler_params=params(6),
+        ]
+        + [pltpu.VMEM((missing,) + retained.shape[2:], BF16), pltpu.SemaphoreType.DMA] * late,
+        compiler_params=params(6 + 6 * late),
         name="read",
-    )(*terms, gate_bias, *[resident(array) for array in (*picks, *held)])
+    )(
+        *terms,
+        gate_bias,
+        *[resident(array) for array in (*picks, *held)],
+        *[off_chip(retained)] * late,
+    )
 
 
 def mix_kernel(layer, count, held, *refs):
@@ -486,7 +508,7 @@
         )
         terms = exchange(own, wires, "feat", feat_size)
         held = held + fetch_state(layer, 2)
-        own, wire = read(layer, sizes, feat_wire, terms, gate_bias, picks, held)
+        own, wire = read(layer, sizes, feat_wire, terms, gate_bias, picks, held, retained)
         terms = exchange(own, [wire], "feat", feat_size)
         held = fetch_state(layer + 1, 0)
         wire = mix(layer, head_wire, terms, read_gain, out_weight, held)

time: 60.8 us -> 59.3 us (0.975)
  starting transfers between devices: 24.9 us -> 21.8 us
  waiting for transfers between devices: 8.38 us -> 11.1 us
  Pallas kernels: 26.8 us -> 25.8 us
    ppermute x21, starting transfers between devices: 24.9 us -> 21.8 us  [exchange(): lax.ppermute(wire, axis, [(rank, rank ^ step) for rank in range(size)])]
    ppermute x21, waiting for transfers between devices: 8.38 us -> 11.1 us  [exchange(): lax.ppermute(wire, axis, [(rank, rank ^ step) for rank in range(size)])]
    pallas_call x5, Pallas kernels: 14.6 us -> 13.4 us  [fetch(): pl.pallas_call(functools.partial(fetch_kernel, plan, len(sources)), out_s...]
  transfers between devices with their start and end apart: 21 -> 21, of which waited for: 9 -> 10; matrix products, arithmetic and copies ran while one was open for 0% -> 0% of each run, Pallas kernels for 24% -> 23%
where the time goes in v4:
time: 59.3 us; the launch traced here: 59 us
  Pallas kernels  25.8 us (44%)
  starting transfers between devices  21.8 us (37%)
  waiting for transfers between devices  11.1 us (19%)
    ppermute x21, starting transfers between devices, exchange(): lax.ppermute(wire, axis, [(rank, rank ^ step) for rank in range(size)])  21.8 us
    pallas_call x5, Pallas kernels, fetch(): pl.pallas_call(functools.partial(fetch_kernel, plan, len(sources)), out_s...  13.4 us
    ppermute x21, waiting for transfers between devices, exchange(): lax.ppermute(wire, axis, [(rank, rank ^ step) for rank in range(size)])  11.1 us
    pallas_call x2, Pallas kernels, read(): pl.pallas_call(functools.partial(read_kernel, layer, sizes, len(terms), c...  6.57 us
    pallas_call x1, Pallas kernels, pick_rows(): pl.pallas_call(pick_kernel, out_shape=[jax.ShapeDtypeStruct((requests, wi...  1.97 us
    pallas_call x2, Pallas kernels, project(): pl.pallas_call(functools.partial(project_kernel, layer, len(terms), len(c...  1.71 us
    pallas_call x2, Pallas kernels, mix(): pl.pallas_call(functools.partial(mix_kernel, layer, len(terms), len(held)...  1.44 us
  transfers between devices with their start and end apart: 21, of which 10 were waited for; matrix products, arithmetic and copies ran while one was open for 0% of the time, Pallas kernels for 23%

profile of v4, /device:TPU:0, one launch (start us, length us, event | category | flops | bytes accessed | tf_op | source)
XLA Modules:
  0.0 59.0 jit_solution(4476343880827899450)
XLA Ops:
  0.0 2.0 %pick_rows.1 = (bf16[16,1280]{1,0:T(8,128)(2,1)S(1)}, bf16[256,2064]{1,0:T(8,128)(2,1)S(1)}, bf16[256,2064]{1,0:T(8,128)(2,1)S(1)}, f32[1,2064]{1,0:T(1,128)S(1)}) custom-call(s32[16]{0:T(128)} %ids_ref.1, bf16[18992,1280]{1,0:T(8,128)(2,1)} %table_ref.1), custom_call_target="tpu_custom_call" | custom-call | tf_op jit(solution)/shard_map/pick_rows/pallas_call | solution.py:161
  2.0 0.0 slice-start
  2.0 0.0 copy-start.2
  2.0 0.0 copy-start.3
  2.1 2.4 %collective-permute-start = (bf16[16,1280]{1,0:T(8,128)(2,1)S(1)}, bf16[16,1280]{1,0:T(8,128)(2,1)S(1)}, u32[]{:S(2)}, u32[]{:S(2)}) collective-permute-start(bf16[16,1280]{1,0:T(8,128)(2,1)S(1)} %get-tuple-element.23.refs_0_), channel_id=1, source_target_pairs={{0,3},{1,2},{2,1},{3,0},{4,7},{5,6},{6,5},{7,4},{8,11},{9,10},{10,... | collective-permute-start | bytes 122888 | tf_op jit(solution)/shard_map/ppermute | solution.py:58
  4.5 0.7 %collective-permute-start.1 = (bf16[16,1280]{1,0:T(8,128)(2,1)S(1)}, bf16[16,1280]{1,0:T(8,128)(2,1)S(1)}, u32[]{:S(2)}, u32[]{:S(2)}) collective-permute-start(bf16[16,1280]{1,0:T(8,128)(2,1)S(1)} %get-tuple-element.23.refs_0_), channel_id=1, source_target_pairs={{0,2},{1,3},{2,0},{3,1},{4,6},{5,7},{6,4},{7,5},{8,10},{9,11},{10,... | collective-permute-start | bytes 122888 | tf_op jit(solution)/shard_map/ppermute | solution.py:58
  5.2 0.0 collective-permute-start.2
  5.2 2.2 %fetch.5.refs_9_.refs_8_ = bf16[4,2,2064,128]{3,2,1,0:T(8,128)(2,1)S(1)} custom-call(bf16[2,16,2,2064,128]{4,3,2,1,0:T(8,128)(2,1)} %refs_0_.9), custom_call_target="tpu_custom_call" | custom-call | tf_op jit(solution)/shard_map/fetch/pallas_call | solution.py:199
  7.4 1.2 %collective-permute-done.1.refs_2_ = bf16[16,1280]{1,0:T(8,128)(2,1)S(1)} collective-permute-done((bf16[16,1280]{1,0:T(8,128)(2,1)S(1)}, bf16[16,1280]{1,0:T(8,128)(2,1)S(1)}, u32[]{:S(2)}, u32[]{:S(2)}) %collective-permute-start.1) | collective-permute-done | bytes 40992 | tf_op jit(solution)/shard_map/ppermute | solution.py:58
  8.7 0.9 %project.2 = (bf16[16,1280]{1,0:T(8,128)(2,1)S(1)}, f32[16,1920]{1,0:T(8,128)S(1)}, bf16[16,1536]{1,0:T(8,128)(2,1)S(1)}, bf16[16,1536]{1,0:T(8,128)(2,1)S(1)}, bf16[16,1536]{1,0:T(8,128)(2,1)S(1)}) custom-call(bf16[16,1280]{1,0:T(8,128)(2,1)S(1)} %get-tuple-element.23.refs_0_, bf16[16,1280]{1,0:T(8,128)(2,1)S(1)} %collective-permute-done.refs_1_, ...), custom_call_target="tpu_custom_call" | custom-call | tf_op jit(solution)/shard_map/project/pallas_call | solution.py:271
  9.6 2.7 %collective-permute-start.3 = (bf16[16,1536]{1,0:T(8,128)(2,1)S(1)}, bf16[16,1536]{1,0:T(8,128)(2,1)S(1)}, u32[]{:S(2)}, u32[]{:S(2)}) collective-permute-start(bf16[16,1536]{1,0:T(8,128)(2,1)S(1)} %get-tuple-element.26), channel_id=1, source_target_pairs={{0,8},{4,12},{8,0},{12,4},{1,9},{5,13},{9,1},{13,5},{2,10},{6,14},... | collective-permute-start | bytes 147464 | tf_op jit(solution)/shard_map/ppermute | solution.py:58
  12.3 1.3 %collective-permute-start.4 = (bf16[16,1536]{1,0:T(8,128)(2,1)S(1)}, bf16[16,1536]{1,0:T(8,128)(2,1)S(1)}, u32[]{:S(2)}, u32[]{:S(2)}) collective-permute-start(bf16[16,1536]{1,0:T(8,128)(2,1)S(1)} %get-tuple-element.27), channel_id=1, source_target_pairs={{0,12},{4,8},{8,4},{12,0},{1,13},{5,9},{9,5},{13,1},{2,14},{6,10},... | collective-permute-start | bytes 147464 | tf_op jit(solution)/shard_map/ppermute | solution.py:58
  13.6 0.2 collective-permute-start.5
  13.9 3.4 %fetch.6.refs_9_ = bf16[8,2,2064,128]{3,2,1,0:T(8,128)(2,1)S(1)} custom-call(bf16[2,16,2,2064,128]{4,3,2,1,0:T(8,128)(2,1)} %refs_0_.9), custom_call_target="tpu_custom_call" | custom-call | tf_op jit(solution)/shard_map/fetch/pallas_call | solution.py:199
  17.3 1.0 %collective-permute-done.4.refs_2_ = bf16[16,1536]{1,0:T(8,128)(2,1)S(1)} collective-permute-done((bf16[16,1536]{1,0:T(8,128)(2,1)S(1)}, bf16[16,1536]{1,0:T(8,128)(2,1)S(1)}, u32[]{:S(2)}, u32[]{:S(2)}) %collective-permute-start.4) | collective-permute-done | bytes 49184 | tf_op jit(solution)/shard_map/ppermute | solution.py:58
  18.2 3.4 %read.2 = (f32[16,1280]{1,0:T(8,128)S(1)}, bf16[16,1280]{1,0:T(8,128)(2,1)S(1)}) custom-call(f32[16,1920]{1,0:T(8,128)S(1)} %get-tuple-element.25.refs_0_, bf16[16,1536]{1,0:T(8,128)(2,1)S(1)} %collective-permute-done.3.refs_1_, bf16[16,1536]{1,0:T(8,128)(2,1)S(1)} %collective-permute-done.4.refs_2_, bf16[16,1536]{1,0:T(8,128)(2,1)S(1)} %collective-permute-done.5.refs_3_, ...), custom_call_target="tpu_custom_call" | custom-call | tf_op jit(solution)/shard_map/read/pallas_call | solution.py:400
  21.6 0.0 slice-start.2
  21.6 1.9 %collective-permute-start.6 = (bf16[16,1280]{1,0:T(8,128)(2,1)S(1)}, bf16[16,1280]{1,0:T(8,128)(2,1)S(1)}, u32[]{:S(2)}, u32[]{:S(2)}) collective-permute-start(bf16[16,1280]{1,0:T(8,128)(2,1)S(1)} %get-tuple-element.33), channel_id=1, source_target_pairs={{0,8},{4,12},{8,0},{12,4},{1,9},{5,13},{9,1},{13,5},{2,10},{6,14},... | collective-permute-start | bytes 122888 | tf_op jit(solution)/shard_map/ppermute | solution.py:58
  23.6 1.3 %collective-permute-start.7 = (bf16[16,1280]{1,0:T(8,128)(2,1)S(1)}, bf16[16,1280]{1,0:T(8,128)(2,1)S(1)}, u32[]{:S(2)}, u32[]{:S(2)}) collective-permute-start(bf16[16,1280]{1,0:T(8,128)(2,1)S(1)} %get-tuple-element.33), channel_id=1, source_target_pairs={{0,12},{4,8},{8,4},{12,0},{1,13},{5,9},{9,5},{13,1},{2,14},{6,10},... | collective-permute-start | bytes 122888 | tf_op jit(solution)/shard_map/ppermute | solution.py:58
  24.9 0.3 collective-permute-start.8
  25.2 2.5 %fetch.7.refs_6_.refs_10_.refs_8_ = bf16[5,2,2064,128]{3,2,1,0:T(8,128)(2,1)S(1)} custom-call(bf16[2,16,2,2064,128]{4,3,2,1,0:T(8,128)(2,1)} %refs_0_.9), custom_call_target="tpu_custom_call" | custom-call | tf_op jit(solution)/shard_map/fetch/pallas_call | solution.py:199
  27.7 1.7 %collective-permute-done.7.refs_2_ = bf16[16,1280]{1,0:T(8,128)(2,1)S(1)} collective-permute-done((bf16[16,1280]{1,0:T(8,128)(2,1)S(1)}, bf16[16,1280]{1,0:T(8,128)(2,1)S(1)}, u32[]{:S(2)}, u32[]{:S(2)}) %collective-permute-start.7) | collective-permute-done | bytes 40992 | tf_op jit(solution)/shard_map/ppermute | solution.py:58
  29.4 0.7 %mix.2.refs_1_ = bf16[16,1280]{1,0:T(8,128)(2,1)S(1)} custom-call(f32[16,1280]{1,0:T(8,128)S(1)} %get-tuple-element.32.refs_0_, bf16[16,1280]{1,0:T(8,128)(2,1)S(1)} %collective-permute-done.6.refs_1_, bf16[16,1280]{1,0:T(8,128)(2,1)S(1)} %collective-permute-done.7.refs_2_, bf16[16,1280]{1,0:T(8,128)(2,1)S(1)} %collective-permute-done.8.refs_3_, ...), custom_call_target="tpu_custom_call" | custom-call | tf_op jit(solution)/shard_map/mix/pallas_call | solution.py:440
  30.1 0.0 collective-permute-start.9
  30.2 1.3 %collective-permute-start.10 = (bf16[16,1280]{1,0:T(8,128)(2,1)S(1)}, bf16[16,1280]{1,0:T(8,128)(2,1)S(1)}, u32[]{:S(2)}, u32[]{:S(2)}) collective-permute-start(bf16[16,1280]{1,0:T(8,128)(2,1)S(1)} %mix.2.refs_1_), channel_id=1, source_target_pairs={{0,2},{1,3},{2,0},{3,1},{4,6},{5,7},{6,4},{7,5},{8,10},{9,11},{10,... | collective-permute-start | bytes 122888 | tf_op jit(solution)/shard_map/ppermute | solution.py:58
  31.5 0.5 collective-permute-start.11
  32.0 2.2 %fetch.8.refs_11_.refs_9_ = bf16[4,2,2064,128]{3,2,1,0:T(8,128)(2,1)S(1)} custom-call(bf16[2,16,2,2064,128]{4,3,2,1,0:T(8,128)(2,1)} %refs_0_.9), custom_call_target="tpu_custom_call" | custom-call | tf_op jit(solution)/shard_map/fetch/pallas_call | solution.py:199
  34.2 0.2 collective-permute-done.10.refs_3_
  34.4 0.8 %project.3 = (bf16[16,1280]{1,0:T(8,128)(2,1)S(1)}, f32[16,1920]{1,0:T(8,128)S(1)}, bf16[16,1536]{1,0:T(8,128)(2,1)S(1)}, bf16[16,1536]{1,0:T(8,128)(2,1)S(1)}, bf16[16,1536]{1,0:T(8,128)(2,1)S(1)}) custom-call(bf16[16,1280]{1,0:T(8,128)(2,1)S(1)} %get-tuple-element.24.refs_0_, bf16[16,1280]{1,0:T(8,128)(2,1)S(1)} %mix.2.refs_1_, ...), custom_call_target="tpu_custom_call" | custom-call | tf_op jit(solution)/shard_map/project/pallas_call | solution.py:271
  35.3 1.2 %collective-permute-start.12 = (bf16[16,1536]{1,0:T(8,128)(2,1)S(1)}, bf16[16,1536]{1,0:T(8,128)(2,1)S(1)}, u32[]{:S(2)}, u32[]{:S(2)}) collective-permute-start(bf16[16,1536]{1,0:T(8,128)(2,1)S(1)} %get-tuple-element.36), channel_id=1, source_target_pairs={{0,8},{4,12},{8,0},{12,4},{1,9},{5,13},{9,1},{13,5},{2,10},{6,14},... | collective-permute-start | bytes 147464 | tf_op jit(solution)/shard_map/ppermute | solution.py:58
  36.5 1.4 %collective-permute-start.13 = (bf16[16,1536]{1,0:T(8,128)(2,1)S(1)}, bf16[16,1536]{1,0:T(8,128)(2,1)S(1)}, u32[]{:S(2)}, u32[]{:S(2)}) collective-permute-start(bf16[16,1536]{1,0:T(8,128)(2,1)S(1)} %get-tuple-element.37), channel_id=1, source_target_pairs={{0,12},{4,8},{8,4},{12,0},{1,13},{5,9},{9,5},{13,1},{2,14},{6,10},... | collective-permute-start | bytes 147464 | tf_op jit(solution)/shard_map/ppermute | solution.py:58
  37.8 1.0 %collective-permute-start.14 = (bf16[16,1536]{1,0:T(8,128)(2,1)S(1)}, bf16[16,1536]{1,0:T(8,128)(2,1)S(1)}, u32[]{:S(2)}, u32[]{:S(2)}) collective-permute-start(bf16[16,1536]{1,0:T(8,128)(2,1)S(1)} %get-tuple-element.38), channel_id=1, source_target_pairs={{0,4},{4,0},{8,12},{12,8},{1,5},{5,1},{9,13},{13,9},{2,6},{6,2},{1... | collective-permute-start | bytes 147464 | tf_op jit(solution)/shard_map/ppermute | solution.py:58
  38.8 3.1 %fetch.9.refs_10_ = bf16[7,2,2064,128]{3,2,1,0:T(8,128)(2,1)S(1)} custom-call(bf16[2,16,2,2064,128]{4,3,2,1,0:T(8,128)(2,1)} %refs_0_.9), custom_call_target="tpu_custom_call" | custom-call | tf_op jit(solution)/shard_map/fetch/pallas_call | solution.py:199
  41.9 0.6 collective-permute-done.13.refs_2_
  42.5 0.2 collective-permute-done.14.refs_3_
  42.7 3.2 %read.3 = (f32[16,1280]{1,0:T(8,128)S(1)}, bf16[16,1280]{1,0:T(8,128)(2,1)S(1)}) custom-call(f32[16,1920]{1,0:T(8,128)S(1)} %get-tuple-element.35.refs_0_, bf16[16,1536]{1,0:T(8,128)(2,1)S(1)} %collective-permute-done.12.refs_1_, bf16[16,1536]{1,0:T(8,128)(2,1)S(1)} %collective-permute-done.13.refs_2_, bf16[16,1536]{1,0:T(8,128)(2,1)S(1)} %collective-permute-done.14.refs_3_, ...), custom_call_target="tpu_custom_call" | custom-call | tf_op jit(solution)/shard_map/read/pallas_call | solution.py:400
  45.9 1.6 %collective-permute-start.15 = (bf16[16,1280]{1,0:T(8,128)(2,1)S(1)}, bf16[16,1280]{1,0:T(8,128)(2,1)S(1)}, u32[]{:S(2)}, u32[]{:S(2)}) collective-permute-start(bf16[16,1280]{1,0:T(8,128)(2,1)S(1)} %get-tuple-element.40), channel_id=1, source_target_pairs={{0,8},{4,12},{8,0},{12,4},{1,9},{5,13},{9,1},{13,5},{2,10},{6,14},... | collective-permute-start | bytes 122888 | tf_op jit(solution)/shard_map/ppermute | solution.py:58
  47.6 1.4 %collective-permute-start.16 = (bf16[16,1280]{1,0:T(8,128)(2,1)S(1)}, bf16[16,1280]{1,0:T(8,128)(2,1)S(1)}, u32[]{:S(2)}, u32[]{:S(2)}) collective-permute-start(bf16[16,1280]{1,0:T(8,128)(2,1)S(1)} %get-tuple-element.40), channel_id=1, source_target_pairs={{0,12},{4,8},{8,4},{12,0},{1,13},{5,9},{9,5},{13,1},{2,14},{6,10},... | collective-permute-start | bytes 122888 | tf_op jit(solution)/shard_map/ppermute | solution.py:58
  48.9 0.6 collective-permute-start.17
  49.5 2.7 %collective-permute-done.15.refs_1_ = bf16[16,1280]{1,0:T(8,128)(2,1)S(1)} collective-permute-done((bf16[16,1280]{1,0:T(8,128)(2,1)S(1)}, bf16[16,1280]{1,0:T(8,128)(2,1)S(1)}, u32[]{:S(2)}, u32[]{:S(2)}) %collective-permute-start.15) | collective-permute-done | bytes 40992 | tf_op jit(solution)/shard_map/ppermute | solution.py:58
  52.2 1.2 %collective-permute-done.16.refs_2_ = bf16[16,1280]{1,0:T(8,128)(2,1)S(1)} collective-permute-done((bf16[16,1280]{1,0:T(8,128)(2,1)S(1)}, bf16[16,1280]{1,0:T(8,128)(2,1)S(1)}, u32[]{:S(2)}, u32[]{:S(2)}) %collective-permute-start.16) | collective-permute-done | bytes 40992 | tf_op jit(solution)/shard_map/ppermute | solution.py:58
  53.4 0.7 %mix.3.refs_1_ = bf16[16,1280]{1,0:T(8,128)(2,1)S(1)} custom-call(f32[16,1280]{1,0:T(8,128)S(1)} %get-tuple-element.39.refs_0_, bf16[16,1280]{1,0:T(8,128)(2,1)S(1)} %collective-permute-done.15.refs_1_, bf16[16,1280]{1,0:T(8,128)(2,1)S(1)} %collective-permute-done.16.refs_2_, bf16[16,1280]{1,0:T(8,128)(2,1)S(1)} %collective-permute-done.17.refs_3_, ...), custom_call_target="tpu_custom_call" | custom-call | tf_op jit(solution)/shard_map/mix/pallas_call | solution.py:440
  54.1 0.0 collective-permute-start.18
  54.1 1.3 %collective-permute-start.19 = (bf16[16,1280]{1,0:T(8,128)(2,1)S(1)}, bf16[16,1280]{1,0:T(8,128)(2,1)S(1)}, u32[]{:S(2)}, u32[]{:S(2)}) collective-permute-start(bf16[16,1280]{1,0:T(8,128)(2,1)S(1)} %mix.3.refs_1_), channel_id=1, source_target_pairs={{0,2},{1,3},{2,0},{3,1},{4,6},{5,7},{6,4},{7,5},{8,10},{9,11},{10,... | collective-permute-start | bytes 122888 | tf_op jit(solution)/shard_map/ppermute | solution.py:58
  55.4 0.6 collective-permute-start.20
  56.0 1.8 %collective-permute-done.18.refs_2_ = bf16[16,1280]{1,0:T(8,128)(2,1)S(1)} collective-permute-done((bf16[16,1280]{1,0:T(8,128)(2,1)S(1)}, bf16[16,1280]{1,0:T(8,128)(2,1)S(1)}, u32[]{:S(2)}, u32[]{:S(2)}) %collective-permute-start.18) | collective-permute-done | bytes 40992 | tf_op jit(solution)/shard_map/ppermute | solution.py:58
  57.7 0.6 %collective-permute-done.19.refs_3_ = bf16[16,1280]{1,0:T(8,128)(2,1)S(1)} collective-permute-done((bf16[16,1280]{1,0:T(8,128)(2,1)S(1)}, bf16[16,1280]{1,0:T(8,128)(2,1)S(1)}, u32[]{:S(2)}, u32[]{:S(2)}) %collective-permute-start.19) | collective-permute-done | bytes 40992 | tf_op jit(solution)/shard_map/ppermute | solution.py:58
  58.4 0.7 %finish.1 = bf16[16,1280]{1,0:T(8,128)(2,1)} custom-call(bf16[16,1280]{1,0:T(8,128)(2,1)S(1)} %get-tuple-element.34.refs_0_, bf16[16,1280]{1,0:T(8,128)(2,1)S(1)} %mix.3.refs_1_, bf16[16,1280]{1,0:T(8,128)(2,1)S(1)} %collective-permute-done.18.refs_2_, bf16[16,1280]{1,0:T(8,128)(2,1)S(1)} %collective-permute-done.19.refs_3_, ...), custom_call_target="tpu_custom_call" | custom-call | tf_op jit(solution)/shard_map/finish/pallas_call | solution.py:457
  (29 shorter events, 0.1 us)
Async XLA Ops:
  2.0 6.7 %slice-start = ((s8[6553600]{0:T(1024)(128)(4,1)}), s8[4194304]{0:T(1024)(128)(4,1)S(1)}, s32[]{:S(2)}) async-start(s8[6553600]{0:T(1024)(128)(4,1)} %bitcast.1), calls=%async_computation | async-start | bytes 8388608
  2.0 6.7 %slice-start.1 = ((s8[6553600]{0:T(1024)(128)(4,1)}), s8[2359296]{0:T(1024)(128)(4,1)S(1)}, s32[]{:S(2)}) async-start(s8[6553600]{0:T(1024)(128)(4,1)} %bitcast.1), calls=%async_computation.1 | async-start | bytes 4718592
  2.0 6.7 %copy-start = (bf16[2,1280,256]{2,1,0:T(8,128)(2,1)S(1)}, bf16[2,1280,256]{2,1,0:T(8,128)(2,1)}, u32[]{:S(2)}) copy-start(bf16[2,1280,256]{2,1,0:T(8,128)(2,1)} %refs_7_.3) | copy-start | bytes 3932164
  2.0 6.7 %copy-start.1 = (bf16[2,1280,256]{2,1,0:T(8,128)(2,1)S(1)}, bf16[2,1280,256]{2,1,0:T(8,128)(2,1)}, u32[]{:S(2)}) copy-start(bf16[2,1280,256]{2,1,0:T(8,128)(2,1)} %refs_8_.1) | copy-start | bytes 3932164
  2.0 6.7 %copy-start.2 = (f32[2,1280]{1,0:T(2,128)S(1)}, f32[2,1280]{1,0:T(2,128)}, u32[]{:S(2)}) copy-start(f32[2,1280]{1,0:T(2,128)} %refs_5_.6) | copy-start | bytes 30724
  2.0 6.7 %copy-start.3 = (bf16[2,1280,2]{1,2,0:T(2,128)(2,1)S(1)}, bf16[2,1280,2]{1,2,0:T(2,128)(2,1)}, u32[]{:S(2)}) copy-start(bf16[2,1280,2]{1,2,0:T(2,128)(2,1)} %param.17) | copy-start | bytes 30724
  2.1 5.4 %collective-permute-start = (bf16[16,1280]{1,0:T(8,128)(2,1)S(1)}, bf16[16,1280]{1,0:T(8,128)(2,1)S(1)}, u32[]{:S(2)}, u32[]{:S(2)}) collective-permute-start(bf16[16,1280]{1,0:T(8,128)(2,1)S(1)} %get-tuple-element.23.refs_0_), channel_id=1, source_target_pairs={{0,3},{1,2},{2,1},{3,0},{4,7},{5,6},{6,5},{7,4},{8,11},{9,10},{10,... | collective-permute-start | bytes 122888 | tf_op jit(solution)/shard_map/ppermute | solution.py:58
  4.5 4.2 %collective-permute-start.1 = (bf16[16,1280]{1,0:T(8,128)(2,1)S(1)}, bf16[16,1280]{1,0:T(8,128)(2,1)S(1)}, u32[]{:S(2)}, u32[]{:S(2)}) collective-permute-start(bf16[16,1280]{1,0:T(8,128)(2,1)S(1)} %get-tuple-element.23.refs_0_), channel_id=1, source_target_pairs={{0,2},{1,3},{2,0},{3,1},{4,6},{5,7},{6,4},{7,5},{8,10},{9,11},{10,... | collective-permute-start | bytes 122888 | tf_op jit(solution)/shard_map/ppermute | solution.py:58
  5.2 3.5 %collective-permute-start.2 = (bf16[16,1280]{1,0:T(8,128)(2,1)S(1)}, bf16[16,1280]{1,0:T(8,128)(2,1)S(1)}, u32[]{:S(2)}, u32[]{:S(2)}) collective-permute-start(bf16[16,1280]{1,0:T(8,128)(2,1)S(1)} %get-tuple-element.23.refs_0_), channel_id=1, source_target_pairs={{0,1},{1,0},{2,3},{3,2},{4,5},{5,4},{6,7},{7,6},{8,9},{9,8},{10,11... | collective-permute-start | bytes 122888 | tf_op jit(solution)/shard_map/ppermute | solution.py:58
  9.6 7.7 %collective-permute-start.3 = (bf16[16,1536]{1,0:T(8,128)(2,1)S(1)}, bf16[16,1536]{1,0:T(8,128)(2,1)S(1)}, u32[]{:S(2)}, u32[]{:S(2)}) collective-permute-start(bf16[16,1536]{1,0:T(8,128)(2,1)S(1)} %get-tuple-element.26), channel_id=1, source_target_pairs={{0,8},{4,12},{8,0},{12,4},{1,9},{5,13},{9,1},{13,5},{2,10},{6,14},... | collective-permute-start | bytes 147464 | tf_op jit(solution)/shard_map/ppermute | solution.py:58
  12.3 6.0 %collective-permute-start.4 = (bf16[16,1536]{1,0:T(8,128)(2,1)S(1)}, bf16[16,1536]{1,0:T(8,128)(2,1)S(1)}, u32[]{:S(2)}, u32[]{:S(2)}) collective-permute-start(bf16[16,1536]{1,0:T(8,128)(2,1)S(1)} %get-tuple-element.27), channel_id=1, source_target_pairs={{0,12},{4,8},{8,4},{12,0},{1,13},{5,9},{9,5},{13,1},{2,14},{6,10},... | collective-permute-start | bytes 147464 | tf_op jit(solution)/shard_map/ppermute | solution.py:58
  13.6 4.6 %copy-start.4 = (f32[2,2]{1,0:T(2,128)S(1)}, f32[2,2]{1,0:T(2,128)}, u32[]{:S(2)}) copy-start(f32[2,2]{1,0:T(2,128)} %refs_4_.8) | copy-start | bytes 52
  13.6 4.6 %collective-permute-start.5 = (bf16[16,1536]{1,0:T(8,128)(2,1)S(1)}, bf16[16,1536]{1,0:T(8,128)(2,1)S(1)}, u32[]{:S(2)}, u32[]{:S(2)}) collective-permute-start(bf16[16,1536]{1,0:T(8,128)(2,1)S(1)} %get-tuple-element.28), channel_id=1, source_target_pairs={{0,4},{4,0},{8,12},{12,8},{1,5},{5,1},{9,13},{13,9},{2,6},{6,2},{1... | collective-permute-start | bytes 147464 | tf_op jit(solution)/shard_map/ppermute | solution.py:58
  21.6 7.8 %slice-start.2 = ((s8[6553600]{0:T(1024)(128)(4,1)}), s8[4194304]{0:T(1024)(128)(4,1)S(1)}, s32[]{:S(2)}) async-start(s8[6553600]{0:T(1024)(128)(4,1)} %bitcast.3), calls=%async_computation.2 | async-start | bytes 8388608
  21.6 7.8 %slice-start.3 = ((s8[6553600]{0:T(1024)(128)(4,1)}), s8[2359296]{0:T(1024)(128)(4,1)S(1)}, s32[]{:S(2)}) async-start(s8[6553600]{0:T(1024)(128)(4,1)} %bitcast.3), calls=%async_computation.3 | async-start | bytes 4718592
  21.6 7.8 %copy-start.5 = (f32[2,128]{1,0:T(2,128)S(1)}, f32[2,128]{1,0:T(2,128)}, u32[]{:S(2)}) copy-start(f32[2,128]{1,0:T(2,128)} %refs_4_.9) | copy-start | bytes 3076
  21.6 6.1 %collective-permute-start.6 = (bf16[16,1280]{1,0:T(8,128)(2,1)S(1)}, bf16[16,1280]{1,0:T(8,128)(2,1)S(1)}, u32[]{:S(2)}, u32[]{:S(2)}) collective-permute-start(bf16[16,1280]{1,0:T(8,128)(2,1)S(1)} %get-tuple-element.33), channel_id=1, source_target_pairs={{0,8},{4,12},{8,0},{12,4},{1,9},{5,13},{9,1},{13,5},{2,10},{6,14},... | collective-permute-start | bytes 122888 | tf_op jit(solution)/shard_map/ppermute | solution.py:58
  23.6 5.8 %collective-permute-start.7 = (bf16[16,1280]{1,0:T(8,128)(2,1)S(1)}, bf16[16,1280]{1,0:T(8,128)(2,1)S(1)}, u32[]{:S(2)}, u32[]{:S(2)}) collective-permute-start(bf16[16,1280]{1,0:T(8,128)(2,1)S(1)} %get-tuple-element.33), channel_id=1, source_target_pairs={{0,12},{4,8},{8,4},{12,0},{1,13},{5,9},{9,5},{13,1},{2,14},{6,10},... | collective-permute-start | bytes 122888 | tf_op jit(solution)/shard_map/ppermute | solution.py:58
  24.9 4.5 %collective-permute-start.8 = (bf16[16,1280]{1,0:T(8,128)(2,1)S(1)}, bf16[16,1280]{1,0:T(8,128)(2,1)S(1)}, u32[]{:S(2)}, u32[]{:S(2)}) collective-permute-start(bf16[16,1280]{1,0:T(8,128)(2,1)S(1)} %get-tuple-element.33), channel_id=1, source_target_pairs={{0,4},{4,0},{8,12},{12,8},{1,5},{5,1},{9,13},{13,9},{2,6},{6,2},{1... | collective-permute-start | bytes 122888 | tf_op jit(solution)/shard_map/ppermute | solution.py:58
  30.1 4.1 %collective-permute-start.9 = (bf16[16,1280]{1,0:T(8,128)(2,1)S(1)}, bf16[16,1280]{1,0:T(8,128)(2,1)S(1)}, u32[]{:S(2)}, u32[]{:S(2)}) collective-permute-start(bf16[16,1280]{1,0:T(8,128)(2,1)S(1)} %mix.2.refs_1_), channel_id=1, source_target_pairs={{0,3},{1,2},{2,1},{3,0},{4,7},{5,6},{6,5},{7,4},{8,11},{9,10},{10,... | collective-permute-start | bytes 122888 | tf_op jit(solution)/shard_map/ppermute | solution.py:58
  30.2 4.2 %collective-permute-start.10 = (bf16[16,1280]{1,0:T(8,128)(2,1)S(1)}, bf16[16,1280]{1,0:T(8,128)(2,1)S(1)}, u32[]{:S(2)}, u32[]{:S(2)}) collective-permute-start(bf16[16,1280]{1,0:T(8,128)(2,1)S(1)} %mix.2.refs_1_), channel_id=1, source_target_pairs={{0,2},{1,3},{2,0},{3,1},{4,6},{5,7},{6,4},{7,5},{8,10},{9,11},{10,... | collective-permute-start | bytes 122888 | tf_op jit(solution)/shard_map/ppermute | solution.py:58
  31.5 2.9 %collective-permute-start.11 = (bf16[16,1280]{1,0:T(8,128)(2,1)S(1)}, bf16[16,1280]{1,0:T(8,128)(2,1)S(1)}, u32[]{:S(2)}, u32[]{:S(2)}) collective-permute-start(bf16[16,1280]{1,0:T(8,128)(2,1)S(1)} %mix.2.refs_1_), channel_id=1, source_target_pairs={{0,1},{1,0},{2,3},{3,2},{4,5},{5,4},{6,7},{7,6},{8,9},{9,8},{10,11... | collective-permute-start | bytes 122888 | tf_op jit(solution)/shard_map/ppermute | solution.py:58
  35.3 6.7 %collective-permute-start.12 = (bf16[16,1536]{1,0:T(8,128)(2,1)S(1)}, bf16[16,1536]{1,0:T(8,128)(2,1)S(1)}, u32[]{:S(2)}, u32[]{:S(2)}) collective-permute-start(bf16[16,1536]{1,0:T(8,128)(2,1)S(1)} %get-tuple-element.36), channel_id=1, source_target_pairs={{0,8},{4,12},{8,0},{12,4},{1,9},{5,13},{9,1},{13,5},{2,10},{6,14},... | collective-permute-start | bytes 147464 | tf_op jit(solution)/shard_map/ppermute | solution.py:58
  36.5 6.0 %collective-permute-start.13 = (bf16[16,1536]{1,0:T(8,128)(2,1)S(1)}, bf16[16,1536]{1,0:T(8,128)(2,1)S(1)}, u32[]{:S(2)}, u32[]{:S(2)}) collective-permute-start(bf16[16,1536]{1,0:T(8,128)(2,1)S(1)} %get-tuple-element.37), channel_id=1, source_target_pairs={{0,12},{4,8},{8,4},{12,0},{1,13},{5,9},{9,5},{13,1},{2,14},{6,10},... | collective-permute-start | bytes 147464 | tf_op jit(solution)/shard_map/ppermute | solution.py:58
  37.8 4.9 %collective-permute-start.14 = (bf16[16,1536]{1,0:T(8,128)(2,1)S(1)}, bf16[16,1536]{1,0:T(8,128)(2,1)S(1)}, u32[]{:S(2)}, u32[]{:S(2)}) collective-permute-start(bf16[16,1536]{1,0:T(8,128)(2,1)S(1)} %get-tuple-element.38), channel_id=1, source_target_pairs={{0,4},{4,0},{8,12},{12,8},{1,5},{5,1},{9,13},{13,9},{2,6},{6,2},{1... | collective-permute-start | bytes 147464 | tf_op jit(solution)/shard_map/ppermute | solution.py:58
  45.9 6.2 %collective-permute-start.15 = (bf16[16,1280]{1,0:T(8,128)(2,1)S(1)}, bf16[16,1280]{1,0:T(8,128)(2,1)S(1)}, u32[]{:S(2)}, u32[]{:S(2)}) collective-permute-start(bf16[16,1280]{1,0:T(8,128)(2,1)S(1)} %get-tuple-element.40), channel_id=1, source_target_pairs={{0,8},{4,12},{8,0},{12,4},{1,9},{5,13},{9,1},{13,5},{2,10},{6,14},... | collective-permute-start | bytes 122888 | tf_op jit(solution)/shard_map/ppermute | solution.py:58
  47.6 5.8 %collective-permute-start.16 = (bf16[16,1280]{1,0:T(8,128)(2,1)S(1)}, bf16[16,1280]{1,0:T(8,128)(2,1)S(1)}, u32[]{:S(2)}, u32[]{:S(2)}) collective-permute-start(bf16[16,1280]{1,0:T(8,128)(2,1)S(1)} %get-tuple-element.40), channel_id=1, source_target_pairs={{0,12},{4,8},{8,4},{12,0},{1,13},{5,9},{9,5},{13,1},{2,14},{6,10},... | collective-permute-start | bytes 122888 | tf_op jit(solution)/shard_map/ppermute | solution.py:58
  48.9 4.4 %collective-permute-start.17 = (bf16[16,1280]{1,0:T(8,128)(2,1)S(1)}, bf16[16,1280]{1,0:T(8,128)(2,1)S(1)}, u32[]{:S(2)}, u32[]{:S(2)}) collective-permute-start(bf16[16,1280]{1,0:T(8,128)(2,1)S(1)} %get-tuple-element.40), channel_id=1, source_target_pairs={{0,4},{4,0},{8,12},{12,8},{1,5},{5,1},{9,13},{13,9},{2,6},{6,2},{1... | collective-permute-start | bytes 122888 | tf_op jit(solution)/shard_map/ppermute | solution.py:58
  54.1 3.6 %collective-permute-start.18 = (bf16[16,1280]{1,0:T(8,128)(2,1)S(1)}, bf16[16,1280]{1,0:T(8,128)(2,1)S(1)}, u32[]{:S(2)}, u32[]{:S(2)}) collective-permute-start(bf16[16,1280]{1,0:T(8,128)(2,1)S(1)} %mix.3.refs_1_), channel_id=1, source_target_pairs={{0,3},{1,2},{2,1},{3,0},{4,7},{5,6},{6,5},{7,4},{8,11},{9,10},{10,... | collective-permute-start | bytes 122888 | tf_op jit(solution)/shard_map/ppermute | solution.py:58
  54.1 4.2 %collective-permute-start.19 = (bf16[16,1280]{1,0:T(8,128)(2,1)S(1)}, bf16[16,1280]{1,0:T(8,128)(2,1)S(1)}, u32[]{:S(2)}, u32[]{:S(2)}) collective-permute-start(bf16[16,1280]{1,0:T(8,128)(2,1)S(1)} %mix.3.refs_1_), channel_id=1, source_target_pairs={{0,2},{1,3},{2,0},{3,1},{4,6},{5,7},{6,4},{7,5},{8,10},{9,11},{10,... | collective-permute-start | bytes 122888 | tf_op jit(solution)/shard_map/ppermute | solution.py:58
  55.4 3.0 %collective-permute-start.20 = (bf16[16,1280]{1,0:T(8,128)(2,1)S(1)}, bf16[16,1280]{1,0:T(8,128)(2,1)S(1)}, u32[]{:S(2)}, u32[]{:S(2)}) collective-permute-start(bf16[16,1280]{1,0:T(8,128)(2,1)S(1)} %mix.3.refs_1_), channel_id=1, source_target_pairs={{0,1},{1,0},{2,3},{3,2},{4,5},{5,4},{6,7},{7,6},{8,9},{9,8},{10,11... | collective-permute-start | bytes 122888 | tf_op jit(solution)/shard_map/ppermute | solution.py:58

commit v5 on v4

--- a/solution.py
+++ b/solution.py
@@ -12,7 +12,7 @@
 LANES = 128
 SUBLANES = 8
 ROWS = 16
-FIRST_LAYER = (0, 4, 8, 4)
+FIRST_LAYER = (0, 3, 9, 4)
 LATER_LAYER = (5, 4, 7, 0)
 MIB = 2**20
 F32 = jnp.float32

time: 59.3 us -> 59.9 us (1.010)
  no operation moved by 1% of the time
where the time goes in v5:
time: 59.9 us; the launch traced here: 59.3 us
  Pallas kernels  25.7 us (43%)
  starting transfers between devices  21.8 us (36%)
  waiting for transfers between devices  11.4 us (19%)
    ppermute x21, starting transfers between devices, exchange(): lax.ppermute(wire, axis, [(rank, rank ^ step) for rank in range(size)])  21.8 us
    pallas_call x5, Pallas kernels, fetch(): pl.pallas_call(functools.partial(fetch_kernel, plan, len(sources)), out_s...  13.4 us
    ppermute x21, waiting for transfers between devices, exchange(): lax.ppermute(wire, axis, [(rank, rank ^ step) for rank in range(size)])  11.4 us
    pallas_call x2, Pallas kernels, read(): pl.pallas_call(functools.partial(read_kernel, layer, sizes, len(terms), c...  6.55 us
    pallas_call x1, Pallas kernels, pick_rows(): pl.pallas_call(pick_kernel, out_shape=[jax.ShapeDtypeStruct((requests, wi...  1.93 us
    pallas_call x2, Pallas kernels, project(): pl.pallas_call(functools.partial(project_kernel, layer, len(terms), len(c...  1.7 us
    pallas_call x2, Pallas kernels, mix(): pl.pallas_call(functools.partial(mix_kernel, layer, len(terms), len(held)...  1.44 us
  transfers between devices with their start and end apart: 21, of which 10 were waited for; matrix products, arithmetic and copies ran while one was open for 0% of the time, Pallas kernels for 23%

profile of v5, /device:TPU:0, one launch (start us, length us, event | category | flops | bytes accessed | tf_op | source)
XLA Modules:
  0.0 59.3 jit_solution(8405132193469315148)
XLA Ops:
  0.0 1.9 %pick_rows.1 = (bf16[16,1280]{1,0:T(8,128)(2,1)S(1)}, bf16[256,2064]{1,0:T(8,128)(2,1)S(1)}, bf16[256,2064]{1,0:T(8,128)(2,1)S(1)}, f32[1,2064]{1,0:T(1,128)S(1)}) custom-call(s32[16]{0:T(128)} %ids_ref.1, bf16[18992,1280]{1,0:T(8,128)(2,1)} %table_ref.1), custom_call_target="tpu_custom_call" | custom-call | tf_op jit(solution)/shard_map/pick_rows/pallas_call | solution.py:161
  1.9 0.0 slice-start
  2.0 0.0 copy-start
  2.0 0.0 copy-start.2
  2.0 0.0 copy-start.3
  2.0 2.5 %collective-permute-start = (bf16[16,1280]{1,0:T(8,128)(2,1)S(1)}, bf16[16,1280]{1,0:T(8,128)(2,1)S(1)}, u32[]{:S(2)}, u32[]{:S(2)}) collective-permute-start(bf16[16,1280]{1,0:T(8,128)(2,1)S(1)} %get-tuple-element.23.refs_0_), channel_id=1, source_target_pairs={{0,3},{1,2},{2,1},{3,0},{4,7},{5,6},{6,5},{7,4},{8,11},{9,10},{10,... | collective-permute-start | bytes 122888 | tf_op jit(solution)/shard_map/ppermute | solution.py:58
  4.5 0.6 collective-permute-start.1
  5.1 0.0 collective-permute-start.2
  5.2 1.9 %fetch.5.refs_9_.refs_8_ = bf16[3,2,2064,128]{3,2,1,0:T(8,128)(2,1)S(1)} custom-call(bf16[2,16,2,2064,128]{4,3,2,1,0:T(8,128)(2,1)} %refs_0_.9), custom_call_target="tpu_custom_call" | custom-call | tf_op jit(solution)/shard_map/fetch/pallas_call | solution.py:199
  7.1 1.5 %collective-permute-done.1.refs_2_ = bf16[16,1280]{1,0:T(8,128)(2,1)S(1)} collective-permute-done((bf16[16,1280]{1,0:T(8,128)(2,1)S(1)}, bf16[16,1280]{1,0:T(8,128)(2,1)S(1)}, u32[]{:S(2)}, u32[]{:S(2)}) %collective-permute-start.1) | collective-permute-done | bytes 40992 | tf_op jit(solution)/shard_map/ppermute | solution.py:58
  8.7 0.9 %project.2 = (bf16[16,1280]{1,0:T(8,128)(2,1)S(1)}, f32[16,1920]{1,0:T(8,128)S(1)}, bf16[16,1536]{1,0:T(8,128)(2,1)S(1)}, bf16[16,1536]{1,0:T(8,128)(2,1)S(1)}, bf16[16,1536]{1,0:T(8,128)(2,1)S(1)}) custom-call(bf16[16,1280]{1,0:T(8,128)(2,1)S(1)} %get-tuple-element.23.refs_0_, bf16[16,1280]{1,0:T(8,128)(2,1)S(1)} %collective-permute-done.refs_1_, ...), custom_call_target="tpu_custom_call" | custom-call | tf_op jit(solution)/shard_map/project/pallas_call | solution.py:271
  9.6 2.7 %collective-permute-start.3 = (bf16[16,1536]{1,0:T(8,128)(2,1)S(1)}, bf16[16,1536]{1,0:T(8,128)(2,1)S(1)}, u32[]{:S(2)}, u32[]{:S(2)}) collective-permute-start(bf16[16,1536]{1,0:T(8,128)(2,1)S(1)} %get-tuple-element.26), channel_id=1, source_target_pairs={{0,8},{4,12},{8,0},{12,4},{1,9},{5,13},{9,1},{13,5},{2,10},{6,14},... | collective-permute-start | bytes 147464 | tf_op jit(solution)/shard_map/ppermute | solution.py:58
  12.2 1.3 %collective-permute-start.4 = (bf16[16,1536]{1,0:T(8,128)(2,1)S(1)}, bf16[16,1536]{1,0:T(8,128)(2,1)S(1)}, u32[]{:S(2)}, u32[]{:S(2)}) collective-permute-start(bf16[16,1536]{1,0:T(8,128)(2,1)S(1)} %get-tuple-element.27), channel_id=1, source_target_pairs={{0,12},{4,8},{8,4},{12,0},{1,13},{5,9},{9,5},{13,1},{2,14},{6,10},... | collective-permute-start | bytes 147464 | tf_op jit(solution)/shard_map/ppermute | solution.py:58
  13.6 0.2 collective-permute-start.5
  13.8 3.7 %fetch.6.refs_9_ = bf16[9,2,2064,128]{3,2,1,0:T(8,128)(2,1)S(1)} custom-call(bf16[2,16,2,2064,128]{4,3,2,1,0:T(8,128)(2,1)} %refs_0_.9), custom_call_target="tpu_custom_call" | custom-call | tf_op jit(solution)/shard_map/fetch/pallas_call | solution.py:199
  17.5 0.7 %collective-permute-done.4.refs_2_ = bf16[16,1536]{1,0:T(8,128)(2,1)S(1)} collective-permute-done((bf16[16,1536]{1,0:T(8,128)(2,1)S(1)}, bf16[16,1536]{1,0:T(8,128)(2,1)S(1)}, u32[]{:S(2)}, u32[]{:S(2)}) %collective-permute-start.4) | collective-permute-done | bytes 49184 | tf_op jit(solution)/shard_map/ppermute | solution.py:58
  18.2 3.3 %read.2 = (f32[16,1280]{1,0:T(8,128)S(1)}, bf16[16,1280]{1,0:T(8,128)(2,1)S(1)}) custom-call(f32[16,1920]{1,0:T(8,128)S(1)} %get-tuple-element.25.refs_0_, bf16[16,1536]{1,0:T(8,128)(2,1)S(1)} %collective-permute-done.3.refs_1_, bf16[16,1536]{1,0:T(8,128)(2,1)S(1)} %collective-permute-done.4.refs_2_, bf16[16,1536]{1,0:T(8,128)(2,1)S(1)} %collective-permute-done.5.refs_3_, ...), custom_call_target="tpu_custom_call" | custom-call | tf_op jit(solution)/shard_map/read/pallas_call | solution.py:400
  21.5 0.0 slice-start.2
  21.6 2.2 %collective-permute-start.6 = (bf16[16,1280]{1,0:T(8,128)(2,1)S(1)}, bf16[16,1280]{1,0:T(8,128)(2,1)S(1)}, u32[]{:S(2)}, u32[]{:S(2)}) collective-permute-start(bf16[16,1280]{1,0:T(8,128)(2,1)S(1)} %get-tuple-element.33), channel_id=1, source_target_pairs={{0,8},{4,12},{8,0},{12,4},{1,9},{5,13},{9,1},{13,5},{2,10},{6,14},... | collective-permute-start | bytes 122888 | tf_op jit(solution)/shard_map/ppermute | solution.py:58
  23.8 1.3 %collective-permute-start.7 = (bf16[16,1280]{1,0:T(8,128)(2,1)S(1)}, bf16[16,1280]{1,0:T(8,128)(2,1)S(1)}, u32[]{:S(2)}, u32[]{:S(2)}) collective-permute-start(bf16[16,1280]{1,0:T(8,128)(2,1)S(1)} %get-tuple-element.33), channel_id=1, source_target_pairs={{0,12},{4,8},{8,4},{12,0},{1,13},{5,9},{9,5},{13,1},{2,14},{6,10},... | collective-permute-start | bytes 122888 | tf_op jit(solution)/shard_map/ppermute | solution.py:58
  25.2 2.5 %fetch.7.refs_6_.refs_10_.refs_8_ = bf16[5,2,2064,128]{3,2,1,0:T(8,128)(2,1)S(1)} custom-call(bf16[2,16,2,2064,128]{4,3,2,1,0:T(8,128)(2,1)} %refs_0_.9), custom_call_target="tpu_custom_call" | custom-call | tf_op jit(solution)/shard_map/fetch/pallas_call | solution.py:199
  27.7 1.9 %collective-permute-done.7.refs_2_ = bf16[16,1280]{1,0:T(8,128)(2,1)S(1)} collective-permute-done((bf16[16,1280]{1,0:T(8,128)(2,1)S(1)}, bf16[16,1280]{1,0:T(8,128)(2,1)S(1)}, u32[]{:S(2)}, u32[]{:S(2)}) %collective-permute-start.7) | collective-permute-done | bytes 40992 | tf_op jit(solution)/shard_map/ppermute | solution.py:58
  29.7 0.7 %mix.2.refs_1_ = bf16[16,1280]{1,0:T(8,128)(2,1)S(1)} custom-call(f32[16,1280]{1,0:T(8,128)S(1)} %get-tuple-element.32.refs_0_, bf16[16,1280]{1,0:T(8,128)(2,1)S(1)} %collective-permute-done.6.refs_1_, bf16[16,1280]{1,0:T(8,128)(2,1)S(1)} %collective-permute-done.7.refs_2_, bf16[16,1280]{1,0:T(8,128)(2,1)S(1)} %collective-permute-done.8.refs_3_, ...), custom_call_target="tpu_custom_call" | custom-call | tf_op jit(solution)/shard_map/mix/pallas_call | solution.py:440
  30.4 0.0 collective-permute-start.9
  30.4 1.2 %collective-permute-start.10 = (bf16[16,1280]{1,0:T(8,128)(2,1)S(1)}, bf16[16,1280]{1,0:T(8,128)(2,1)S(1)}, u32[]{:S(2)}, u32[]{:S(2)}) collective-permute-start(bf16[16,1280]{1,0:T(8,128)(2,1)S(1)} %mix.2.refs_1_), channel_id=1, source_target_pairs={{0,2},{1,3},{2,0},{3,1},{4,6},{5,7},{6,4},{7,5},{8,10},{9,11},{10,... | collective-permute-start | bytes 122888 | tf_op jit(solution)/shard_map/ppermute | solution.py:58
  31.6 0.6 %collective-permute-start.11 = (bf16[16,1280]{1,0:T(8,128)(2,1)S(1)}, bf16[16,1280]{1,0:T(8,128)(2,1)S(1)}, u32[]{:S(2)}, u32[]{:S(2)}) collective-permute-start(bf16[16,1280]{1,0:T(8,128)(2,1)S(1)} %mix.2.refs_1_), channel_id=1, source_target_pairs={{0,1},{1,0},{2,3},{3,2},{4,5},{5,4},{6,7},{7,6},{8,9},{9,8},{10,11... | collective-permute-start | bytes 122888 | tf_op jit(solution)/shard_map/ppermute | solution.py:58
  32.3 2.2 %fetch.8.refs_11_.refs_9_ = bf16[4,2,2064,128]{3,2,1,0:T(8,128)(2,1)S(1)} custom-call(bf16[2,16,2,2064,128]{4,3,2,1,0:T(8,128)(2,1)} %refs_0_.9), custom_call_target="tpu_custom_call" | custom-call | tf_op jit(solution)/shard_map/fetch/pallas_call | solution.py:199
  34.5 0.2 collective-permute-done.10.refs_3_
  34.7 0.8 %project.3 = (bf16[16,1280]{1,0:T(8,128)(2,1)S(1)}, f32[16,1920]{1,0:T(8,128)S(1)}, bf16[16,1536]{1,0:T(8,128)(2,1)S(1)}, bf16[16,1536]{1,0:T(8,128)(2,1)S(1)}, bf16[16,1536]{1,0:T(8,128)(2,1)S(1)}) custom-call(bf16[16,1280]{1,0:T(8,128)(2,1)S(1)} %get-tuple-element.24.refs_0_, bf16[16,1280]{1,0:T(8,128)(2,1)S(1)} %mix.2.refs_1_, ...), custom_call_target="tpu_custom_call" | custom-call | tf_op jit(solution)/shard_map/project/pallas_call | solution.py:271
  35.5 1.2 %collective-permute-start.12 = (bf16[16,1536]{1,0:T(8,128)(2,1)S(1)}, bf16[16,1536]{1,0:T(8,128)(2,1)S(1)}, u32[]{:S(2)}, u32[]{:S(2)}) collective-permute-start(bf16[16,1536]{1,0:T(8,128)(2,1)S(1)} %get-tuple-element.36), channel_id=1, source_target_pairs={{0,8},{4,12},{8,0},{12,4},{1,9},{5,13},{9,1},{13,5},{2,10},{6,14},... | collective-permute-start | bytes 147464 | tf_op jit(solution)/shard_map/ppermute | solution.py:58
  36.8 1.3 %collective-permute-start.13 = (bf16[16,1536]{1,0:T(8,128)(2,1)S(1)}, bf16[16,1536]{1,0:T(8,128)(2,1)S(1)}, u32[]{:S(2)}, u32[]{:S(2)}) collective-permute-start(bf16[16,1536]{1,0:T(8,128)(2,1)S(1)} %get-tuple-element.37), channel_id=1, source_target_pairs={{0,12},{4,8},{8,4},{12,0},{1,13},{5,9},{9,5},{13,1},{2,14},{6,10},... | collective-permute-start | bytes 147464 | tf_op jit(solution)/shard_map/ppermute | solution.py:58
  38.1 1.0 %collective-permute-start.14 = (bf16[16,1536]{1,0:T(8,128)(2,1)S(1)}, bf16[16,1536]{1,0:T(8,128)(2,1)S(1)}, u32[]{:S(2)}, u32[]{:S(2)}) collective-permute-start(bf16[16,1536]{1,0:T(8,128)(2,1)S(1)} %get-tuple-element.38), channel_id=1, source_target_pairs={{0,4},{4,0},{8,12},{12,8},{1,5},{5,1},{9,13},{13,9},{2,6},{6,2},{1... | collective-permute-start | bytes 147464 | tf_op jit(solution)/shard_map/ppermute | solution.py:58
  39.1 3.1 %fetch.9.refs_10_ = bf16[7,2,2064,128]{3,2,1,0:T(8,128)(2,1)S(1)} custom-call(bf16[2,16,2,2064,128]{4,3,2,1,0:T(8,128)(2,1)} %refs_0_.9), custom_call_target="tpu_custom_call" | custom-call | tf_op jit(solution)/shard_map/fetch/pallas_call | solution.py:199
  42.2 0.6 collective-permute-done.13.refs_2_
  42.8 0.2 collective-permute-done.14.refs_3_
  43.0 3.2 %read.3 = (f32[16,1280]{1,0:T(8,128)S(1)}, bf16[16,1280]{1,0:T(8,128)(2,1)S(1)}) custom-call(f32[16,1920]{1,0:T(8,128)S(1)} %get-tuple-element.35.refs_0_, bf16[16,1536]{1,0:T(8,128)(2,1)S(1)} %collective-permute-done.12.refs_1_, bf16[16,1536]{1,0:T(8,128)(2,1)S(1)} %collective-permute-done.13.refs_2_, bf16[16,1536]{1,0:T(8,128)(2,1)S(1)} %collective-permute-done.14.refs_3_, ...), custom_call_target="tpu_custom_call" | custom-call | tf_op jit(solution)/shard_map/read/pallas_call | solution.py:400
  46.2 1.6 %collective-permute-start.15 = (bf16[16,1280]{1,0:T(8,128)(2,1)S(1)}, bf16[16,1280]{1,0:T(8,128)(2,1)S(1)}, u32[]{:S(2)}, u32[]{:S(2)}) collective-permute-start(bf16[16,1280]{1,0:T(8,128)(2,1)S(1)} %get-tuple-element.40), channel_id=1, source_target_pairs={{0,8},{4,12},{8,0},{12,4},{1,9},{5,13},{9,1},{13,5},{2,10},{6,14},... | collective-permute-start | bytes 122888 | tf_op jit(solution)/shard_map/ppermute | solution.py:58
  47.8 1.4 %collective-permute-start.16 = (bf16[16,1280]{1,0:T(8,128)(2,1)S(1)}, bf16[16,1280]{1,0:T(8,128)(2,1)S(1)}, u32[]{:S(2)}, u32[]{:S(2)}) collective-permute-start(bf16[16,1280]{1,0:T(8,128)(2,1)S(1)} %get-tuple-element.40), channel_id=1, source_target_pairs={{0,12},{4,8},{8,4},{12,0},{1,13},{5,9},{9,5},{13,1},{2,14},{6,10},... | collective-permute-start | bytes 122888 | tf_op jit(solution)/shard_map/ppermute | solution.py:58
  49.2 0.6 collective-permute-start.17
  49.8 2.7 %collective-permute-done.15.refs_1_ = bf16[16,1280]{1,0:T(8,128)(2,1)S(1)} collective-permute-done((bf16[16,1280]{1,0:T(8,128)(2,1)S(1)}, bf16[16,1280]{1,0:T(8,128)(2,1)S(1)}, u32[]{:S(2)}, u32[]{:S(2)}) %collective-permute-start.15) | collective-permute-done | bytes 40992 | tf_op jit(solution)/shard_map/ppermute | solution.py:58
  52.4 1.2 %collective-permute-done.16.refs_2_ = bf16[16,1280]{1,0:T(8,128)(2,1)S(1)} collective-permute-done((bf16[16,1280]{1,0:T(8,128)(2,1)S(1)}, bf16[16,1280]{1,0:T(8,128)(2,1)S(1)}, u32[]{:S(2)}, u32[]{:S(2)}) %collective-permute-start.16) | collective-permute-done | bytes 40992 | tf_op jit(solution)/shard_map/ppermute | solution.py:58
  53.6 0.7 %mix.3.refs_1_ = bf16[16,1280]{1,0:T(8,128)(2,1)S(1)} custom-call(f32[16,1280]{1,0:T(8,128)S(1)} %get-tuple-element.39.refs_0_, bf16[16,1280]{1,0:T(8,128)(2,1)S(1)} %collective-permute-done.15.refs_1_, bf16[16,1280]{1,0:T(8,128)(2,1)S(1)} %collective-permute-done.16.refs_2_, bf16[16,1280]{1,0:T(8,128)(2,1)S(1)} %collective-permute-done.17.refs_3_, ...), custom_call_target="tpu_custom_call" | custom-call | tf_op jit(solution)/shard_map/mix/pallas_call | solution.py:440
  54.4 0.0 collective-permute-start.18
  54.4 1.3 %collective-permute-start.19 = (bf16[16,1280]{1,0:T(8,128)(2,1)S(1)}, bf16[16,1280]{1,0:T(8,128)(2,1)S(1)}, u32[]{:S(2)}, u32[]{:S(2)}) collective-permute-start(bf16[16,1280]{1,0:T(8,128)(2,1)S(1)} %mix.3.refs_1_), channel_id=1, source_target_pairs={{0,2},{1,3},{2,0},{3,1},{4,6},{5,7},{6,4},{7,5},{8,10},{9,11},{10,... | collective-permute-start | bytes 122888 | tf_op jit(solution)/shard_map/ppermute | solution.py:58
  55.7 0.5 collective-permute-start.20
  56.2 1.9 %collective-permute-done.18.refs_2_ = bf16[16,1280]{1,0:T(8,128)(2,1)S(1)} collective-permute-done((bf16[16,1280]{1,0:T(8,128)(2,1)S(1)}, bf16[16,1280]{1,0:T(8,128)(2,1)S(1)}, u32[]{:S(2)}, u32[]{:S(2)}) %collective-permute-start.18) | collective-permute-done | bytes 40992 | tf_op jit(solution)/shard_map/ppermute | solution.py:58
  58.1 0.5 collective-permute-done.19.refs_3_
  58.6 0.7 %finish.1 = bf16[16,1280]{1,0:T(8,128)(2,1)} custom-call(bf16[16,1280]{1,0:T(8,128)(2,1)S(1)} %get-tuple-element.34.refs_0_, bf16[16,1280]{1,0:T(8,128)(2,1)S(1)} %mix.3.refs_1_, bf16[16,1280]{1,0:T(8,128)(2,1)S(1)} %collective-permute-done.18.refs_2_, bf16[16,1280]{1,0:T(8,128)(2,1)S(1)} %collective-permute-done.19.refs_3_, ...), custom_call_target="tpu_custom_call" | custom-call | tf_op jit(solution)/shard_map/finish/pallas_call | solution.py:457
  (29 shorter events, 0.1 us)
Async XLA Ops:
  1.9 6.7 %slice-start = ((s8[6553600]{0:T(1024)(128)(4,1)}), s8[4194304]{0:T(1024)(128)(4,1)S(1)}, s32[]{:S(2)}) async-start(s8[6553600]{0:T(1024)(128)(4,1)} %bitcast.1), calls=%async_computation | async-start | bytes 8388608
  1.9 6.7 %slice-start.1 = ((s8[6553600]{0:T(1024)(128)(4,1)}), s8[2359296]{0:T(1024)(128)(4,1)S(1)}, s32[]{:S(2)}) async-start(s8[6553600]{0:T(1024)(128)(4,1)} %bitcast.1), calls=%async_computation.1 | async-start | bytes 4718592
  2.0 6.7 %copy-start = (bf16[2,1280,256]{2,1,0:T(8,128)(2,1)S(1)}, bf16[2,1280,256]{2,1,0:T(8,128)(2,1)}, u32[]{:S(2)}) copy-start(bf16[2,1280,256]{2,1,0:T(8,128)(2,1)} %refs_7_.3) | copy-start | bytes 3932164
  2.0 6.7 %copy-start.1 = (bf16[2,1280,256]{2,1,0:T(8,128)(2,1)S(1)}, bf16[2,1280,256]{2,1,0:T(8,128)(2,1)}, u32[]{:S(2)}) copy-start(bf16[2,1280,256]{2,1,0:T(8,128)(2,1)} %refs_8_.1) | copy-start | bytes 3932164
  2.0 6.7 %copy-start.2 = (f32[2,1280]{1,0:T(2,128)S(1)}, f32[2,1280]{1,0:T(2,128)}, u32[]{:S(2)}) copy-start(f32[2,1280]{1,0:T(2,128)} %refs_5_.6) | copy-start | bytes 30724
  2.0 6.7 %copy-start.3 = (bf16[2,1280,2]{1,2,0:T(2,128)(2,1)S(1)}, bf16[2,1280,2]{1,2,0:T(2,128)(2,1)}, u32[]{:S(2)}) copy-start(bf16[2,1280,2]{1,2,0:T(2,128)(2,1)} %param.17) | copy-start | bytes 30724
  2.0 5.1 %collective-permute-start = (bf16[16,1280]{1,0:T(8,128)(2,1)S(1)}, bf16[16,1280]{1,0:T(8,128)(2,1)S(1)}, u32[]{:S(2)}, u32[]{:S(2)}) collective-permute-start(bf16[16,1280]{1,0:T(8,128)(2,1)S(1)} %get-tuple-element.23.refs_0_), channel_id=1, source_target_pairs={{0,3},{1,2},{2,1},{3,0},{4,7},{5,6},{6,5},{7,4},{8,11},{9,10},{10,... | collective-permute-start | bytes 122888 | tf_op jit(solution)/shard_map/ppermute | solution.py:58
  4.5 4.1 %collective-permute-start.1 = (bf16[16,1280]{1,0:T(8,128)(2,1)S(1)}, bf16[16,1280]{1,0:T(8,128)(2,1)S(1)}, u32[]{:S(2)}, u32[]{:S(2)}) collective-permute-start(bf16[16,1280]{1,0:T(8,128)(2,1)S(1)} %get-tuple-element.23.refs_0_), channel_id=1, source_target_pairs={{0,2},{1,3},{2,0},{3,1},{4,6},{5,7},{6,4},{7,5},{8,10},{9,11},{10,... | collective-permute-start | bytes 122888 | tf_op jit(solution)/shard_map/ppermute | solution.py:58
  5.1 3.5 %collective-permute-start.2 = (bf16[16,1280]{1,0:T(8,128)(2,1)S(1)}, bf16[16,1280]{1,0:T(8,128)(2,1)S(1)}, u32[]{:S(2)}, u32[]{:S(2)}) collective-permute-start(bf16[16,1280]{1,0:T(8,128)(2,1)S(1)} %get-tuple-element.23.refs_0_), channel_id=1, source_target_pairs={{0,1},{1,0},{2,3},{3,2},{4,5},{5,4},{6,7},{7,6},{8,9},{9,8},{10,11... | collective-permute-start | bytes 122888 | tf_op jit(solution)/shard_map/ppermute | solution.py:58
  9.6 8.0 %collective-permute-start.3 = (bf16[16,1536]{1,0:T(8,128)(2,1)S(1)}, bf16[16,1536]{1,0:T(8,128)(2,1)S(1)}, u32[]{:S(2)}, u32[]{:S(2)}) collective-permute-start(bf16[16,1536]{1,0:T(8,128)(2,1)S(1)} %get-tuple-element.26), channel_id=1, source_target_pairs={{0,8},{4,12},{8,0},{12,4},{1,9},{5,13},{9,1},{13,5},{2,10},{6,14},... | collective-permute-start | bytes 147464 | tf_op jit(solution)/shard_map/ppermute | solution.py:58
  12.2 6.0 %collective-permute-start.4 = (bf16[16,1536]{1,0:T(8,128)(2,1)S(1)}, bf16[16,1536]{1,0:T(8,128)(2,1)S(1)}, u32[]{:S(2)}, u32[]{:S(2)}) collective-permute-start(bf16[16,1536]{1,0:T(8,128)(2,1)S(1)} %get-tuple-element.27), channel_id=1, source_target_pairs={{0,12},{4,8},{8,4},{12,0},{1,13},{5,9},{9,5},{13,1},{2,14},{6,10},... | collective-permute-start | bytes 147464 | tf_op jit(solution)/shard_map/ppermute | solution.py:58
  13.6 4.6 %copy-start.4 = (f32[2,2]{1,0:T(2,128)S(1)}, f32[2,2]{1,0:T(2,128)}, u32[]{:S(2)}) copy-start(f32[2,2]{1,0:T(2,128)} %refs_4_.8) | copy-start | bytes 52
  13.6 4.6 %collective-permute-start.5 = (bf16[16,1536]{1,0:T(8,128)(2,1)S(1)}, bf16[16,1536]{1,0:T(8,128)(2,1)S(1)}, u32[]{:S(2)}, u32[]{:S(2)}) collective-permute-start(bf16[16,1536]{1,0:T(8,128)(2,1)S(1)} %get-tuple-element.28), channel_id=1, source_target_pairs={{0,4},{4,0},{8,12},{12,8},{1,5},{5,1},{9,13},{13,9},{2,6},{6,2},{1... | collective-permute-start | bytes 147464 | tf_op jit(solution)/shard_map/ppermute | solution.py:58
  21.5 8.1 %slice-start.2 = ((s8[6553600]{0:T(1024)(128)(4,1)}), s8[4194304]{0:T(1024)(128)(4,1)S(1)}, s32[]{:S(2)}) async-start(s8[6553600]{0:T(1024)(128)(4,1)} %bitcast.3), calls=%async_computation.2 | async-start | bytes 8388608
  21.6 8.1 %slice-start.3 = ((s8[6553600]{0:T(1024)(128)(4,1)}), s8[2359296]{0:T(1024)(128)(4,1)S(1)}, s32[]{:S(2)}) async-start(s8[6553600]{0:T(1024)(128)(4,1)} %bitcast.3), calls=%async_computation.3 | async-start | bytes 4718592
  21.6 8.1 %copy-start.5 = (f32[2,128]{1,0:T(2,128)S(1)}, f32[2,128]{1,0:T(2,128)}, u32[]{:S(2)}) copy-start(f32[2,128]{1,0:T(2,128)} %refs_4_.9) | copy-start | bytes 3076
  21.6 6.1 %collective-permute-start.6 = (bf16[16,1280]{1,0:T(8,128)(2,1)S(1)}, bf16[16,1280]{1,0:T(8,128)(2,1)S(1)}, u32[]{:S(2)}, u32[]{:S(2)}) collective-permute-start(bf16[16,1280]{1,0:T(8,128)(2,1)S(1)} %get-tuple-element.33), channel_id=1, source_target_pairs={{0,8},{4,12},{8,0},{12,4},{1,9},{5,13},{9,1},{13,5},{2,10},{6,14},... | collective-permute-start | bytes 122888 | tf_op jit(solution)/shard_map/ppermute | solution.py:58
  23.8 5.8 %collective-permute-start.7 = (bf16[16,1280]{1,0:T(8,128)(2,1)S(1)}, bf16[16,1280]{1,0:T(8,128)(2,1)S(1)}, u32[]{:S(2)}, u32[]{:S(2)}) collective-permute-start(bf16[16,1280]{1,0:T(8,128)(2,1)S(1)} %get-tuple-element.33), channel_id=1, source_target_pairs={{0,12},{4,8},{8,4},{12,0},{1,13},{5,9},{9,5},{13,1},{2,14},{6,10},... | collective-permute-start | bytes 122888 | tf_op jit(solution)/shard_map/ppermute | solution.py:58
  25.2 4.5 %collective-permute-start.8 = (bf16[16,1280]{1,0:T(8,128)(2,1)S(1)}, bf16[16,1280]{1,0:T(8,128)(2,1)S(1)}, u32[]{:S(2)}, u32[]{:S(2)}) collective-permute-start(bf16[16,1280]{1,0:T(8,128)(2,1)S(1)} %get-tuple-element.33), channel_id=1, source_target_pairs={{0,4},{4,0},{8,12},{12,8},{1,5},{5,1},{9,13},{13,9},{2,6},{6,2},{1... | collective-permute-start | bytes 122888 | tf_op jit(solution)/shard_map/ppermute | solution.py:58
  30.4 4.1 %collective-permute-start.9 = (bf16[16,1280]{1,0:T(8,128)(2,1)S(1)}, bf16[16,1280]{1,0:T(8,128)(2,1)S(1)}, u32[]{:S(2)}, u32[]{:S(2)}) collective-permute-start(bf16[16,1280]{1,0:T(8,128)(2,1)S(1)} %mix.2.refs_1_), channel_id=1, source_target_pairs={{0,3},{1,2},{2,1},{3,0},{4,7},{5,6},{6,5},{7,4},{8,11},{9,10},{10,... | collective-permute-start | bytes 122888 | tf_op jit(solution)/shard_map/ppermute | solution.py:58
  30.4 4.3 %collective-permute-start.10 = (bf16[16,1280]{1,0:T(8,128)(2,1)S(1)}, bf16[16,1280]{1,0:T(8,128)(2,1)S(1)}, u32[]{:S(2)}, u32[]{:S(2)}) collective-permute-start(bf16[16,1280]{1,0:T(8,128)(2,1)S(1)} %mix.2.refs_1_), channel_id=1, source_target_pairs={{0,2},{1,3},{2,0},{3,1},{4,6},{5,7},{6,4},{7,5},{8,10},{9,11},{10,... | collective-permute-start | bytes 122888 | tf_op jit(solution)/shard_map/ppermute | solution.py:58
  31.6 3.1 %collective-permute-start.11 = (bf16[16,1280]{1,0:T(8,128)(2,1)S(1)}, bf16[16,1280]{1,0:T(8,128)(2,1)S(1)}, u32[]{:S(2)}, u32[]{:S(2)}) collective-permute-start(bf16[16,1280]{1,0:T(8,128)(2,1)S(1)} %mix.2.refs_1_), channel_id=1, source_target_pairs={{0,1},{1,0},{2,3},{3,2},{4,5},{5,4},{6,7},{7,6},{8,9},{9,8},{10,11... | collective-permute-start | bytes 122888 | tf_op jit(solution)/shard_map/ppermute | solution.py:58
  35.5 6.7 %collective-permute-start.12 = (bf16[16,1536]{1,0:T(8,128)(2,1)S(1)}, bf16[16,1536]{1,0:T(8,128)(2,1)S(1)}, u32[]{:S(2)}, u32[]{:S(2)}) collective-permute-start(bf16[16,1536]{1,0:T(8,128)(2,1)S(1)} %get-tuple-element.36), channel_id=1, source_target_pairs={{0,8},{4,12},{8,0},{12,4},{1,9},{5,13},{9,1},{13,5},{2,10},{6,14},... | collective-permute-start | bytes 147464 | tf_op jit(solution)/shard_map/ppermute | solution.py:58
  36.8 6.0 %collective-permute-start.13 = (bf16[16,1536]{1,0:T(8,128)(2,1)S(1)}, bf16[16,1536]{1,0:T(8,128)(2,1)S(1)}, u32[]{:S(2)}, u32[]{:S(2)}) collective-permute-start(bf16[16,1536]{1,0:T(8,128)(2,1)S(1)} %get-tuple-element.37), channel_id=1, source_target_pairs={{0,12},{4,8},{8,4},{12,0},{1,13},{5,9},{9,5},{13,1},{2,14},{6,10},... | collective-permute-start | bytes 147464 | tf_op jit(solution)/shard_map/ppermute | solution.py:58
  38.1 4.9 %collective-permute-start.14 = (bf16[16,1536]{1,0:T(8,128)(2,1)S(1)}, bf16[16,1536]{1,0:T(8,128)(2,1)S(1)}, u32[]{:S(2)}, u32[]{:S(2)}) collective-permute-start(bf16[16,1536]{1,0:T(8,128)(2,1)S(1)} %get-tuple-element.38), channel_id=1, source_target_pairs={{0,4},{4,0},{8,12},{12,8},{1,5},{5,1},{9,13},{13,9},{2,6},{6,2},{1... | collective-permute-start | bytes 147464 | tf_op jit(solution)/shard_map/ppermute | solution.py:58
  46.2 6.2 %collective-permute-start.15 = (bf16[16,1280]{1,0:T(8,128)(2,1)S(1)}, bf16[16,1280]{1,0:T(8,128)(2,1)S(1)}, u32[]{:S(2)}, u32[]{:S(2)}) collective-permute-start(bf16[16,1280]{1,0:T(8,128)(2,1)S(1)} %get-tuple-element.40), channel_id=1, source_target_pairs={{0,8},{4,12},{8,0},{12,4},{1,9},{5,13},{9,1},{13,5},{2,10},{6,14},... | collective-permute-start | bytes 122888 | tf_op jit(solution)/shard_map/ppermute | solution.py:58
  47.8 5.8 %collective-permute-start.16 = (bf16[16,1280]{1,0:T(8,128)(2,1)S(1)}, bf16[16,1280]{1,0:T(8,128)(2,1)S(1)}, u32[]{:S(2)}, u32[]{:S(2)}) collective-permute-start(bf16[16,1280]{1,0:T(8,128)(2,1)S(1)} %get-tuple-element.40), channel_id=1, source_target_pairs={{0,12},{4,8},{8,4},{12,0},{1,13},{5,9},{9,5},{13,1},{2,14},{6,10},... | collective-permute-start | bytes 122888 | tf_op jit(solution)/shard_map/ppermute | solution.py:58
  49.2 4.4 %collective-permute-start.17 = (bf16[16,1280]{1,0:T(8,128)(2,1)S(1)}, bf16[16,1280]{1,0:T(8,128)(2,1)S(1)}, u32[]{:S(2)}, u32[]{:S(2)}) collective-permute-start(bf16[16,1280]{1,0:T(8,128)(2,1)S(1)} %get-tuple-element.40), channel_id=1, source_target_pairs={{0,4},{4,0},{8,12},{12,8},{1,5},{5,1},{9,13},{13,9},{2,6},{6,2},{1... | collective-permute-start | bytes 122888 | tf_op jit(solution)/shard_map/ppermute | solution.py:58
  54.4 3.8 %collective-permute-start.18 = (bf16[16,1280]{1,0:T(8,128)(2,1)S(1)}, bf16[16,1280]{1,0:T(8,128)(2,1)S(1)}, u32[]{:S(2)}, u32[]{:S(2)}) collective-permute-start(bf16[16,1280]{1,0:T(8,128)(2,1)S(1)} %mix.3.refs_1_), channel_id=1, source_target_pairs={{0,3},{1,2},{2,1},{3,0},{4,7},{5,6},{6,5},{7,4},{8,11},{9,10},{10,... | collective-permute-start | bytes 122888 | tf_op jit(solution)/shard_map/ppermute | solution.py:58
  54.4 4.2 %collective-permute-start.19 = (bf16[16,1280]{1,0:T(8,128)(2,1)S(1)}, bf16[16,1280]{1,0:T(8,128)(2,1)S(1)}, u32[]{:S(2)}, u32[]{:S(2)}) collective-permute-start(bf16[16,1280]{1,0:T(8,128)(2,1)S(1)} %mix.3.refs_1_), channel_id=1, source_target_pairs={{0,2},{1,3},{2,0},{3,1},{4,6},{5,7},{6,4},{7,5},{8,10},{9,11},{10,... | collective-permute-start | bytes 122888 | tf_op jit(solution)/shard_map/ppermute | solution.py:58
  55.7 2.9 %collective-permute-start.20 = (bf16[16,1280]{1,0:T(8,128)(2,1)S(1)}, bf16[16,1280]{1,0:T(8,128)(2,1)S(1)}, u32[]{:S(2)}, u32[]{:S(2)}) collective-permute-start(bf16[16,1280]{1,0:T(8,128)(2,1)S(1)} %mix.3.refs_1_), channel_id=1, source_target_pairs={{0,1},{1,0},{2,3},{3,2},{4,5},{5,4},{6,7},{7,6},{8,9},{9,8},{10,11... | collective-permute-start | bytes 122888 | tf_op jit(solution)/shard_map/ppermute | solution.py:58

commit v6 on v4

--- a/solution.py
+++ b/solution.py
@@ -73,9 +73,11 @@
 
 
 def split_dot(wide, weight):
-    rows = wide.shape[0]
-    out = jnp.dot(jnp.concatenate(split(wide), axis=0), weight, preferred_element_type=F32)
-    return out[:rows] + out[rows:]
+    rows, depth = wide.shape
+    empty = jnp.zeros((max(LANES - 2 * rows, 0), depth), BF16)
+    parts = jnp.concatenate((*split(wide), empty), axis=0)
+    out = jnp.dot(parts, weight, preferred_element_type=F32)
+    return out[:rows] + out[rows : 2 * rows]
 
 
 def add_terms(refs):
@@ -431,8 +433,10 @@
     for start in range(0, readout.shape[1], head_size):
         part = readout[:, start : start + head_size]
         mean = jnp.mean(part * part, axis=1, keepdims=True)
-        mixed_ref[:, start : start + head_size] = part * lax.rsqrt(mean + EPS) * gain
-    wire_ref[...] = split_dot(mixed_ref[...], weight_ref[layer]).astype(wire_ref.dtype)
+        mixed = part * lax.rsqrt(mean + EPS) * gain
+        mixed_ref[:, start : start + head_size] = mixed.astype(BF16)
+    out = jnp.dot(mixed_ref[...], weight_ref[layer], preferred_element_type=F32)
+    wire_ref[...] = out.astype(wire_ref.dtype)
 
 
 def mix(layer, wire, terms, read_gain, weight, held):
@@ -442,7 +446,7 @@
         out_shape=jax.ShapeDtypeStruct((requests, weight.shape[2]), wire),
         in_specs=[VMEM_SPEC] * (len(terms) + 2) + [ANY_SPEC] * len(held),
         out_specs=VMEM_SPEC,
-        scratch_shapes=[pltpu.VMEM((requests, rows), F32)],
+        scratch_shapes=[pltpu.VMEM((requests, rows), BF16)],
         compiler_params=params(8),
         name="mix",
     )(*terms, read_gain, resident(weight), *[resident(part) for part in held])

time: 59.3 us -> 59.1 us (level)
  no operation moved by 1% of the time
where the time goes in v6:
time: 59.1 us; the launch traced here: 58.8 us
  Pallas kernels  25.5 us (43%)
  starting transfers between devices  21.8 us (37%)
  waiting for transfers between devices  11.1 us (19%)
    ppermute x21, starting transfers between devices, exchange(): lax.ppermute(wire, axis, [(rank, rank ^ step) for rank in range(size)])  21.8 us
    pallas_call x5, Pallas kernels, fetch(): pl.pallas_call(functools.partial(fetch_kernel, plan, len(sources)), out_s...  13.4 us
    ppermute x21, waiting for transfers between devices, exchange(): lax.ppermute(wire, axis, [(rank, rank ^ step) for rank in range(size)])  11.1 us
    pallas_call x2, Pallas kernels, read(): pl.pallas_call(functools.partial(read_kernel, layer, sizes, len(terms), c...  6.58 us
    pallas_call x1, Pallas kernels, pick_rows(): pl.pallas_call(pick_kernel, out_shape=[jax.ShapeDtypeStruct((requests, wi...  1.98 us
    pallas_call x2, Pallas kernels, project(): pl.pallas_call(functools.partial(project_kernel, layer, len(terms), len(c...  1.66 us
    pallas_call x2, Pallas kernels, mix(): pl.pallas_call(functools.partial(mix_kernel, layer, len(terms), len(held)...  1.24 us
  transfers between devices with their start and end apart: 21, of which 10 were waited for; matrix products, arithmetic and copies ran while one was open for 0% of the time, Pallas kernels for 23%

profile of v6, /device:TPU:0, one launch (start us, length us, event | category | flops | bytes accessed | tf_op | source)
XLA Modules:
  0.0 58.8 jit_solution(8215984839515052071)
XLA Ops:
  0.0 2.0 %pick_rows.1 = (bf16[16,1280]{1,0:T(8,128)(2,1)S(1)}, bf16[256,2064]{1,0:T(8,128)(2,1)S(1)}, bf16[256,2064]{1,0:T(8,128)(2,1)S(1)}, f32[1,2064]{1,0:T(1,128)S(1)}) custom-call(s32[16]{0:T(128)} %ids_ref.1, bf16[18992,1280]{1,0:T(8,128)(2,1)} %table_ref.1), custom_call_target="tpu_custom_call" | custom-call | tf_op jit(solution)/shard_map/pick_rows/pallas_call | solution.py:163
  2.0 0.0 slice-start
  2.0 0.0 copy-start
  2.0 0.0 copy-start.1
  2.0 0.0 copy-start.2
  2.1 0.0 copy-start.3
  2.1 2.4 %collective-permute-start = (bf16[16,1280]{1,0:T(8,128)(2,1)S(1)}, bf16[16,1280]{1,0:T(8,128)(2,1)S(1)}, u32[]{:S(2)}, u32[]{:S(2)}) collective-permute-start(bf16[16,1280]{1,0:T(8,128)(2,1)S(1)} %get-tuple-element.23.refs_0_), channel_id=1, source_target_pairs={{0,3},{1,2},{2,1},{3,0},{4,7},{5,6},{6,5},{7,4},{8,11},{9,10},{10,... | collective-permute-start | bytes 122888 | tf_op jit(solution)/shard_map/ppermute | solution.py:58
  4.5 0.7 %collective-permute-start.1 = (bf16[16,1280]{1,0:T(8,128)(2,1)S(1)}, bf16[16,1280]{1,0:T(8,128)(2,1)S(1)}, u32[]{:S(2)}, u32[]{:S(2)}) collective-permute-start(bf16[16,1280]{1,0:T(8,128)(2,1)S(1)} %get-tuple-element.23.refs_0_), channel_id=1, source_target_pairs={{0,2},{1,3},{2,0},{3,1},{4,6},{5,7},{6,4},{7,5},{8,10},{9,11},{10,... | collective-permute-start | bytes 122888 | tf_op jit(solution)/shard_map/ppermute | solution.py:58
  5.2 0.0 collective-permute-start.2
  5.2 2.2 %fetch.5.refs_9_.refs_8_ = bf16[4,2,2064,128]{3,2,1,0:T(8,128)(2,1)S(1)} custom-call(bf16[2,16,2,2064,128]{4,3,2,1,0:T(8,128)(2,1)} %refs_0_.9), custom_call_target="tpu_custom_call" | custom-call | tf_op jit(solution)/shard_map/fetch/pallas_call | solution.py:201
  7.4 1.2 %collective-permute-done.1.refs_2_ = bf16[16,1280]{1,0:T(8,128)(2,1)S(1)} collective-permute-done((bf16[16,1280]{1,0:T(8,128)(2,1)S(1)}, bf16[16,1280]{1,0:T(8,128)(2,1)S(1)}, u32[]{:S(2)}, u32[]{:S(2)}) %collective-permute-start.1) | collective-permute-done | bytes 40992 | tf_op jit(solution)/shard_map/ppermute | solution.py:58
  8.7 0.8 %project.2 = (bf16[16,1280]{1,0:T(8,128)(2,1)S(1)}, f32[16,1920]{1,0:T(8,128)S(1)}, bf16[16,1536]{1,0:T(8,128)(2,1)S(1)}, bf16[16,1536]{1,0:T(8,128)(2,1)S(1)}, bf16[16,1536]{1,0:T(8,128)(2,1)S(1)}) custom-call(bf16[16,1280]{1,0:T(8,128)(2,1)S(1)} %get-tuple-element.23.refs_0_, bf16[16,1280]{1,0:T(8,128)(2,1)S(1)} %collective-permute-done.refs_1_, ...), custom_call_target="tpu_custom_call" | custom-call | tf_op jit(solution)/shard_map/project/pallas_call | solution.py:273
  9.6 2.7 %collective-permute-start.3 = (bf16[16,1536]{1,0:T(8,128)(2,1)S(1)}, bf16[16,1536]{1,0:T(8,128)(2,1)S(1)}, u32[]{:S(2)}, u32[]{:S(2)}) collective-permute-start(bf16[16,1536]{1,0:T(8,128)(2,1)S(1)} %get-tuple-element.26), channel_id=1, source_target_pairs={{0,8},{4,12},{8,0},{12,4},{1,9},{5,13},{9,1},{13,5},{2,10},{6,14},... | collective-permute-start | bytes 147464 | tf_op jit(solution)/shard_map/ppermute | solution.py:58
  12.2 1.3 %collective-permute-start.4 = (bf16[16,1536]{1,0:T(8,128)(2,1)S(1)}, bf16[16,1536]{1,0:T(8,128)(2,1)S(1)}, u32[]{:S(2)}, u32[]{:S(2)}) collective-permute-start(bf16[16,1536]{1,0:T(8,128)(2,1)S(1)} %get-tuple-element.27), channel_id=1, source_target_pairs={{0,12},{4,8},{8,4},{12,0},{1,13},{5,9},{9,5},{13,1},{2,14},{6,10},... | collective-permute-start | bytes 147464 | tf_op jit(solution)/shard_map/ppermute | solution.py:58
  13.6 0.2 collective-permute-start.5
  13.8 3.4 %fetch.6.refs_9_ = bf16[8,2,2064,128]{3,2,1,0:T(8,128)(2,1)S(1)} custom-call(bf16[2,16,2,2064,128]{4,3,2,1,0:T(8,128)(2,1)} %refs_0_.9), custom_call_target="tpu_custom_call" | custom-call | tf_op jit(solution)/shard_map/fetch/pallas_call | solution.py:201
  17.2 1.0 %collective-permute-done.4.refs_2_ = bf16[16,1536]{1,0:T(8,128)(2,1)S(1)} collective-permute-done((bf16[16,1536]{1,0:T(8,128)(2,1)S(1)}, bf16[16,1536]{1,0:T(8,128)(2,1)S(1)}, u32[]{:S(2)}, u32[]{:S(2)}) %collective-permute-start.4) | collective-permute-done | bytes 49184 | tf_op jit(solution)/shard_map/ppermute | solution.py:58
  18.2 3.4 %read.2 = (f32[16,1280]{1,0:T(8,128)S(1)}, bf16[16,1280]{1,0:T(8,128)(2,1)S(1)}) custom-call(f32[16,1920]{1,0:T(8,128)S(1)} %get-tuple-element.25.refs_0_, bf16[16,1536]{1,0:T(8,128)(2,1)S(1)} %collective-permute-done.3.refs_1_, bf16[16,1536]{1,0:T(8,128)(2,1)S(1)} %collective-permute-done.4.refs_2_, bf16[16,1536]{1,0:T(8,128)(2,1)S(1)} %collective-permute-done.5.refs_3_, ...), custom_call_target="tpu_custom_call" | custom-call | tf_op jit(solution)/shard_map/read/pallas_call | solution.py:402
  21.6 0.0 slice-start.2
  21.6 1.9 %collective-permute-start.6 = (bf16[16,1280]{1,0:T(8,128)(2,1)S(1)}, bf16[16,1280]{1,0:T(8,128)(2,1)S(1)}, u32[]{:S(2)}, u32[]{:S(2)}) collective-permute-start(bf16[16,1280]{1,0:T(8,128)(2,1)S(1)} %get-tuple-element.33), channel_id=1, source_target_pairs={{0,8},{4,12},{8,0},{12,4},{1,9},{5,13},{9,1},{13,5},{2,10},{6,14},... | collective-permute-start | bytes 122888 | tf_op jit(solution)/shard_map/ppermute | solution.py:58
  23.5 1.3 %collective-permute-start.7 = (bf16[16,1280]{1,0:T(8,128)(2,1)S(1)}, bf16[16,1280]{1,0:T(8,128)(2,1)S(1)}, u32[]{:S(2)}, u32[]{:S(2)}) collective-permute-start(bf16[16,1280]{1,0:T(8,128)(2,1)S(1)} %get-tuple-element.33), channel_id=1, source_target_pairs={{0,12},{4,8},{8,4},{12,0},{1,13},{5,9},{9,5},{13,1},{2,14},{6,10},... | collective-permute-start | bytes 122888 | tf_op jit(solution)/shard_map/ppermute | solution.py:58
  24.9 0.3 collective-permute-start.8
  25.2 2.5 %fetch.7.refs_6_.refs_10_.refs_8_ = bf16[5,2,2064,128]{3,2,1,0:T(8,128)(2,1)S(1)} custom-call(bf16[2,16,2,2064,128]{4,3,2,1,0:T(8,128)(2,1)} %refs_0_.9), custom_call_target="tpu_custom_call" | custom-call | tf_op jit(solution)/shard_map/fetch/pallas_call | solution.py:201
  27.7 1.7 %collective-permute-done.7.refs_2_ = bf16[16,1280]{1,0:T(8,128)(2,1)S(1)} collective-permute-done((bf16[16,1280]{1,0:T(8,128)(2,1)S(1)}, bf16[16,1280]{1,0:T(8,128)(2,1)S(1)}, u32[]{:S(2)}, u32[]{:S(2)}) %collective-permute-start.7) | collective-permute-done | bytes 40992 | tf_op jit(solution)/shard_map/ppermute | solution.py:58
  29.4 0.6 %mix.2.refs_1_ = bf16[16,1280]{1,0:T(8,128)(2,1)S(1)} custom-call(f32[16,1280]{1,0:T(8,128)S(1)} %get-tuple-element.32.refs_0_, bf16[16,1280]{1,0:T(8,128)(2,1)S(1)} %collective-permute-done.6.refs_1_, bf16[16,1280]{1,0:T(8,128)(2,1)S(1)} %collective-permute-done.7.refs_2_, bf16[16,1280]{1,0:T(8,128)(2,1)S(1)} %collective-permute-done.8.refs_3_, ...), custom_call_target="tpu_custom_call" | custom-call | tf_op jit(solution)/shard_map/mix/pallas_call | solution.py:444
  30.0 1.3 %collective-permute-start.10 = (bf16[16,1280]{1,0:T(8,128)(2,1)S(1)}, bf16[16,1280]{1,0:T(8,128)(2,1)S(1)}, u32[]{:S(2)}, u32[]{:S(2)}) collective-permute-start(bf16[16,1280]{1,0:T(8,128)(2,1)S(1)} %mix.2.refs_1_), channel_id=1, source_target_pairs={{0,2},{1,3},{2,0},{3,1},{4,6},{5,7},{6,4},{7,5},{8,10},{9,11},{10,... | collective-permute-start | bytes 122888 | tf_op jit(solution)/shard_map/ppermute | solution.py:58
  31.3 0.6 collective-permute-start.11
  31.9 2.2 %fetch.8.refs_11_.refs_9_ = bf16[4,2,2064,128]{3,2,1,0:T(8,128)(2,1)S(1)} custom-call(bf16[2,16,2,2064,128]{4,3,2,1,0:T(8,128)(2,1)} %refs_0_.9), custom_call_target="tpu_custom_call" | custom-call | tf_op jit(solution)/shard_map/fetch/pallas_call | solution.py:201
  34.1 0.2 collective-permute-done.10.refs_3_
  34.3 0.8 %project.3 = (bf16[16,1280]{1,0:T(8,128)(2,1)S(1)}, f32[16,1920]{1,0:T(8,128)S(1)}, bf16[16,1536]{1,0:T(8,128)(2,1)S(1)}, bf16[16,1536]{1,0:T(8,128)(2,1)S(1)}, bf16[16,1536]{1,0:T(8,128)(2,1)S(1)}) custom-call(bf16[16,1280]{1,0:T(8,128)(2,1)S(1)} %get-tuple-element.24.refs_0_, bf16[16,1280]{1,0:T(8,128)(2,1)S(1)} %mix.2.refs_1_, ...), custom_call_target="tpu_custom_call" | custom-call | tf_op jit(solution)/shard_map/project/pallas_call | solution.py:273
  35.1 1.2 %collective-permute-start.12 = (bf16[16,1536]{1,0:T(8,128)(2,1)S(1)}, bf16[16,1536]{1,0:T(8,128)(2,1)S(1)}, u32[]{:S(2)}, u32[]{:S(2)}) collective-permute-start(bf16[16,1536]{1,0:T(8,128)(2,1)S(1)} %get-tuple-element.36), channel_id=1, source_target_pairs={{0,8},{4,12},{8,0},{12,4},{1,9},{5,13},{9,1},{13,5},{2,10},{6,14},... | collective-permute-start | bytes 147464 | tf_op jit(solution)/shard_map/ppermute | solution.py:58
  36.3 1.4 %collective-permute-start.13 = (bf16[16,1536]{1,0:T(8,128)(2,1)S(1)}, bf16[16,1536]{1,0:T(8,128)(2,1)S(1)}, u32[]{:S(2)}, u32[]{:S(2)}) collective-permute-start(bf16[16,1536]{1,0:T(8,128)(2,1)S(1)} %get-tuple-element.37), channel_id=1, source_target_pairs={{0,12},{4,8},{8,4},{12,0},{1,13},{5,9},{9,5},{13,1},{2,14},{6,10},... | collective-permute-start | bytes 147464 | tf_op jit(solution)/shard_map/ppermute | solution.py:58
  37.7 1.0 %collective-permute-start.14 = (bf16[16,1536]{1,0:T(8,128)(2,1)S(1)}, bf16[16,1536]{1,0:T(8,128)(2,1)S(1)}, u32[]{:S(2)}, u32[]{:S(2)}) collective-permute-start(bf16[16,1536]{1,0:T(8,128)(2,1)S(1)} %get-tuple-element.38), channel_id=1, source_target_pairs={{0,4},{4,0},{8,12},{12,8},{1,5},{5,1},{9,13},{13,9},{2,6},{6,2},{1... | collective-permute-start | bytes 147464 | tf_op jit(solution)/shard_map/ppermute | solution.py:58
  38.7 3.1 %fetch.9.refs_10_ = bf16[7,2,2064,128]{3,2,1,0:T(8,128)(2,1)S(1)} custom-call(bf16[2,16,2,2064,128]{4,3,2,1,0:T(8,128)(2,1)} %refs_0_.9), custom_call_target="tpu_custom_call" | custom-call | tf_op jit(solution)/shard_map/fetch/pallas_call | solution.py:201
  41.8 0.6 collective-permute-done.13.refs_2_
  42.4 0.2 collective-permute-done.14.refs_3_
  42.6 3.2 %read.3 = (f32[16,1280]{1,0:T(8,128)S(1)}, bf16[16,1280]{1,0:T(8,128)(2,1)S(1)}) custom-call(f32[16,1920]{1,0:T(8,128)S(1)} %get-tuple-element.35.refs_0_, bf16[16,1536]{1,0:T(8,128)(2,1)S(1)} %collective-permute-done.12.refs_1_, bf16[16,1536]{1,0:T(8,128)(2,1)S(1)} %collective-permute-done.13.refs_2_, bf16[16,1536]{1,0:T(8,128)(2,1)S(1)} %collective-permute-done.14.refs_3_, ...), custom_call_target="tpu_custom_call" | custom-call | tf_op jit(solution)/shard_map/read/pallas_call | solution.py:402
  45.8 1.6 %collective-permute-start.15 = (bf16[16,1280]{1,0:T(8,128)(2,1)S(1)}, bf16[16,1280]{1,0:T(8,128)(2,1)S(1)}, u32[]{:S(2)}, u32[]{:S(2)}) collective-permute-start(bf16[16,1280]{1,0:T(8,128)(2,1)S(1)} %get-tuple-element.40), channel_id=1, source_target_pairs={{0,8},{4,12},{8,0},{12,4},{1,9},{5,13},{9,1},{13,5},{2,10},{6,14},... | collective-permute-start | bytes 122888 | tf_op jit(solution)/shard_map/ppermute | solution.py:58
  47.4 1.4 %collective-permute-start.16 = (bf16[16,1280]{1,0:T(8,128)(2,1)S(1)}, bf16[16,1280]{1,0:T(8,128)(2,1)S(1)}, u32[]{:S(2)}, u32[]{:S(2)}) collective-permute-start(bf16[16,1280]{1,0:T(8,128)(2,1)S(1)} %get-tuple-element.40), channel_id=1, source_target_pairs={{0,12},{4,8},{8,4},{12,0},{1,13},{5,9},{9,5},{13,1},{2,14},{6,10},... | collective-permute-start | bytes 122888 | tf_op jit(solution)/shard_map/ppermute | solution.py:58
  48.8 0.6 collective-permute-start.17
  49.3 2.7 %collective-permute-done.15.refs_1_ = bf16[16,1280]{1,0:T(8,128)(2,1)S(1)} collective-permute-done((bf16[16,1280]{1,0:T(8,128)(2,1)S(1)}, bf16[16,1280]{1,0:T(8,128)(2,1)S(1)}, u32[]{:S(2)}, u32[]{:S(2)}) %collective-permute-start.15) | collective-permute-done | bytes 40992 | tf_op jit(solution)/shard_map/ppermute | solution.py:58
  52.0 1.2 %collective-permute-done.16.refs_2_ = bf16[16,1280]{1,0:T(8,128)(2,1)S(1)} collective-permute-done((bf16[16,1280]{1,0:T(8,128)(2,1)S(1)}, bf16[16,1280]{1,0:T(8,128)(2,1)S(1)}, u32[]{:S(2)}, u32[]{:S(2)}) %collective-permute-start.16) | collective-permute-done | bytes 40992 | tf_op jit(solution)/shard_map/ppermute | solution.py:58
  53.2 0.6 %mix.3.refs_1_ = bf16[16,1280]{1,0:T(8,128)(2,1)S(1)} custom-call(f32[16,1280]{1,0:T(8,128)S(1)} %get-tuple-element.39.refs_0_, bf16[16,1280]{1,0:T(8,128)(2,1)S(1)} %collective-permute-done.15.refs_1_, bf16[16,1280]{1,0:T(8,128)(2,1)S(1)} %collective-permute-done.16.refs_2_, bf16[16,1280]{1,0:T(8,128)(2,1)S(1)} %collective-permute-done.17.refs_3_, ...), custom_call_target="tpu_custom_call" | custom-call | tf_op jit(solution)/shard_map/mix/pallas_call | solution.py:444
  53.8 1.3 %collective-permute-start.19 = (bf16[16,1280]{1,0:T(8,128)(2,1)S(1)}, bf16[16,1280]{1,0:T(8,128)(2,1)S(1)}, u32[]{:S(2)}, u32[]{:S(2)}) collective-permute-start(bf16[16,1280]{1,0:T(8,128)(2,1)S(1)} %mix.3.refs_1_), channel_id=1, source_target_pairs={{0,2},{1,3},{2,0},{3,1},{4,6},{5,7},{6,4},{7,5},{8,10},{9,11},{10,... | collective-permute-start | bytes 122888 | tf_op jit(solution)/shard_map/ppermute | solution.py:58
  55.1 0.6 collective-permute-start.20
  55.7 1.9 %collective-permute-done.18.refs_2_ = bf16[16,1280]{1,0:T(8,128)(2,1)S(1)} collective-permute-done((bf16[16,1280]{1,0:T(8,128)(2,1)S(1)}, bf16[16,1280]{1,0:T(8,128)(2,1)S(1)}, u32[]{:S(2)}, u32[]{:S(2)}) %collective-permute-start.18) | collective-permute-done | bytes 40992 | tf_op jit(solution)/shard_map/ppermute | solution.py:58
  57.6 0.5 collective-permute-done.19.refs_3_
  58.1 0.7 %finish.1 = bf16[16,1280]{1,0:T(8,128)(2,1)} custom-call(bf16[16,1280]{1,0:T(8,128)(2,1)S(1)} %get-tuple-element.34.refs_0_, bf16[16,1280]{1,0:T(8,128)(2,1)S(1)} %mix.3.refs_1_, bf16[16,1280]{1,0:T(8,128)(2,1)S(1)} %collective-permute-done.18.refs_2_, bf16[16,1280]{1,0:T(8,128)(2,1)S(1)} %collective-permute-done.19.refs_3_, ...), custom_call_target="tpu_custom_call" | custom-call | tf_op jit(solution)/shard_map/finish/pallas_call | solution.py:461
  (29 shorter events, 0.1 us)
Async XLA Ops:
  2.0 6.7 %slice-start = ((s8[6553600]{0:T(1024)(128)(4,1)}), s8[4194304]{0:T(1024)(128)(4,1)S(1)}, s32[]{:S(2)}) async-start(s8[6553600]{0:T(1024)(128)(4,1)} %bitcast.1), calls=%async_computation | async-start | bytes 8388608
  2.0 6.7 %slice-start.1 = ((s8[6553600]{0:T(1024)(128)(4,1)}), s8[2359296]{0:T(1024)(128)(4,1)S(1)}, s32[]{:S(2)}) async-start(s8[6553600]{0:T(1024)(128)(4,1)} %bitcast.1), calls=%async_computation.1 | async-start | bytes 4718592
  2.0 6.7 %copy-start = (bf16[2,1280,256]{2,1,0:T(8,128)(2,1)S(1)}, bf16[2,1280,256]{2,1,0:T(8,128)(2,1)}, u32[]{:S(2)}) copy-start(bf16[2,1280,256]{2,1,0:T(8,128)(2,1)} %refs_7_.3) | copy-start | bytes 3932164
  2.0 6.7 %copy-start.1 = (bf16[2,1280,256]{2,1,0:T(8,128)(2,1)S(1)}, bf16[2,1280,256]{2,1,0:T(8,128)(2,1)}, u32[]{:S(2)}) copy-start(bf16[2,1280,256]{2,1,0:T(8,128)(2,1)} %refs_8_.1) | copy-start | bytes 3932164
  2.0 6.7 %copy-start.2 = (f32[2,1280]{1,0:T(2,128)S(1)}, f32[2,1280]{1,0:T(2,128)}, u32[]{:S(2)}) copy-start(f32[2,1280]{1,0:T(2,128)} %refs_5_.6) | copy-start | bytes 30724
  2.1 6.7 %copy-start.3 = (bf16[2,1280,2]{1,2,0:T(2,128)(2,1)S(1)}, bf16[2,1280,2]{1,2,0:T(2,128)(2,1)}, u32[]{:S(2)}) copy-start(bf16[2,1280,2]{1,2,0:T(2,128)(2,1)} %param.17) | copy-start | bytes 30724
  2.1 5.4 %collective-permute-start = (bf16[16,1280]{1,0:T(8,128)(2,1)S(1)}, bf16[16,1280]{1,0:T(8,128)(2,1)S(1)}, u32[]{:S(2)}, u32[]{:S(2)}) collective-permute-start(bf16[16,1280]{1,0:T(8,128)(2,1)S(1)} %get-tuple-element.23.refs_0_), channel_id=1, source_target_pairs={{0,3},{1,2},{2,1},{3,0},{4,7},{5,6},{6,5},{7,4},{8,11},{9,10},{10,... | collective-permute-start | bytes 122888 | tf_op jit(solution)/shard_map/ppermute | solution.py:58
  4.5 4.2 %collective-permute-start.1 = (bf16[16,1280]{1,0:T(8,128)(2,1)S(1)}, bf16[16,1280]{1,0:T(8,128)(2,1)S(1)}, u32[]{:S(2)}, u32[]{:S(2)}) collective-permute-start(bf16[16,1280]{1,0:T(8,128)(2,1)S(1)} %get-tuple-element.23.refs_0_), channel_id=1, source_target_pairs={{0,2},{1,3},{2,0},{3,1},{4,6},{5,7},{6,4},{7,5},{8,10},{9,11},{10,... | collective-permute-start | bytes 122888 | tf_op jit(solution)/shard_map/ppermute | solution.py:58
  5.2 3.5 %collective-permute-start.2 = (bf16[16,1280]{1,0:T(8,128)(2,1)S(1)}, bf16[16,1280]{1,0:T(8,128)(2,1)S(1)}, u32[]{:S(2)}, u32[]{:S(2)}) collective-permute-start(bf16[16,1280]{1,0:T(8,128)(2,1)S(1)} %get-tuple-element.23.refs_0_), channel_id=1, source_target_pairs={{0,1},{1,0},{2,3},{3,2},{4,5},{5,4},{6,7},{7,6},{8,9},{9,8},{10,11... | collective-permute-start | bytes 122888 | tf_op jit(solution)/shard_map/ppermute | solution.py:58
  9.6 7.7 %collective-permute-start.3 = (bf16[16,1536]{1,0:T(8,128)(2,1)S(1)}, bf16[16,1536]{1,0:T(8,128)(2,1)S(1)}, u32[]{:S(2)}, u32[]{:S(2)}) collective-permute-start(bf16[16,1536]{1,0:T(8,128)(2,1)S(1)} %get-tuple-element.26), channel_id=1, source_target_pairs={{0,8},{4,12},{8,0},{12,4},{1,9},{5,13},{9,1},{13,5},{2,10},{6,14},... | collective-permute-start | bytes 147464 | tf_op jit(solution)/shard_map/ppermute | solution.py:58
  12.2 6.0 %collective-permute-start.4 = (bf16[16,1536]{1,0:T(8,128)(2,1)S(1)}, bf16[16,1536]{1,0:T(8,128)(2,1)S(1)}, u32[]{:S(2)}, u32[]{:S(2)}) collective-permute-start(bf16[16,1536]{1,0:T(8,128)(2,1)S(1)} %get-tuple-element.27), channel_id=1, source_target_pairs={{0,12},{4,8},{8,4},{12,0},{1,13},{5,9},{9,5},{13,1},{2,14},{6,10},... | collective-permute-start | bytes 147464 | tf_op jit(solution)/shard_map/ppermute | solution.py:58
  13.6 4.6 %copy-start.4 = (f32[2,2]{1,0:T(2,128)S(1)}, f32[2,2]{1,0:T(2,128)}, u32[]{:S(2)}) copy-start(f32[2,2]{1,0:T(2,128)} %refs_4_.8) | copy-start | bytes 52
  13.6 4.6 %collective-permute-start.5 = (bf16[16,1536]{1,0:T(8,128)(2,1)S(1)}, bf16[16,1536]{1,0:T(8,128)(2,1)S(1)}, u32[]{:S(2)}, u32[]{:S(2)}) collective-permute-start(bf16[16,1536]{1,0:T(8,128)(2,1)S(1)} %get-tuple-element.28), channel_id=1, source_target_pairs={{0,4},{4,0},{8,12},{12,8},{1,5},{5,1},{9,13},{13,9},{2,6},{6,2},{1... | collective-permute-start | bytes 147464 | tf_op jit(solution)/shard_map/ppermute | solution.py:58
  21.6 7.8 %slice-start.2 = ((s8[6553600]{0:T(1024)(128)(4,1)}), s8[4194304]{0:T(1024)(128)(4,1)S(1)}, s32[]{:S(2)}) async-start(s8[6553600]{0:T(1024)(128)(4,1)} %bitcast.3), calls=%async_computation.2 | async-start | bytes 8388608
  21.6 7.8 %slice-start.3 = ((s8[6553600]{0:T(1024)(128)(4,1)}), s8[2359296]{0:T(1024)(128)(4,1)S(1)}, s32[]{:S(2)}) async-start(s8[6553600]{0:T(1024)(128)(4,1)} %bitcast.3), calls=%async_computation.3 | async-start | bytes 4718592
  21.6 7.8 %copy-start.5 = (f32[2,128]{1,0:T(2,128)S(1)}, f32[2,128]{1,0:T(2,128)}, u32[]{:S(2)}) copy-start(f32[2,128]{1,0:T(2,128)} %refs_4_.9) | copy-start | bytes 3076
  21.6 6.1 %collective-permute-start.6 = (bf16[16,1280]{1,0:T(8,128)(2,1)S(1)}, bf16[16,1280]{1,0:T(8,128)(2,1)S(1)}, u32[]{:S(2)}, u32[]{:S(2)}) collective-permute-start(bf16[16,1280]{1,0:T(8,128)(2,1)S(1)} %get-tuple-element.33), channel_id=1, source_target_pairs={{0,8},{4,12},{8,0},{12,4},{1,9},{5,13},{9,1},{13,5},{2,10},{6,14},... | collective-permute-start | bytes 122888 | tf_op jit(solution)/shard_map/ppermute | solution.py:58
  23.5 5.8 %collective-permute-start.7 = (bf16[16,1280]{1,0:T(8,128)(2,1)S(1)}, bf16[16,1280]{1,0:T(8,128)(2,1)S(1)}, u32[]{:S(2)}, u32[]{:S(2)}) collective-permute-start(bf16[16,1280]{1,0:T(8,128)(2,1)S(1)} %get-tuple-element.33), channel_id=1, source_target_pairs={{0,12},{4,8},{8,4},{12,0},{1,13},{5,9},{9,5},{13,1},{2,14},{6,10},... | collective-permute-start | bytes 122888 | tf_op jit(solution)/shard_map/ppermute | solution.py:58
  24.9 4.5 %collective-permute-start.8 = (bf16[16,1280]{1,0:T(8,128)(2,1)S(1)}, bf16[16,1280]{1,0:T(8,128)(2,1)S(1)}, u32[]{:S(2)}, u32[]{:S(2)}) collective-permute-start(bf16[16,1280]{1,0:T(8,128)(2,1)S(1)} %get-tuple-element.33), channel_id=1, source_target_pairs={{0,4},{4,0},{8,12},{12,8},{1,5},{5,1},{9,13},{13,9},{2,6},{6,2},{1... | collective-permute-start | bytes 122888 | tf_op jit(solution)/shard_map/ppermute | solution.py:58
  30.0 4.1 %collective-permute-start.9 = (bf16[16,1280]{1,0:T(8,128)(2,1)S(1)}, bf16[16,1280]{1,0:T(8,128)(2,1)S(1)}, u32[]{:S(2)}, u32[]{:S(2)}) collective-permute-start(bf16[16,1280]{1,0:T(8,128)(2,1)S(1)} %mix.2.refs_1_), channel_id=1, source_target_pairs={{0,3},{1,2},{2,1},{3,0},{4,7},{5,6},{6,5},{7,4},{8,11},{9,10},{10,... | collective-permute-start | bytes 122888 | tf_op jit(solution)/shard_map/ppermute | solution.py:58
  30.0 4.3 %collective-permute-start.10 = (bf16[16,1280]{1,0:T(8,128)(2,1)S(1)}, bf16[16,1280]{1,0:T(8,128)(2,1)S(1)}, u32[]{:S(2)}, u32[]{:S(2)}) collective-permute-start(bf16[16,1280]{1,0:T(8,128)(2,1)S(1)} %mix.2.refs_1_), channel_id=1, source_target_pairs={{0,2},{1,3},{2,0},{3,1},{4,6},{5,7},{6,4},{7,5},{8,10},{9,11},{10,... | collective-permute-start | bytes 122888 | tf_op jit(solution)/shard_map/ppermute | solution.py:58
  31.3 3.0 %collective-permute-start.11 = (bf16[16,1280]{1,0:T(8,128)(2,1)S(1)}, bf16[16,1280]{1,0:T(8,128)(2,1)S(1)}, u32[]{:S(2)}, u32[]{:S(2)}) collective-permute-start(bf16[16,1280]{1,0:T(8,128)(2,1)S(1)} %mix.2.refs_1_), channel_id=1, source_target_pairs={{0,1},{1,0},{2,3},{3,2},{4,5},{5,4},{6,7},{7,6},{8,9},{9,8},{10,11... | collective-permute-start | bytes 122888 | tf_op jit(solution)/shard_map/ppermute | solution.py:58
  35.1 6.7 %collective-permute-start.12 = (bf16[16,1536]{1,0:T(8,128)(2,1)S(1)}, bf16[16,1536]{1,0:T(8,128)(2,1)S(1)}, u32[]{:S(2)}, u32[]{:S(2)}) collective-permute-start(bf16[16,1536]{1,0:T(8,128)(2,1)S(1)} %get-tuple-element.36), channel_id=1, source_target_pairs={{0,8},{4,12},{8,0},{12,4},{1,9},{5,13},{9,1},{13,5},{2,10},{6,14},... | collective-permute-start | bytes 147464 | tf_op jit(solution)/shard_map/ppermute | solution.py:58
  36.3 6.0 %collective-permute-start.13 = (bf16[16,1536]{1,0:T(8,128)(2,1)S(1)}, bf16[16,1536]{1,0:T(8,128)(2,1)S(1)}, u32[]{:S(2)}, u32[]{:S(2)}) collective-permute-start(bf16[16,1536]{1,0:T(8,128)(2,1)S(1)} %get-tuple-element.37), channel_id=1, source_target_pairs={{0,12},{4,8},{8,4},{12,0},{1,13},{5,9},{9,5},{13,1},{2,14},{6,10},... | collective-permute-start | bytes 147464 | tf_op jit(solution)/shard_map/ppermute | solution.py:58
  37.7 4.9 %collective-permute-start.14 = (bf16[16,1536]{1,0:T(8,128)(2,1)S(1)}, bf16[16,1536]{1,0:T(8,128)(2,1)S(1)}, u32[]{:S(2)}, u32[]{:S(2)}) collective-permute-start(bf16[16,1536]{1,0:T(8,128)(2,1)S(1)} %get-tuple-element.38), channel_id=1, source_target_pairs={{0,4},{4,0},{8,12},{12,8},{1,5},{5,1},{9,13},{13,9},{2,6},{6,2},{1... | collective-permute-start | bytes 147464 | tf_op jit(solution)/shard_map/ppermute | solution.py:58
  45.8 6.2 %collective-permute-start.15 = (bf16[16,1280]{1,0:T(8,128)(2,1)S(1)}, bf16[16,1280]{1,0:T(8,128)(2,1)S(1)}, u32[]{:S(2)}, u32[]{:S(2)}) collective-permute-start(bf16[16,1280]{1,0:T(8,128)(2,1)S(1)} %get-tuple-element.40), channel_id=1, source_target_pairs={{0,8},{4,12},{8,0},{12,4},{1,9},{5,13},{9,1},{13,5},{2,10},{6,14},... | collective-permute-start | bytes 122888 | tf_op jit(solution)/shard_map/ppermute | solution.py:58
  47.4 5.8 %collective-permute-start.16 = (bf16[16,1280]{1,0:T(8,128)(2,1)S(1)}, bf16[16,1280]{1,0:T(8,128)(2,1)S(1)}, u32[]{:S(2)}, u32[]{:S(2)}) collective-permute-start(bf16[16,1280]{1,0:T(8,128)(2,1)S(1)} %get-tuple-element.40), channel_id=1, source_target_pairs={{0,12},{4,8},{8,4},{12,0},{1,13},{5,9},{9,5},{13,1},{2,14},{6,10},... | collective-permute-start | bytes 122888 | tf_op jit(solution)/shard_map/ppermute | solution.py:58
  48.8 4.4 %collective-permute-start.17 = (bf16[16,1280]{1,0:T(8,128)(2,1)S(1)}, bf16[16,1280]{1,0:T(8,128)(2,1)S(1)}, u32[]{:S(2)}, u32[]{:S(2)}) collective-permute-start(bf16[16,1280]{1,0:T(8,128)(2,1)S(1)} %get-tuple-element.40), channel_id=1, source_target_pairs={{0,4},{4,0},{8,12},{12,8},{1,5},{5,1},{9,13},{13,9},{2,6},{6,2},{1... | collective-permute-start | bytes 122888 | tf_op jit(solution)/shard_map/ppermute | solution.py:58
  53.8 3.8 %collective-permute-start.18 = (bf16[16,1280]{1,0:T(8,128)(2,1)S(1)}, bf16[16,1280]{1,0:T(8,128)(2,1)S(1)}, u32[]{:S(2)}, u32[]{:S(2)}) collective-permute-start(bf16[16,1280]{1,0:T(8,128)(2,1)S(1)} %mix.3.refs_1_), channel_id=1, source_target_pairs={{0,3},{1,2},{2,1},{3,0},{4,7},{5,6},{6,5},{7,4},{8,11},{9,10},{10,... | collective-permute-start | bytes 122888 | tf_op jit(solution)/shard_map/ppermute | solution.py:58
  53.8 4.3 %collective-permute-start.19 = (bf16[16,1280]{1,0:T(8,128)(2,1)S(1)}, bf16[16,1280]{1,0:T(8,128)(2,1)S(1)}, u32[]{:S(2)}, u32[]{:S(2)}) collective-permute-start(bf16[16,1280]{1,0:T(8,128)(2,1)S(1)} %mix.3.refs_1_), channel_id=1, source_target_pairs={{0,2},{1,3},{2,0},{3,1},{4,6},{5,7},{6,4},{7,5},{8,10},{9,11},{10,... | collective-permute-start | bytes 122888 | tf_op jit(solution)/shard_map/ppermute | solution.py:58
  55.1 3.0 %collective-permute-start.20 = (bf16[16,1280]{1,0:T(8,128)(2,1)S(1)}, bf16[16,1280]{1,0:T(8,128)(2,1)S(1)}, u32[]{:S(2)}, u32[]{:S(2)}) collective-permute-start(bf16[16,1280]{1,0:T(8,128)(2,1)S(1)} %mix.3.refs_1_), channel_id=1, source_target_pairs={{0,1},{1,0},{2,3},{3,2},{4,5},{5,4},{6,7},{7,6},{8,9},{9,8},{10,11... | collective-permute-start | bytes 122888 | tf_op jit(solution)/shard_map/ppermute | solution.py:58

commit v7 on v6

--- a/solution.py
+++ b/solution.py
@@ -88,8 +88,7 @@
 
 
 def make_selectors(left_ref, right_ref, scale_ref):
-    depth, block_feat = left_ref.shape
-    size = depth // 2
+    size, block_feat = left_ref.shape
 
     def first_of(row):
         return row * size - row * (row - 1) // 2
@@ -103,7 +102,6 @@
     left = jnp.where(first_of(left + 1) <= feature, left + 1, left)
     right = feature - first_of(left) + left
     at = lax.broadcasted_iota(jnp.int32, left_ref.shape, 0)
-    at = jnp.where(at >= size, at - size, at)
     left_ref[...] = jnp.where(at == left, 1.0, 0.0).astype(BF16)
     right_ref[...] = jnp.where(at == right, 1.0, 0.0).astype(BF16)
     scale_ref[...] = jnp.where(left == right, 1.0, math.sqrt(2.0)).astype(F32)
@@ -144,8 +142,8 @@
     table_rows, width = embedding.shape
     requests = token_ids.shape[0]
     picks = [
-        pltpu.VMEM((2 * head_size, block_feat), BF16),
-        pltpu.VMEM((2 * head_size, block_feat), BF16),
+        pltpu.VMEM((head_size, block_feat), BF16),
+        pltpu.VMEM((head_size, block_feat), BF16),
         pltpu.VMEM((1, block_feat), F32),
     ]
     if table_rows % ROWS:
@@ -342,7 +340,7 @@
             else:
                 part = jnp.zeros((requests, head_size), F32)
             rows_ref[pl.ds(head * slots + slot, requests, stride=span), :] = part
-    vectors = jnp.concatenate(split(rows_ref[...]), axis=1)
+    vectors = rows_ref[...].astype(BF16)
 
     step = 2 * LANES
     for start in range(0, block_feat, step):

time: 59.1 us -> 59 us (level)
  no operation moved by 1% of the time
where the time goes in v7:
time: 59 us; the launch traced here: 58.6 us
  Pallas kernels  25.4 us (43%)
  starting transfers between devices  21.8 us (37%)
  waiting for transfers between devices  11.1 us (19%)
    ppermute x21, starting transfers between devices, exchange(): lax.ppermute(wire, axis, [(rank, rank ^ step) for rank in range(size)])  21.8 us
    pallas_call x5, Pallas kernels, fetch(): pl.pallas_call(functools.partial(fetch_kernel, plan, len(sources)), out_s...  13.4 us
    ppermute x21, waiting for transfers between devices, exchange(): lax.ppermute(wire, axis, [(rank, rank ^ step) for rank in range(size)])  11.1 us
    pallas_call x2, Pallas kernels, read(): pl.pallas_call(functools.partial(read_kernel, layer, sizes, len(terms), c...  6.47 us
    pallas_call x1, Pallas kernels, pick_rows(): pl.pallas_call(pick_kernel, out_shape=[jax.ShapeDtypeStruct((requests, wi...  1.97 us
    pallas_call x2, Pallas kernels, project(): pl.pallas_call(functools.partial(project_kernel, layer, len(terms), len(c...  1.65 us
    pallas_call x2, Pallas kernels, mix(): pl.pallas_call(functools.partial(mix_kernel, layer, len(terms), len(held)...  1.24 us
  transfers between devices with their start and end apart: 21, of which 10 were waited for; matrix products, arithmetic and copies ran while one was open for 0% of the time, Pallas kernels for 23%

profile of v7, /device:TPU:0, one launch (start us, length us, event | category | flops | bytes accessed | tf_op | source)
XLA Modules:
  0.0 58.6 jit_solution(9554131895643171450)
XLA Ops:
  0.0 2.0 %pick_rows.1 = (bf16[16,1280]{1,0:T(8,128)(2,1)S(1)}, bf16[128,2064]{1,0:T(8,128)(2,1)S(1)}, bf16[128,2064]{1,0:T(8,128)(2,1)S(1)}, f32[1,2064]{1,0:T(1,128)S(1)}) custom-call(s32[16]{0:T(128)} %ids_ref.1, bf16[18992,1280]{1,0:T(8,128)(2,1)} %table_ref.1), custom_call_target="tpu_custom_call" | custom-call | tf_op jit(solution)/shard_map/pick_rows/pallas_call | solution.py:161
  2.0 0.0 slice-start
  2.0 0.0 copy-start
  2.0 0.0 copy-start.1
  2.0 0.0 copy-start.2
  2.0 2.4 %collective-permute-start = (bf16[16,1280]{1,0:T(8,128)(2,1)S(1)}, bf16[16,1280]{1,0:T(8,128)(2,1)S(1)}, u32[]{:S(2)}, u32[]{:S(2)}) collective-permute-start(bf16[16,1280]{1,0:T(8,128)(2,1)S(1)} %get-tuple-element.23.refs_0_), channel_id=1, source_target_pairs={{0,3},{1,2},{2,1},{3,0},{4,7},{5,6},{6,5},{7,4},{8,11},{9,10},{10,... | collective-permute-start | bytes 122888 | tf_op jit(solution)/shard_map/ppermute | solution.py:58
  4.4 0.7 %collective-permute-start.1 = (bf16[16,1280]{1,0:T(8,128)(2,1)S(1)}, bf16[16,1280]{1,0:T(8,128)(2,1)S(1)}, u32[]{:S(2)}, u32[]{:S(2)}) collective-permute-start(bf16[16,1280]{1,0:T(8,128)(2,1)S(1)} %get-tuple-element.23.refs_0_), channel_id=1, source_target_pairs={{0,2},{1,3},{2,0},{3,1},{4,6},{5,7},{6,4},{7,5},{8,10},{9,11},{10,... | collective-permute-start | bytes 122888 | tf_op jit(solution)/shard_map/ppermute | solution.py:58
  5.1 0.0 collective-permute-start.2
  5.2 2.2 %fetch.5.refs_9_.refs_8_ = bf16[4,2,2064,128]{3,2,1,0:T(8,128)(2,1)S(1)} custom-call(bf16[2,16,2,2064,128]{4,3,2,1,0:T(8,128)(2,1)} %refs_0_.9), custom_call_target="tpu_custom_call" | custom-call | tf_op jit(solution)/shard_map/fetch/pallas_call | solution.py:199
  7.4 1.2 %collective-permute-done.1.refs_2_ = bf16[16,1280]{1,0:T(8,128)(2,1)S(1)} collective-permute-done((bf16[16,1280]{1,0:T(8,128)(2,1)S(1)}, bf16[16,1280]{1,0:T(8,128)(2,1)S(1)}, u32[]{:S(2)}, u32[]{:S(2)}) %collective-permute-start.1) | collective-permute-done | bytes 40992 | tf_op jit(solution)/shard_map/ppermute | solution.py:58
  8.7 0.8 %project.2 = (bf16[16,1280]{1,0:T(8,128)(2,1)S(1)}, f32[16,1920]{1,0:T(8,128)S(1)}, bf16[16,1536]{1,0:T(8,128)(2,1)S(1)}, bf16[16,1536]{1,0:T(8,128)(2,1)S(1)}, bf16[16,1536]{1,0:T(8,128)(2,1)S(1)}) custom-call(bf16[16,1280]{1,0:T(8,128)(2,1)S(1)} %get-tuple-element.23.refs_0_, bf16[16,1280]{1,0:T(8,128)(2,1)S(1)} %collective-permute-done.refs_1_, ...), custom_call_target="tpu_custom_call" | custom-call | tf_op jit(solution)/shard_map/project/pallas_call | solution.py:271
  9.5 2.7 %collective-permute-start.3 = (bf16[16,1536]{1,0:T(8,128)(2,1)S(1)}, bf16[16,1536]{1,0:T(8,128)(2,1)S(1)}, u32[]{:S(2)}, u32[]{:S(2)}) collective-permute-start(bf16[16,1536]{1,0:T(8,128)(2,1)S(1)} %get-tuple-element.26), channel_id=1, source_target_pairs={{0,8},{4,12},{8,0},{12,4},{1,9},{5,13},{9,1},{13,5},{2,10},{6,14},... | collective-permute-start | bytes 147464 | tf_op jit(solution)/shard_map/ppermute | solution.py:58
  12.2 1.3 %collective-permute-start.4 = (bf16[16,1536]{1,0:T(8,128)(2,1)S(1)}, bf16[16,1536]{1,0:T(8,128)(2,1)S(1)}, u32[]{:S(2)}, u32[]{:S(2)}) collective-permute-start(bf16[16,1536]{1,0:T(8,128)(2,1)S(1)} %get-tuple-element.27), channel_id=1, source_target_pairs={{0,12},{4,8},{8,4},{12,0},{1,13},{5,9},{9,5},{13,1},{2,14},{6,10},... | collective-permute-start | bytes 147464 | tf_op jit(solution)/shard_map/ppermute | solution.py:58
  13.5 0.2 collective-permute-start.5
  13.8 3.4 %fetch.6.refs_9_ = bf16[8,2,2064,128]{3,2,1,0:T(8,128)(2,1)S(1)} custom-call(bf16[2,16,2,2064,128]{4,3,2,1,0:T(8,128)(2,1)} %refs_0_.9), custom_call_target="tpu_custom_call" | custom-call | tf_op jit(solution)/shard_map/fetch/pallas_call | solution.py:199
  17.2 1.0 %collective-permute-done.4.refs_2_ = bf16[16,1536]{1,0:T(8,128)(2,1)S(1)} collective-permute-done((bf16[16,1536]{1,0:T(8,128)(2,1)S(1)}, bf16[16,1536]{1,0:T(8,128)(2,1)S(1)}, u32[]{:S(2)}, u32[]{:S(2)}) %collective-permute-start.4) | collective-permute-done | bytes 49184 | tf_op jit(solution)/shard_map/ppermute | solution.py:58
  18.2 3.3 %read.2 = (f32[16,1280]{1,0:T(8,128)S(1)}, bf16[16,1280]{1,0:T(8,128)(2,1)S(1)}) custom-call(f32[16,1920]{1,0:T(8,128)S(1)} %get-tuple-element.25.refs_0_, bf16[16,1536]{1,0:T(8,128)(2,1)S(1)} %collective-permute-done.3.refs_1_, bf16[16,1536]{1,0:T(8,128)(2,1)S(1)} %collective-permute-done.4.refs_2_, bf16[16,1536]{1,0:T(8,128)(2,1)S(1)} %collective-permute-done.5.refs_3_, ...), custom_call_target="tpu_custom_call" | custom-call | tf_op jit(solution)/shard_map/read/pallas_call | solution.py:400
  21.5 0.0 slice-start.2
  21.5 0.0 copy-start.5
  21.5 1.9 %collective-permute-start.6 = (bf16[16,1280]{1,0:T(8,128)(2,1)S(1)}, bf16[16,1280]{1,0:T(8,128)(2,1)S(1)}, u32[]{:S(2)}, u32[]{:S(2)}) collective-permute-start(bf16[16,1280]{1,0:T(8,128)(2,1)S(1)} %get-tuple-element.33), channel_id=1, source_target_pairs={{0,8},{4,12},{8,0},{12,4},{1,9},{5,13},{9,1},{13,5},{2,10},{6,14},... | collective-permute-start | bytes 122888 | tf_op jit(solution)/shard_map/ppermute | solution.py:58
  23.5 1.3 %collective-permute-start.7 = (bf16[16,1280]{1,0:T(8,128)(2,1)S(1)}, bf16[16,1280]{1,0:T(8,128)(2,1)S(1)}, u32[]{:S(2)}, u32[]{:S(2)}) collective-permute-start(bf16[16,1280]{1,0:T(8,128)(2,1)S(1)} %get-tuple-element.33), channel_id=1, source_target_pairs={{0,12},{4,8},{8,4},{12,0},{1,13},{5,9},{9,5},{13,1},{2,14},{6,10},... | collective-permute-start | bytes 122888 | tf_op jit(solution)/shard_map/ppermute | solution.py:58
  24.8 0.3 collective-permute-start.8
  25.1 2.5 %fetch.7.refs_6_.refs_10_.refs_8_ = bf16[5,2,2064,128]{3,2,1,0:T(8,128)(2,1)S(1)} custom-call(bf16[2,16,2,2064,128]{4,3,2,1,0:T(8,128)(2,1)} %refs_0_.9), custom_call_target="tpu_custom_call" | custom-call | tf_op jit(solution)/shard_map/fetch/pallas_call | solution.py:199
  27.6 1.7 %collective-permute-done.7.refs_2_ = bf16[16,1280]{1,0:T(8,128)(2,1)S(1)} collective-permute-done((bf16[16,1280]{1,0:T(8,128)(2,1)S(1)}, bf16[16,1280]{1,0:T(8,128)(2,1)S(1)}, u32[]{:S(2)}, u32[]{:S(2)}) %collective-permute-start.7) | collective-permute-done | bytes 40992 | tf_op jit(solution)/shard_map/ppermute | solution.py:58
  29.3 0.6 %mix.2.refs_1_ = bf16[16,1280]{1,0:T(8,128)(2,1)S(1)} custom-call(f32[16,1280]{1,0:T(8,128)S(1)} %get-tuple-element.32.refs_0_, bf16[16,1280]{1,0:T(8,128)(2,1)S(1)} %collective-permute-done.6.refs_1_, bf16[16,1280]{1,0:T(8,128)(2,1)S(1)} %collective-permute-done.7.refs_2_, bf16[16,1280]{1,0:T(8,128)(2,1)S(1)} %collective-permute-done.8.refs_3_, ...), custom_call_target="tpu_custom_call" | custom-call | tf_op jit(solution)/shard_map/mix/pallas_call | solution.py:442
  29.9 1.3 %collective-permute-start.10 = (bf16[16,1280]{1,0:T(8,128)(2,1)S(1)}, bf16[16,1280]{1,0:T(8,128)(2,1)S(1)}, u32[]{:S(2)}, u32[]{:S(2)}) collective-permute-start(bf16[16,1280]{1,0:T(8,128)(2,1)S(1)} %mix.2.refs_1_), channel_id=1, source_target_pairs={{0,2},{1,3},{2,0},{3,1},{4,6},{5,7},{6,4},{7,5},{8,10},{9,11},{10,... | collective-permute-start | bytes 122888 | tf_op jit(solution)/shard_map/ppermute | solution.py:58
  31.2 0.6 collective-permute-start.11
  31.8 2.2 %fetch.8.refs_11_.refs_9_ = bf16[4,2,2064,128]{3,2,1,0:T(8,128)(2,1)S(1)} custom-call(bf16[2,16,2,2064,128]{4,3,2,1,0:T(8,128)(2,1)} %refs_0_.9), custom_call_target="tpu_custom_call" | custom-call | tf_op jit(solution)/shard_map/fetch/pallas_call | solution.py:199
  34.0 0.2 collective-permute-done.10.refs_3_
  34.2 0.8 %project.3 = (bf16[16,1280]{1,0:T(8,128)(2,1)S(1)}, f32[16,1920]{1,0:T(8,128)S(1)}, bf16[16,1536]{1,0:T(8,128)(2,1)S(1)}, bf16[16,1536]{1,0:T(8,128)(2,1)S(1)}, bf16[16,1536]{1,0:T(8,128)(2,1)S(1)}) custom-call(bf16[16,1280]{1,0:T(8,128)(2,1)S(1)} %get-tuple-element.24.refs_0_, bf16[16,1280]{1,0:T(8,128)(2,1)S(1)} %mix.2.refs_1_, ...), custom_call_target="tpu_custom_call" | custom-call | tf_op jit(solution)/shard_map/project/pallas_call | solution.py:271
  35.0 1.2 %collective-permute-start.12 = (bf16[16,1536]{1,0:T(8,128)(2,1)S(1)}, bf16[16,1536]{1,0:T(8,128)(2,1)S(1)}, u32[]{:S(2)}, u32[]{:S(2)}) collective-permute-start(bf16[16,1536]{1,0:T(8,128)(2,1)S(1)} %get-tuple-element.36), channel_id=1, source_target_pairs={{0,8},{4,12},{8,0},{12,4},{1,9},{5,13},{9,1},{13,5},{2,10},{6,14},... | collective-permute-start | bytes 147464 | tf_op jit(solution)/shard_map/ppermute | solution.py:58
  36.2 1.3 %collective-permute-start.13 = (bf16[16,1536]{1,0:T(8,128)(2,1)S(1)}, bf16[16,1536]{1,0:T(8,128)(2,1)S(1)}, u32[]{:S(2)}, u32[]{:S(2)}) collective-permute-start(bf16[16,1536]{1,0:T(8,128)(2,1)S(1)} %get-tuple-element.37), channel_id=1, source_target_pairs={{0,12},{4,8},{8,4},{12,0},{1,13},{5,9},{9,5},{13,1},{2,14},{6,10},... | collective-permute-start | bytes 147464 | tf_op jit(solution)/shard_map/ppermute | solution.py:58
  37.6 1.0 %collective-permute-start.14 = (bf16[16,1536]{1,0:T(8,128)(2,1)S(1)}, bf16[16,1536]{1,0:T(8,128)(2,1)S(1)}, u32[]{:S(2)}, u32[]{:S(2)}) collective-permute-start(bf16[16,1536]{1,0:T(8,128)(2,1)S(1)} %get-tuple-element.38), channel_id=1, source_target_pairs={{0,4},{4,0},{8,12},{12,8},{1,5},{5,1},{9,13},{13,9},{2,6},{6,2},{1... | collective-permute-start | bytes 147464 | tf_op jit(solution)/shard_map/ppermute | solution.py:58
  38.6 3.1 %fetch.9.refs_10_ = bf16[7,2,2064,128]{3,2,1,0:T(8,128)(2,1)S(1)} custom-call(bf16[2,16,2,2064,128]{4,3,2,1,0:T(8,128)(2,1)} %refs_0_.9), custom_call_target="tpu_custom_call" | custom-call | tf_op jit(solution)/shard_map/fetch/pallas_call | solution.py:199
  41.7 0.6 collective-permute-done.13.refs_2_
  42.3 0.2 collective-permute-done.14.refs_3_
  42.5 3.2 %read.3 = (f32[16,1280]{1,0:T(8,128)S(1)}, bf16[16,1280]{1,0:T(8,128)(2,1)S(1)}) custom-call(f32[16,1920]{1,0:T(8,128)S(1)} %get-tuple-element.35.refs_0_, bf16[16,1536]{1,0:T(8,128)(2,1)S(1)} %collective-permute-done.12.refs_1_, bf16[16,1536]{1,0:T(8,128)(2,1)S(1)} %collective-permute-done.13.refs_2_, bf16[16,1536]{1,0:T(8,128)(2,1)S(1)} %collective-permute-done.14.refs_3_, ...), custom_call_target="tpu_custom_call" | custom-call | tf_op jit(solution)/shard_map/read/pallas_call | solution.py:400
  45.6 1.6 %collective-permute-start.15 = (bf16[16,1280]{1,0:T(8,128)(2,1)S(1)}, bf16[16,1280]{1,0:T(8,128)(2,1)S(1)}, u32[]{:S(2)}, u32[]{:S(2)}) collective-permute-start(bf16[16,1280]{1,0:T(8,128)(2,1)S(1)} %get-tuple-element.40), channel_id=1, source_target_pairs={{0,8},{4,12},{8,0},{12,4},{1,9},{5,13},{9,1},{13,5},{2,10},{6,14},... | collective-permute-start | bytes 122888 | tf_op jit(solution)/shard_map/ppermute | solution.py:58
  47.3 1.4 %collective-permute-start.16 = (bf16[16,1280]{1,0:T(8,128)(2,1)S(1)}, bf16[16,1280]{1,0:T(8,128)(2,1)S(1)}, u32[]{:S(2)}, u32[]{:S(2)}) collective-permute-start(bf16[16,1280]{1,0:T(8,128)(2,1)S(1)} %get-tuple-element.40), channel_id=1, source_target_pairs={{0,12},{4,8},{8,4},{12,0},{1,13},{5,9},{9,5},{13,1},{2,14},{6,10},... | collective-permute-start | bytes 122888 | tf_op jit(solution)/shard_map/ppermute | solution.py:58
  48.6 0.6 collective-permute-start.17
  49.2 2.7 %collective-permute-done.15.refs_1_ = bf16[16,1280]{1,0:T(8,128)(2,1)S(1)} collective-permute-done((bf16[16,1280]{1,0:T(8,128)(2,1)S(1)}, bf16[16,1280]{1,0:T(8,128)(2,1)S(1)}, u32[]{:S(2)}, u32[]{:S(2)}) %collective-permute-start.15) | collective-permute-done | bytes 40992 | tf_op jit(solution)/shard_map/ppermute | solution.py:58
  51.9 1.2 %collective-permute-done.16.refs_2_ = bf16[16,1280]{1,0:T(8,128)(2,1)S(1)} collective-permute-done((bf16[16,1280]{1,0:T(8,128)(2,1)S(1)}, bf16[16,1280]{1,0:T(8,128)(2,1)S(1)}, u32[]{:S(2)}, u32[]{:S(2)}) %collective-permute-start.16) | collective-permute-done | bytes 40992 | tf_op jit(solution)/shard_map/ppermute | solution.py:58
  53.1 0.6 %mix.3.refs_1_ = bf16[16,1280]{1,0:T(8,128)(2,1)S(1)} custom-call(f32[16,1280]{1,0:T(8,128)S(1)} %get-tuple-element.39.refs_0_, bf16[16,1280]{1,0:T(8,128)(2,1)S(1)} %collective-permute-done.15.refs_1_, bf16[16,1280]{1,0:T(8,128)(2,1)S(1)} %collective-permute-done.16.refs_2_, bf16[16,1280]{1,0:T(8,128)(2,1)S(1)} %collective-permute-done.17.refs_3_, ...), custom_call_target="tpu_custom_call" | custom-call | tf_op jit(solution)/shard_map/mix/pallas_call | solution.py:442
  53.7 1.3 %collective-permute-start.19 = (bf16[16,1280]{1,0:T(8,128)(2,1)S(1)}, bf16[16,1280]{1,0:T(8,128)(2,1)S(1)}, u32[]{:S(2)}, u32[]{:S(2)}) collective-permute-start(bf16[16,1280]{1,0:T(8,128)(2,1)S(1)} %mix.3.refs_1_), channel_id=1, source_target_pairs={{0,2},{1,3},{2,0},{3,1},{4,6},{5,7},{6,4},{7,5},{8,10},{9,11},{10,... | collective-permute-start | bytes 122888 | tf_op jit(solution)/shard_map/ppermute | solution.py:58
  55.0 0.6 collective-permute-start.20
  55.6 1.9 %collective-permute-done.18.refs_2_ = bf16[16,1280]{1,0:T(8,128)(2,1)S(1)} collective-permute-done((bf16[16,1280]{1,0:T(8,128)(2,1)S(1)}, bf16[16,1280]{1,0:T(8,128)(2,1)S(1)}, u32[]{:S(2)}, u32[]{:S(2)}) %collective-permute-start.18) | collective-permute-done | bytes 40992 | tf_op jit(solution)/shard_map/ppermute | solution.py:58
  57.5 0.5 collective-permute-done.19.refs_3_
  58.0 0.7 %finish.1 = bf16[16,1280]{1,0:T(8,128)(2,1)} custom-call(bf16[16,1280]{1,0:T(8,128)(2,1)S(1)} %get-tuple-element.34.refs_0_, bf16[16,1280]{1,0:T(8,128)(2,1)S(1)} %mix.3.refs_1_, bf16[16,1280]{1,0:T(8,128)(2,1)S(1)} %collective-permute-done.18.refs_2_, bf16[16,1280]{1,0:T(8,128)(2,1)S(1)} %collective-permute-done.19.refs_3_, ...), custom_call_target="tpu_custom_call" | custom-call | tf_op jit(solution)/shard_map/finish/pallas_call | solution.py:459
  (29 shorter events, 0.1 us)
Async XLA Ops:
  2.0 6.7 %slice-start = ((s8[6553600]{0:T(1024)(128)(4,1)}), s8[4194304]{0:T(1024)(128)(4,1)S(1)}, s32[]{:S(2)}) async-start(s8[6553600]{0:T(1024)(128)(4,1)} %bitcast.1), calls=%async_computation | async-start | bytes 8388608
  2.0 6.7 %slice-start.1 = ((s8[6553600]{0:T(1024)(128)(4,1)}), s8[2359296]{0:T(1024)(128)(4,1)S(1)}, s32[]{:S(2)}) async-start(s8[6553600]{0:T(1024)(128)(4,1)} %bitcast.1), calls=%async_computation.1 | async-start | bytes 4718592
  2.0 6.7 %copy-start = (bf16[2,1280,256]{2,1,0:T(8,128)(2,1)S(1)}, bf16[2,1280,256]{2,1,0:T(8,128)(2,1)}, u32[]{:S(2)}) copy-start(bf16[2,1280,256]{2,1,0:T(8,128)(2,1)} %refs_7_.3) | copy-start | bytes 3932164
  2.0 6.7 %copy-start.1 = (bf16[2,1280,256]{2,1,0:T(8,128)(2,1)S(1)}, bf16[2,1280,256]{2,1,0:T(8,128)(2,1)}, u32[]{:S(2)}) copy-start(bf16[2,1280,256]{2,1,0:T(8,128)(2,1)} %refs_8_.1) | copy-start | bytes 3932164
  2.0 6.7 %copy-start.2 = (f32[2,1280]{1,0:T(2,128)S(1)}, f32[2,1280]{1,0:T(2,128)}, u32[]{:S(2)}) copy-start(f32[2,1280]{1,0:T(2,128)} %refs_5_.6) | copy-start | bytes 30724
  2.0 6.7 %copy-start.3 = (bf16[2,1280,2]{1,2,0:T(2,128)(2,1)S(1)}, bf16[2,1280,2]{1,2,0:T(2,128)(2,1)}, u32[]{:S(2)}) copy-start(bf16[2,1280,2]{1,2,0:T(2,128)(2,1)} %param.17) | copy-start | bytes 30724
  2.0 5.3 %collective-permute-start = (bf16[16,1280]{1,0:T(8,128)(2,1)S(1)}, bf16[16,1280]{1,0:T(8,128)(2,1)S(1)}, u32[]{:S(2)}, u32[]{:S(2)}) collective-permute-start(bf16[16,1280]{1,0:T(8,128)(2,1)S(1)} %get-tuple-element.23.refs_0_), channel_id=1, source_target_pairs={{0,3},{1,2},{2,1},{3,0},{4,7},{5,6},{6,5},{7,4},{8,11},{9,10},{10,... | collective-permute-start | bytes 122888 | tf_op jit(solution)/shard_map/ppermute | solution.py:58
  4.4 4.2 %collective-permute-start.1 = (bf16[16,1280]{1,0:T(8,128)(2,1)S(1)}, bf16[16,1280]{1,0:T(8,128)(2,1)S(1)}, u32[]{:S(2)}, u32[]{:S(2)}) collective-permute-start(bf16[16,1280]{1,0:T(8,128)(2,1)S(1)} %get-tuple-element.23.refs_0_), channel_id=1, source_target_pairs={{0,2},{1,3},{2,0},{3,1},{4,6},{5,7},{6,4},{7,5},{8,10},{9,11},{10,... | collective-permute-start | bytes 122888 | tf_op jit(solution)/shard_map/ppermute | solution.py:58
  5.1 3.5 %collective-permute-start.2 = (bf16[16,1280]{1,0:T(8,128)(2,1)S(1)}, bf16[16,1280]{1,0:T(8,128)(2,1)S(1)}, u32[]{:S(2)}, u32[]{:S(2)}) collective-permute-start(bf16[16,1280]{1,0:T(8,128)(2,1)S(1)} %get-tuple-element.23.refs_0_), channel_id=1, source_target_pairs={{0,1},{1,0},{2,3},{3,2},{4,5},{5,4},{6,7},{7,6},{8,9},{9,8},{10,11... | collective-permute-start | bytes 122888 | tf_op jit(solution)/shard_map/ppermute | solution.py:58
  9.5 7.7 %collective-permute-start.3 = (bf16[16,1536]{1,0:T(8,128)(2,1)S(1)}, bf16[16,1536]{1,0:T(8,128)(2,1)S(1)}, u32[]{:S(2)}, u32[]{:S(2)}) collective-permute-start(bf16[16,1536]{1,0:T(8,128)(2,1)S(1)} %get-tuple-element.26), channel_id=1, source_target_pairs={{0,8},{4,12},{8,0},{12,4},{1,9},{5,13},{9,1},{13,5},{2,10},{6,14},... | collective-permute-start | bytes 147464 | tf_op jit(solution)/shard_map/ppermute | solution.py:58
  12.2 6.0 %collective-permute-start.4 = (bf16[16,1536]{1,0:T(8,128)(2,1)S(1)}, bf16[16,1536]{1,0:T(8,128)(2,1)S(1)}, u32[]{:S(2)}, u32[]{:S(2)}) collective-permute-start(bf16[16,1536]{1,0:T(8,128)(2,1)S(1)} %get-tuple-element.27), channel_id=1, source_target_pairs={{0,12},{4,8},{8,4},{12,0},{1,13},{5,9},{9,5},{13,1},{2,14},{6,10},... | collective-permute-start | bytes 147464 | tf_op jit(solution)/shard_map/ppermute | solution.py:58
  13.5 4.6 %copy-start.4 = (f32[2,2]{1,0:T(2,128)S(1)}, f32[2,2]{1,0:T(2,128)}, u32[]{:S(2)}) copy-start(f32[2,2]{1,0:T(2,128)} %refs_4_.8) | copy-start | bytes 52
  13.5 4.6 %collective-permute-start.5 = (bf16[16,1536]{1,0:T(8,128)(2,1)S(1)}, bf16[16,1536]{1,0:T(8,128)(2,1)S(1)}, u32[]{:S(2)}, u32[]{:S(2)}) collective-permute-start(bf16[16,1536]{1,0:T(8,128)(2,1)S(1)} %get-tuple-element.28), channel_id=1, source_target_pairs={{0,4},{4,0},{8,12},{12,8},{1,5},{5,1},{9,13},{13,9},{2,6},{6,2},{1... | collective-permute-start | bytes 147464 | tf_op jit(solution)/shard_map/ppermute | solution.py:58
  21.5 7.8 %slice-start.2 = ((s8[6553600]{0:T(1024)(128)(4,1)}), s8[4194304]{0:T(1024)(128)(4,1)S(1)}, s32[]{:S(2)}) async-start(s8[6553600]{0:T(1024)(128)(4,1)} %bitcast.3), calls=%async_computation.2 | async-start | bytes 8388608
  21.5 7.8 %slice-start.3 = ((s8[6553600]{0:T(1024)(128)(4,1)}), s8[2359296]{0:T(1024)(128)(4,1)S(1)}, s32[]{:S(2)}) async-start(s8[6553600]{0:T(1024)(128)(4,1)} %bitcast.3), calls=%async_computation.3 | async-start | bytes 4718592
  21.5 7.8 %copy-start.5 = (f32[2,128]{1,0:T(2,128)S(1)}, f32[2,128]{1,0:T(2,128)}, u32[]{:S(2)}) copy-start(f32[2,128]{1,0:T(2,128)} %refs_4_.9) | copy-start | bytes 3076
  21.5 6.1 %collective-permute-start.6 = (bf16[16,1280]{1,0:T(8,128)(2,1)S(1)}, bf16[16,1280]{1,0:T(8,128)(2,1)S(1)}, u32[]{:S(2)}, u32[]{:S(2)}) collective-permute-start(bf16[16,1280]{1,0:T(8,128)(2,1)S(1)} %get-tuple-element.33), channel_id=1, source_target_pairs={{0,8},{4,12},{8,0},{12,4},{1,9},{5,13},{9,1},{13,5},{2,10},{6,14},... | collective-permute-start | bytes 122888 | tf_op jit(solution)/shard_map/ppermute | solution.py:58
  23.5 5.8 %collective-permute-start.7 = (bf16[16,1280]{1,0:T(8,128)(2,1)S(1)}, bf16[16,1280]{1,0:T(8,128)(2,1)S(1)}, u32[]{:S(2)}, u32[]{:S(2)}) collective-permute-start(bf16[16,1280]{1,0:T(8,128)(2,1)S(1)} %get-tuple-element.33), channel_id=1, source_target_pairs={{0,12},{4,8},{8,4},{12,0},{1,13},{5,9},{9,5},{13,1},{2,14},{6,10},... | collective-permute-start | bytes 122888 | tf_op jit(solution)/shard_map/ppermute | solution.py:58
  24.8 4.5 %collective-permute-start.8 = (bf16[16,1280]{1,0:T(8,128)(2,1)S(1)}, bf16[16,1280]{1,0:T(8,128)(2,1)S(1)}, u32[]{:S(2)}, u32[]{:S(2)}) collective-permute-start(bf16[16,1280]{1,0:T(8,128)(2,1)S(1)} %get-tuple-element.33), channel_id=1, source_target_pairs={{0,4},{4,0},{8,12},{12,8},{1,5},{5,1},{9,13},{13,9},{2,6},{6,2},{1... | collective-permute-start | bytes 122888 | tf_op jit(solution)/shard_map/ppermute | solution.py:58
  29.9 4.1 %collective-permute-start.9 = (bf16[16,1280]{1,0:T(8,128)(2,1)S(1)}, bf16[16,1280]{1,0:T(8,128)(2,1)S(1)}, u32[]{:S(2)}, u32[]{:S(2)}) collective-permute-start(bf16[16,1280]{1,0:T(8,128)(2,1)S(1)} %mix.2.refs_1_), channel_id=1, source_target_pairs={{0,3},{1,2},{2,1},{3,0},{4,7},{5,6},{6,5},{7,4},{8,11},{9,10},{10,... | collective-permute-start | bytes 122888 | tf_op jit(solution)/shard_map/ppermute | solution.py:58
  29.9 4.3 %collective-permute-start.10 = (bf16[16,1280]{1,0:T(8,128)(2,1)S(1)}, bf16[16,1280]{1,0:T(8,128)(2,1)S(1)}, u32[]{:S(2)}, u32[]{:S(2)}) collective-permute-start(bf16[16,1280]{1,0:T(8,128)(2,1)S(1)} %mix.2.refs_1_), channel_id=1, source_target_pairs={{0,2},{1,3},{2,0},{3,1},{4,6},{5,7},{6,4},{7,5},{8,10},{9,11},{10,... | collective-permute-start | bytes 122888 | tf_op jit(solution)/shard_map/ppermute | solution.py:58
  31.2 3.0 %collective-permute-start.11 = (bf16[16,1280]{1,0:T(8,128)(2,1)S(1)}, bf16[16,1280]{1,0:T(8,128)(2,1)S(1)}, u32[]{:S(2)}, u32[]{:S(2)}) collective-permute-start(bf16[16,1280]{1,0:T(8,128)(2,1)S(1)} %mix.2.refs_1_), channel_id=1, source_target_pairs={{0,1},{1,0},{2,3},{3,2},{4,5},{5,4},{6,7},{7,6},{8,9},{9,8},{10,11... | collective-permute-start | bytes 122888 | tf_op jit(solution)/shard_map/ppermute | solution.py:58
  35.0 6.7 %collective-permute-start.12 = (bf16[16,1536]{1,0:T(8,128)(2,1)S(1)}, bf16[16,1536]{1,0:T(8,128)(2,1)S(1)}, u32[]{:S(2)}, u32[]{:S(2)}) collective-permute-start(bf16[16,1536]{1,0:T(8,128)(2,1)S(1)} %get-tuple-element.36), channel_id=1, source_target_pairs={{0,8},{4,12},{8,0},{12,4},{1,9},{5,13},{9,1},{13,5},{2,10},{6,14},... | collective-permute-start | bytes 147464 | tf_op jit(solution)/shard_map/ppermute | solution.py:58
  36.2 6.0 %collective-permute-start.13 = (bf16[16,1536]{1,0:T(8,128)(2,1)S(1)}, bf16[16,1536]{1,0:T(8,128)(2,1)S(1)}, u32[]{:S(2)}, u32[]{:S(2)}) collective-permute-start(bf16[16,1536]{1,0:T(8,128)(2,1)S(1)} %get-tuple-element.37), channel_id=1, source_target_pairs={{0,12},{4,8},{8,4},{12,0},{1,13},{5,9},{9,5},{13,1},{2,14},{6,10},... | collective-permute-start | bytes 147464 | tf_op jit(solution)/shard_map/ppermute | solution.py:58
  37.6 4.9 %collective-permute-start.14 = (bf16[16,1536]{1,0:T(8,128)(2,1)S(1)}, bf16[16,1536]{1,0:T(8,128)(2,1)S(1)}, u32[]{:S(2)}, u32[]{:S(2)}) collective-permute-start(bf16[16,1536]{1,0:T(8,128)(2,1)S(1)} %get-tuple-element.38), channel_id=1, source_target_pairs={{0,4},{4,0},{8,12},{12,8},{1,5},{5,1},{9,13},{13,9},{2,6},{6,2},{1... | collective-permute-start | bytes 147464 | tf_op jit(solution)/shard_map/ppermute | solution.py:58
  45.6 6.2 %collective-permute-start.15 = (bf16[16,1280]{1,0:T(8,128)(2,1)S(1)}, bf16[16,1280]{1,0:T(8,128)(2,1)S(1)}, u32[]{:S(2)}, u32[]{:S(2)}) collective-permute-start(bf16[16,1280]{1,0:T(8,128)(2,1)S(1)} %get-tuple-element.40), channel_id=1, source_target_pairs={{0,8},{4,12},{8,0},{12,4},{1,9},{5,13},{9,1},{13,5},{2,10},{6,14},... | collective-permute-start | bytes 122888 | tf_op jit(solution)/shard_map/ppermute | solution.py:58
  47.3 5.8 %collective-permute-start.16 = (bf16[16,1280]{1,0:T(8,128)(2,1)S(1)}, bf16[16,1280]{1,0:T(8,128)(2,1)S(1)}, u32[]{:S(2)}, u32[]{:S(2)}) collective-permute-start(bf16[16,1280]{1,0:T(8,128)(2,1)S(1)} %get-tuple-element.40), channel_id=1, source_target_pairs={{0,12},{4,8},{8,4},{12,0},{1,13},{5,9},{9,5},{13,1},{2,14},{6,10},... | collective-permute-start | bytes 122888 | tf_op jit(solution)/shard_map/ppermute | solution.py:58
  48.6 4.4 %collective-permute-start.17 = (bf16[16,1280]{1,0:T(8,128)(2,1)S(1)}, bf16[16,1280]{1,0:T(8,128)(2,1)S(1)}, u32[]{:S(2)}, u32[]{:S(2)}) collective-permute-start(bf16[16,1280]{1,0:T(8,128)(2,1)S(1)} %get-tuple-element.40), channel_id=1, source_target_pairs={{0,4},{4,0},{8,12},{12,8},{1,5},{5,1},{9,13},{13,9},{2,6},{6,2},{1... | collective-permute-start | bytes 122888 | tf_op jit(solution)/shard_map/ppermute | solution.py:58
  53.7 3.8 %collective-permute-start.18 = (bf16[16,1280]{1,0:T(8,128)(2,1)S(1)}, bf16[16,1280]{1,0:T(8,128)(2,1)S(1)}, u32[]{:S(2)}, u32[]{:S(2)}) collective-permute-start(bf16[16,1280]{1,0:T(8,128)(2,1)S(1)} %mix.3.refs_1_), channel_id=1, source_target_pairs={{0,3},{1,2},{2,1},{3,0},{4,7},{5,6},{6,5},{7,4},{8,11},{9,10},{10,... | collective-permute-start | bytes 122888 | tf_op jit(solution)/shard_map/ppermute | solution.py:58
  53.7 4.3 %collective-permute-start.19 = (bf16[16,1280]{1,0:T(8,128)(2,1)S(1)}, bf16[16,1280]{1,0:T(8,128)(2,1)S(1)}, u32[]{:S(2)}, u32[]{:S(2)}) collective-permute-start(bf16[16,1280]{1,0:T(8,128)(2,1)S(1)} %mix.3.refs_1_), channel_id=1, source_target_pairs={{0,2},{1,3},{2,0},{3,1},{4,6},{5,7},{6,4},{7,5},{8,10},{9,11},{10,... | collective-permute-start | bytes 122888 | tf_op jit(solution)/shard_map/ppermute | solution.py:58
  55.0 3.0 %collective-permute-start.20 = (bf16[16,1280]{1,0:T(8,128)(2,1)S(1)}, bf16[16,1280]{1,0:T(8,128)(2,1)S(1)}, u32[]{:S(2)}, u32[]{:S(2)}) collective-permute-start(bf16[16,1280]{1,0:T(8,128)(2,1)S(1)} %mix.3.refs_1_), channel_id=1, source_target_pairs={{0,1},{1,0},{2,3},{3,2},{4,5},{5,4},{6,7},{7,6},{8,9},{9,8},{10,11... | collective-permute-start | bytes 122888 | tf_op jit(solution)/shard_map/ppermute | solution.py:58
